TPU v7x, 32 devices: a whole 2x2x4 slice. The times are simulated.
32 devices in a mesh: sec: 2 (over y), dev: 16 (over z, x, core).
Axes of the slice: x: 2, y: 2, z: 4, core: 2. Of those that a mesh axis runs over, the one named last changes fastest.
Arguments:
- hidden_in: bfloat16 [512, 7168], P(('sec', 'dev')), may hold values from -6 to 6
- expert_ids: int32 [512, 8], P(('sec', 'dev')), may hold values from 0 to 15, all different within a row; in each aligned block of 8 rows (0 to 7, 8 to 15, ...) at most 8 rows name the same one
- gate_coef: float32 [512, 8], P(('sec', 'dev')), may hold values from 0.1 to 1
- query_lat: bfloat16 [512, 64, 576], P(('sec', 'dev')), may hold values from -40 to 40
- kv_cache: bfloat16 [512, 128, 576], P(('sec', 'dev')), may hold values from -6 to 6
- cache_len: int32 [512], P(('sec', 'dev')), may hold values from 32 to 128, as said below
- gate_weight: bfloat16 [16, 7168, 1024], P('dev', None, 'sec'), may hold values from -0.0625 to 0.0625
- up_weight: bfloat16 [16, 7168, 1024], P('dev', None, 'sec'), may hold values from -0.0625 to 0.0625
- down_weight: bfloat16 [16, 1024, 7168], P('dev', 'sec'), may hold values from -0.1875 to 0.1875
Outputs:
- attention: bfloat16 [512, 64, 512], P(('sec', 'dev'))
- routed_out: bfloat16 [512, 7168], P(('sec', 'dev'))
Inputs may be any that keep to these rules, and one draw needn't show every extreme that they name: `expert_ids`: each row names 8 different experts. In each aligned block of 8 rows (one micro-batch of one device) no expert is named by more than 8 rows, and in some block an expert is named by exactly 8 rows. `cache_len`: some row uses all 128 slots.
All inputs are finite; a program needn't handle non-finite values.
Results may differ from a plain program's by a relative error of at most 0.0065.
Values may be sent and summed in bfloat16 or wider, within the bound.
No kernel may reach another device: no remote copies, remote signals or barrier semaphores. Data moves between devices by JAX's collectives and lax.ppermute only.
A program may use at most 128 MiB of HBM per device.

v0:
```python
import math

import jax
import jax.numpy as jnp
from jax import lax
from jax.sharding import PartitionSpec as P

LAT = 512
TOP = 8


score_scale = 1.0 / math.sqrt(192.0)


def attend(query_lat, kv_cache, cache_len):
    scores = (
        jnp.einsum("rhk,rlk->rhl", query_lat, kv_cache, preferred_element_type=jnp.float32)
        * score_scale
    )
    positions = jnp.arange(kv_cache.shape[1], dtype=jnp.int32)
    visible = positions[None, None, :] < cache_len[:, None, None]
    scores = jnp.where(visible, scores, jnp.float32(-1e30))
    top_score = jnp.max(scores, axis=2, keepdims=True)
    exponent = jnp.exp(scores - top_score)
    denominator = jnp.sum(exponent, axis=2, keepdims=True)
    weights = (exponent / denominator).astype(jnp.bfloat16)
    return jnp.einsum(
        "rhl,rlc->rhc", weights, kv_cache[:, :, :LAT], preferred_element_type=jnp.float32
    ).astype(jnp.bfloat16)


def routing_tables(expert_ids, gate_coef, expert_count, capacity):
    row_count, top_count = expert_ids.shape
    flat_ids = expert_ids.reshape(-1)
    position_ids = jnp.arange(flat_ids.shape[0], dtype=jnp.int32)
    matches = (flat_ids[:, None] == flat_ids[None, :]) & (
        position_ids[None, :] < position_ids[:, None]
    )
    slot_rank = jnp.sum(matches.astype(jnp.int32), axis=1)
    target = flat_ids * capacity + slot_rank
    slot_ids = jnp.arange(expert_count * capacity, dtype=jnp.int32)
    placed = (target[None, :] == slot_ids[:, None]).astype(jnp.float32)
    owner_hot = (
        (position_ids // top_count)[:, None] == jnp.arange(row_count, dtype=jnp.int32)[None, :]
    ).astype(jnp.float32)
    picker = jnp.dot(placed, owner_hot, precision=lax.Precision.HIGHEST).astype(jnp.bfloat16)
    weighted = owner_hot * gate_coef.reshape(-1)[:, None]
    mixing = jnp.dot(weighted.T, placed.T, precision=lax.Precision.HIGHEST)
    return (picker, mixing)


def expert_rows(tokens, gate_weight, up_weight, down_weight):
    shape_in = tokens.shape
    flat_rows = tokens.reshape(-1, shape_in[-1])
    gate_val = jnp.dot(flat_rows, gate_weight[0], preferred_element_type=jnp.float32)
    up_val = jnp.dot(flat_rows, up_weight[0], preferred_element_type=jnp.float32)
    hidden = (jax.nn.silu(gate_val) * up_val).astype(jnp.bfloat16)
    part_out = jnp.dot(hidden, down_weight[0], preferred_element_type=jnp.float32).astype(
        jnp.bfloat16
    )
    return part_out.reshape(shape_in)


def route_tokens(send_buf, gate_weight, up_weight, down_weight):
    section_count = lax.axis_size("sec")
    doubled = jnp.concatenate([send_buf] * section_count, axis=0)
    halves = expert_rows(
        lax.all_to_all(doubled, ("sec", "dev"), split_axis=0, concat_axis=0, tiled=True),
        gate_weight,
        up_weight,
        down_weight,
    )
    returned = lax.all_to_all(halves, ("sec", "dev"), split_axis=0, concat_axis=0, tiled=True)
    pieces = returned.reshape((section_count,) + send_buf.shape).astype(jnp.float32)
    return jnp.sum(pieces, axis=0).astype(jnp.bfloat16)


def combine(returned, mixing):
    flat_back = returned.reshape(-1, returned.shape[-1]).astype(jnp.float32)
    return jnp.dot(mixing, flat_back, precision=lax.Precision.HIGHEST).astype(jnp.bfloat16)


def per_device(
    hidden_in,
    expert_ids,
    gate_coef,
    query_lat,
    kv_cache,
    cache_len,
    gate_weight,
    up_weight,
    down_weight,
):
    half_rows = hidden_in.shape[0] // 2
    model_width = hidden_in.shape[1]
    expert_count = lax.axis_size("dev")
    capacity = max(2, 2 * TOP * half_rows // expert_count)
    tables = []
    send_bufs = []
    for offset in (0, half_rows):
        picker, mixing = routing_tables(
            expert_ids[offset : offset + half_rows],
            gate_coef[offset : offset + half_rows],
            expert_count,
            capacity,
        )
        tables.append(mixing)
        gathered = jnp.dot(
            picker, hidden_in[offset : offset + half_rows], preferred_element_type=jnp.float32
        ).astype(jnp.bfloat16)
        send_bufs.append(gathered.reshape(expert_count, capacity, model_width))
    first_attention = attend(query_lat[:half_rows], kv_cache[:half_rows], cache_len[:half_rows])
    first_back = route_tokens(send_bufs[0], gate_weight, up_weight, down_weight)
    second_attention = attend(query_lat[half_rows:], kv_cache[half_rows:], cache_len[half_rows:])
    second_back = route_tokens(send_bufs[1], gate_weight, up_weight, down_weight)
    attention = jnp.concatenate([first_attention, second_attention], axis=0)
    routed_out = jnp.concatenate(
        [combine(first_back, tables[0]), combine(second_back, tables[1])], axis=0
    )
    return (attention, routed_out)


def solution(mesh):
    in_specs = (
        P(("sec", "dev"), None),
        P(("sec", "dev"), None),
        P(("sec", "dev"), None),
        P(("sec", "dev"), None, None),
        P(("sec", "dev"), None, None),
        P(("sec", "dev")),
        P("dev", None, "sec"),
        P("dev", None, "sec"),
        P("dev", "sec", None),
    )
    out_specs = (P(("sec", "dev"), None, None), P(("sec", "dev"), None))
    return jax.shard_map(
        per_device, mesh=mesh, in_specs=in_specs, out_specs=out_specs, check_vma=False
    )
```

profile of v0, /device:TPU:0, one launch (start us, length us, event | category | flops | bytes accessed | tf_op | source)
XLA Modules:
  0.0 367.7 jit_solution(8055633101281341949)
XLA Ops:
  0.6 0.9 fusion.113
  2.1 1.5 fusion.5
  3.6 2.1 pad_maximum_fusion.1
  5.7 7.4 %all-to-all-start.2 = ((bf16[32,8,7168]{2,1,0:T(8,128)(2,1)}), bf16[32,8,7168]{2,1,0:T(8,128)(2,1)}, u32[]{:S(2)}, u32[]{:S(2)}) async-start(bf16[32,8,7168]{2,1,0:T(8,128)(2,1)} %pad_maximum_fusion.1), calls=%async_computation.2 | async-start | bytes 7340032 | tf_op jit(solution)/shard_map/all_to_all | solution.py:68
  13.5 0.2 convolution_convert_fusion.9
  13.7 0.6 fusion.4
  14.3 2.2 pad_maximum_fusion
  16.5 80.5 %all-to-all-done.2 = bf16[32,8,7168]{2,1,0:T(8,128)(2,1)} async-done(((bf16[32,8,7168]{2,1,0:T(8,128)(2,1)}), bf16[32,8,7168]{2,1,0:T(8,128)(2,1)}, u32[]{:S(2)}, u32[]{:S(2)}) %all-to-all-start.2) | async-done | bytes 3670048 | tf_op jit(solution)/shard_map/all_to_all | solution.py:68
  97.0 3.5 all-to-all-start
  100.5 6.2 %fusion.12 = f32[256,512]{1,0:T(8,128)S(1)} fusion(bf16[1,7168,512]{2,1,0:T(8,128)(2,1)} %param.15, bf16[32,8,7168]{2,1,0:T(8,128)(2,1)} %all-to-all-done.2), kind=kOutput, calls=%fused_computation.18 | convolution fusion | flops 1879048192 | bytes 11534336 | tf_op jit(solution)/shard_map/dot_general | solution.py:55
  106.8 12.1 %fusion.3 = bf16[32,8,7168]{2,1,0:T(8,128)(2,1)} fusion(bf16[1,512,7168]{2,1,0:T(8,128)(2,1)} %param.17, bf16[1,7168,512]{2,1,0:T(8,128)(2,1)} %param.16, bf16[32,8,7168]{2,1,0:T(8,128)(2,1)} %all-to-all-done.2, f32[256,512]{1,0:T(8,128)S(1)} %fusion.12), kind=kOutput, calls=%fused_computation.5 | convolution fusion | flops 3760717824 | bytes 22544384 | tf_op jit(solution)/shard_map/dot_general | solution.py:58
  118.9 65.5 %all-to-all-done = bf16[32,8,7168]{2,1,0:T(8,128)(2,1)} async-done(((bf16[32,8,7168]{2,1,0:T(8,128)(2,1)}), bf16[32,8,7168]{2,1,0:T(8,128)(2,1)}, u32[]{:S(2)}, u32[]{:S(2)}) %all-to-all-start) | async-done | bytes 3670048 | tf_op jit(solution)/shard_map/all_to_all | solution.py:68
  184.4 3.6 all-to-all-start.3
  188.0 6.2 %fusion.14 = f32[256,512]{1,0:T(8,128)S(1)} fusion(bf16[1,7168,512]{2,1,0:T(8,128)(2,1)} %param.15, bf16[32,8,7168]{2,1,0:T(8,128)(2,1)} %all-to-all-done), kind=kOutput, calls=%fused_computation.20 | convolution fusion | flops 1879048192 | bytes 11534336 | tf_op jit(solution)/shard_map/dot_general | solution.py:55
  194.2 12.2 %fusion.2 = bf16[32,8,7168]{2,1,0:T(8,128)(2,1)} fusion(bf16[1,512,7168]{2,1,0:T(8,128)(2,1)} %param.17, bf16[1,7168,512]{2,1,0:T(8,128)(2,1)} %param.16, bf16[32,8,7168]{2,1,0:T(8,128)(2,1)} %all-to-all-done, f32[256,512]{1,0:T(8,128)S(1)} %fusion.14), kind=kOutput, calls=%fused_computation.4 | convolution fusion | flops 3760717824 | bytes 22544384 | tf_op jit(solution)/shard_map/dot_general | solution.py:58
  206.4 65.4 %all-to-all-done.3 = bf16[32,8,7168]{2,1,0:T(8,128)(2,1)} async-done(((bf16[32,8,7168]{2,1,0:T(8,128)(2,1)}), bf16[32,8,7168]{2,1,0:T(8,128)(2,1)}, u32[]{:S(2)}, u32[]{:S(2)}) %all-to-all-start.3) | async-done | bytes 3670048 | tf_op jit(solution)/shard_map/all_to_all | solution.py:73
  271.8 3.7 %all-to-all-start.1 = ((bf16[32,8,7168]{2,1,0:T(8,128)(2,1)}), bf16[32,8,7168]{2,1,0:T(8,128)(2,1)}, u32[]{:S(2)}, u32[]{:S(2)}) async-start(bf16[32,8,7168]{2,1,0:T(8,128)(2,1)} %fusion.2), calls=%async_computation.1 | async-start | bytes 7340032 | tf_op jit(solution)/shard_map/all_to_all | solution.py:73
  276.1 1.8 fusion.59
  277.9 0.2 fusion.116
  278.1 0.3 fusion.56
  278.5 0.2 fusion.115
  278.7 2.2 convolution_convert_fusion.7
  281.0 2.2 convolution_convert_fusion.6
  283.2 1.1 pad_maximum_fusion.2
  284.3 0.2 fusion.88
  284.5 0.3 fusion.89
  284.8 3.0 reduce_sum.65
  287.8 71.4 %all-to-all-done.1 = bf16[32,8,7168]{2,1,0:T(8,128)(2,1)} async-done(((bf16[32,8,7168]{2,1,0:T(8,128)(2,1)}), bf16[32,8,7168]{2,1,0:T(8,128)(2,1)}, u32[]{:S(2)}, u32[]{:S(2)}) %all-to-all-start.1) | async-done | bytes 3670048 | tf_op jit(solution)/shard_map/all_to_all | solution.py:73
  359.3 4.5 %reduce_sum.63 = bf16[16,8,7168]{2,1,0:T(8,128)(2,1)} reduce(bf16[2,16,8,7168]{3,2,1,0:T(8,128)(2,1)} %bitcast.6, bf16[]{:T(256)} %constant.39.clone.1), dimensions={0}, to_apply=%region_5.6 | reduce | flops 917504 | bytes 5505026 | tf_op jit(solution)/shard_map/reduce_sum | solution.py:75
  363.8 0.8 convolution_convert_fusion.4
  364.6 2.3 convolution_convert_fusion.5
  367.0 0.7 pad_maximum_fusion.3
  (26 shorter events, 1.4 us)
Async XLA Ops:
  0.6 275.5 %copy-start = (bf16[16,64,576]{2,1,0:T(8,128)(2,1)S(1)}, bf16[16,64,576]{2,1,0:T(8,128)(2,1)}, u32[]{:S(2)}) copy-start(bf16[16,64,576]{2,1,0:T(8,128)(2,1)} %param.12) | copy-start | bytes 3538948
  5.7 8.0 %copy-start.2 = (bf16[16,7168]{1,0:T(8,128)(2,1)S(1)}, bf16[16,7168]{1,0:T(8,128)(2,1)}, u32[]{:S(2)}) copy-start(bf16[16,7168]{1,0:T(8,128)(2,1)} %param.9) | copy-start | bytes 688132
  5.7 91.3 %all-to-all-start.2 = ((bf16[32,8,7168]{2,1,0:T(8,128)(2,1)}), bf16[32,8,7168]{2,1,0:T(8,128)(2,1)}, u32[]{:S(2)}, u32[]{:S(2)}) async-start(bf16[32,8,7168]{2,1,0:T(8,128)(2,1)} %pad_maximum_fusion.1), calls=%async_computation.2 | async-start | bytes 7340032 | tf_op jit(solution)/shard_map/all_to_all | solution.py:68
  97.0 87.4 %all-to-all-start = ((bf16[32,8,7168]{2,1,0:T(8,128)(2,1)}), bf16[32,8,7168]{2,1,0:T(8,128)(2,1)}, u32[]{:S(2)}, u32[]{:S(2)}) async-start(bf16[32,8,7168]{2,1,0:T(8,128)(2,1)} %pad_maximum_fusion), calls=%async_computation | async-start | bytes 7340032 | tf_op jit(solution)/shard_map/all_to_all | solution.py:68
  184.4 87.4 %all-to-all-start.3 = ((bf16[32,8,7168]{2,1,0:T(8,128)(2,1)}), bf16[32,8,7168]{2,1,0:T(8,128)(2,1)}, u32[]{:S(2)}, u32[]{:S(2)}) async-start(bf16[32,8,7168]{2,1,0:T(8,128)(2,1)} %fusion.3), calls=%async_computation.3 | async-start | bytes 7340032 | tf_op jit(solution)/shard_map/all_to_all | solution.py:73
  206.4 69.2 %copy-start.3 = (f32[16,8]{0,1:T(8,128)S(1)}, f32[16,8]{0,1:T(8,128)}, u32[]{:S(2)}) copy-start(f32[16,8]{0,1:T(8,128)} %param.11) | copy-start | bytes 1540
  206.4 69.5 %copy-start.4 = (s32[16]{0:T(128)S(1)}, s32[16]{0:T(128)}, u32[]{:S(2)}) copy-start(s32[16]{0:T(128)} %param.14) | copy-start | bytes 196
  271.8 87.4 %all-to-all-start.1 = ((bf16[32,8,7168]{2,1,0:T(8,128)(2,1)}), bf16[32,8,7168]{2,1,0:T(8,128)(2,1)}, u32[]{:S(2)}, u32[]{:S(2)}) async-start(bf16[32,8,7168]{2,1,0:T(8,128)(2,1)} %fusion.2), calls=%async_computation.1 | async-start | bytes 7340032 | tf_op jit(solution)/shard_map/all_to_all | solution.py:73
  276.0 2.2 copy-start.1
where the time goes:
time: 368 us
  waiting for transfers between devices  283 us (77%)
  matrix products  49.6 us (13%)
  starting transfers between devices  18.2 us (5%)
  other arithmetic  14.6 us (4%)
    all_to_all x2, waiting for transfers between devices, route_tokens(): lax.all_to_all(doubled, ('sec', 'dev'), split_axis=0, concat_axis=0, tile...  146 us
    all_to_all x2, waiting for transfers between devices, route_tokens(): lax.all_to_all(halves, ('sec', 'dev'), split_axis=0, concat_axis=0, tiled...  137 us
    dot_general x2, matrix products, expert_rows(): jnp.dot(hidden, down_weight[0], preferred_element_type=jnp.float32)  24.3 us
    dot_general x2, matrix products, expert_rows(): jnp.dot(flat_rows, gate_weight[0], preferred_element_type=jnp.float32)  12.5 us
    all_to_all x2, starting transfers between devices, route_tokens(): lax.all_to_all(doubled, ('sec', 'dev'), split_axis=0, concat_axis=0, tile...  11 us
    reduce_sum x2, other arithmetic, route_tokens(): return jnp.sum(pieces, axis=0).astype(jnp.bfloat16)  7.54 us
  transfers between devices with their start and end apart: 4, of which 4 were waited for; matrix products, arithmetic and copies ran while one was open for 14% of the time, Pallas kernels for 0%

commit v1 on v0

--- a/solution.py
+++ b/solution.py
@@ -7,7 +7,7 @@
 
 LAT = 512
 TOP = 8
-
+AXES = ("sec", "dev")
 
 score_scale = 1.0 / math.sqrt(192.0)
 
@@ -65,12 +65,12 @@
     section_count = lax.axis_size("sec")
     doubled = jnp.concatenate([send_buf] * section_count, axis=0)
     halves = expert_rows(
-        lax.all_to_all(doubled, ("sec", "dev"), split_axis=0, concat_axis=0, tiled=True),
+        lax.all_to_all(doubled, AXES, split_axis=0, concat_axis=0, tiled=True),
         gate_weight,
         up_weight,
         down_weight,
     )
-    returned = lax.all_to_all(halves, ("sec", "dev"), split_axis=0, concat_axis=0, tiled=True)
+    returned = lax.all_to_all(halves, AXES, split_axis=0, concat_axis=0, tiled=True)
     pieces = returned.reshape((section_count,) + send_buf.shape).astype(jnp.float32)
     return jnp.sum(pieces, axis=0).astype(jnp.bfloat16)
 
@@ -78,6 +78,189 @@
 def combine(returned, mixing):
     flat_back = returned.reshape(-1, returned.shape[-1]).astype(jnp.float32)
     return jnp.dot(mixing, flat_back, precision=lax.Precision.HIGHEST).astype(jnp.bfloat16)
+
+
+def routed_sparse(
+    hidden_in, expert_ids, gate_coef, gate_weight, up_weight, down_weight, half_rows, capacity
+):
+    model_width = hidden_in.shape[1]
+    expert_count = lax.axis_size("dev")
+    outs = []
+    for offset in (0, half_rows):
+        picker, mixing = routing_tables(
+            expert_ids[offset : offset + half_rows],
+            gate_coef[offset : offset + half_rows],
+            expert_count,
+            capacity,
+        )
+        gathered = jnp.dot(
+            picker, hidden_in[offset : offset + half_rows], preferred_element_type=jnp.float32
+        ).astype(jnp.bfloat16)
+        send_buf = gathered.reshape(expert_count, capacity, model_width)
+        outs.append(combine(route_tokens(send_buf, gate_weight, up_weight, down_weight), mixing))
+    return jnp.concatenate(outs, axis=0)
+
+
+def permutation(n_dev, move):
+    pairs = []
+    for y in range(2):
+        for d in range(n_dev):
+            there = move(y, d // 4, (d // 2) % 2, d % 2)
+            if there is not None:
+                ty, tz, tx, tc = there
+                pairs.append((y * n_dev + d, ty * n_dev + tz * 4 + tx * 2 + tc))
+    return lambda a: lax.ppermute(a, AXES, pairs)
+
+
+class Moves:
+    def __init__(self, n_dev):
+        line = n_dev // 4
+
+        def along(y, z, x, c):
+            t = z + (1 if c else -1)
+            return (y, t, x, c) if 0 <= t < line else None
+
+        self.line = line
+        self.core = permutation(n_dev, lambda y, z, x, c: (y, z, x, 1 - c))
+        self.first = permutation(
+            n_dev, lambda y, z, x, c: (1 - y, z, x, c) if c else (y, z, 1 - x, c)
+        )
+        self.second = permutation(
+            n_dev, lambda y, z, x, c: (y, z, 1 - x, c) if c else (1 - y, z, x, c)
+        )
+        self.along = permutation(n_dev, along)
+        dev = lax.axis_index("dev")
+        self.core0 = dev % 2 == 0
+        self.place = dev // 4
+
+
+def swap_halves(a):
+    half = a.shape[0] // 2
+    return jnp.concatenate([a[half:], a[:half]], axis=0)
+
+
+def plane_gather(mv, block):
+    one = mv.first(block)
+    two = mv.second(block)
+    both = mv.second(one)
+    own = [block, one, two, both]
+    return own, [mv.core(b) for b in own]
+
+
+def pick_slot(mv, k, mine, theirs):
+    n = mv.line
+    up = jnp.where(mv.core0, mine[k - 1], theirs[k - 1])
+    down = jnp.where(mv.core0, theirs[n - k - 1], mine[n - k - 1])
+    return jnp.where(mv.place + k < n, up, down)
+
+
+def gather_line_first(mv, block):
+    rows = block.shape[0]
+    moving = jnp.concatenate([block, mv.core(block)], axis=0)
+    mine, theirs = [], []
+    for _ in range(mv.line - 1):
+        moving = mv.along(moving)
+        mine.append(moving[:rows])
+        theirs.append(mv.core(moving[rows:]))
+    slots = [block] + [pick_slot(mv, k, mine, theirs) for k in range(1, mv.line)]
+    own, other = plane_gather(mv, jnp.concatenate(slots, axis=0))
+    return jnp.concatenate(own + other, axis=0)
+
+
+def gather_plane_first(mv, block):
+    own, other = plane_gather(mv, block)
+    chip = jnp.concatenate(own + other, axis=0)
+    moving = chip
+    mine, theirs = [], []
+    for _ in range(mv.line - 1):
+        moving = mv.along(moving)
+        mine.append(moving)
+        theirs.append(swap_halves(mv.core(moving)))
+    slots = [chip] + [pick_slot(mv, k, mine, theirs) for k in range(1, mv.line)]
+    rows, width = block.shape
+    stacked = jnp.stack([s.reshape(8, rows, width) for s in slots], axis=1)
+    return stacked.reshape(-1, width)
+
+
+def plus(*terms):
+    total = terms[0].astype(jnp.float32)
+    for t in terms[1:]:
+        total = total + t.astype(jnp.float32)
+    return total.astype(jnp.bfloat16)
+
+
+def plane_sum(mv, s):
+    s1 = plus(s[1], mv.second(s[3]))
+    return plus(s[0], mv.second(s[2]), mv.first(s1))
+
+
+def sum_line_last(mv, y):
+    n = mv.line
+    groups = y.reshape(2, 4, -1, y.shape[1])
+    s = [plus(groups[0, i], mv.core(groups[1, i])) for i in range(4)]
+    slots = plane_sum(mv, s).reshape(n, -1, y.shape[1])
+    rows = slots.shape[1]
+    acc = None
+    for k in range(n - 1, 0, -1):
+        give = jnp.where(mv.core0, slots[k], slots[n - k])
+        keep = jnp.where(mv.core0, slots[n - k], slots[k])
+        term = jnp.concatenate([keep, mv.core(give)], axis=0)
+        acc = mv.along(term if acc is None else plus(term, acc))
+    return plus(slots[0], acc[:rows], mv.core(acc[rows:]))
+
+
+def sum_line_first(mv, y):
+    n = mv.line
+    width = y.shape[1]
+    slots = y.reshape(8, n, -1, width)
+    slots = [slots[:, k].reshape(-1, width) for k in range(n)]
+    acc = None
+    for k in range(n - 1, 0, -1):
+        give = jnp.where(mv.core0, slots[k], slots[n - k])
+        keep = jnp.where(mv.core0, slots[n - k], slots[k])
+        term = (keep, swap_halves(mv.core(give)))
+        acc = mv.along(plus(*term) if acc is None else plus(*term, acc))
+    half = acc.shape[0] // 2
+    t = plus(slots[0], acc)
+    s = plus(t[:half], mv.core(t[half:])).reshape(4, -1, width)
+    return plane_sum(mv, [s[i] for i in range(4)])
+
+
+def spread_coefs(expert_ids, gate_coef, expert_count):
+    hot = expert_ids[:, :, None] == jnp.arange(expert_count, dtype=jnp.int32)[None, None, :]
+    dense = jnp.sum(jnp.where(hot, gate_coef[:, :, None], 0.0), axis=1)
+    high = lax.reduce_precision(dense, 8, 7)
+    parts = jnp.concatenate([high, dense - high], axis=1).astype(jnp.bfloat16)
+    pad = -parts.shape[1] % 128
+    return jnp.pad(parts, ((0, 0), (0, pad)))
+
+
+def routed_dense(hidden_in, expert_ids, gate_coef, gate_weight, up_weight, down_weight):
+    width = hidden_in.shape[1]
+    n_dev = lax.axis_size("dev")
+    mv = Moves(n_dev)
+    cut = width // 256 * 9 // 28 * 256
+    coefs = spread_coefs(expert_ids, gate_coef, n_dev)
+    rows_q = gather_line_first(mv, jnp.concatenate([hidden_in[:, cut:], coefs], axis=1))
+    rows_p = gather_plane_first(mv, hidden_in[:, :cut])
+    me = lax.axis_index("dev")
+    tail = rows_q[:, width - cut :].astype(jnp.float32)
+    coef = lax.dynamic_slice_in_dim(tail, me, 1, 1) + lax.dynamic_slice_in_dim(
+        tail, me + n_dev, 1, 1
+    )
+    rows_q = rows_q[:, : width - cut]
+
+    def project(w):
+        return jnp.dot(rows_p, w[0, :cut], preferred_element_type=jnp.float32) + jnp.dot(
+            rows_q, w[0, cut:], preferred_element_type=jnp.float32
+        )
+
+    hidden = (jax.nn.silu(project(gate_weight)) * project(up_weight)).astype(jnp.bfloat16)
+    y_q = jnp.dot(hidden, down_weight[0, :, cut:], preferred_element_type=jnp.float32)
+    y_p = jnp.dot(hidden, down_weight[0, :, :cut], preferred_element_type=jnp.float32)
+    out_q = sum_line_last(mv, (y_q * coef).astype(jnp.bfloat16))
+    out_p = sum_line_first(mv, (y_p * coef).astype(jnp.bfloat16))
+    return jnp.concatenate([out_p, out_q], axis=1)
 
 
 def per_device(
@@ -92,31 +275,16 @@
     down_weight,
 ):
     half_rows = hidden_in.shape[0] // 2
-    model_width = hidden_in.shape[1]
     expert_count = lax.axis_size("dev")
     capacity = max(2, 2 * TOP * half_rows // expert_count)
-    tables = []
-    send_bufs = []
-    for offset in (0, half_rows):
-        picker, mixing = routing_tables(
-            expert_ids[offset : offset + half_rows],
-            gate_coef[offset : offset + half_rows],
-            expert_count,
-            capacity,
-        )
-        tables.append(mixing)
-        gathered = jnp.dot(
-            picker, hidden_in[offset : offset + half_rows], preferred_element_type=jnp.float32
-        ).astype(jnp.bfloat16)
-        send_bufs.append(gathered.reshape(expert_count, capacity, model_width))
-    first_attention = attend(query_lat[:half_rows], kv_cache[:half_rows], cache_len[:half_rows])
-    first_back = route_tokens(send_bufs[0], gate_weight, up_weight, down_weight)
-    second_attention = attend(query_lat[half_rows:], kv_cache[half_rows:], cache_len[half_rows:])
-    second_back = route_tokens(send_bufs[1], gate_weight, up_weight, down_weight)
-    attention = jnp.concatenate([first_attention, second_attention], axis=0)
-    routed_out = jnp.concatenate(
-        [combine(first_back, tables[0]), combine(second_back, tables[1])], axis=0
-    )
+    weights = (gate_weight, up_weight, down_weight)
+    if capacity < half_rows:
+        routed_out = routed_sparse(
+            hidden_in, expert_ids, gate_coef, *weights, half_rows, capacity
+        )
+    else:
+        routed_out = routed_dense(hidden_in, expert_ids, gate_coef, *weights)
+    attention = attend(query_lat, kv_cache, cache_len)
     return (attention, routed_out)
 
 

time: 368 us -> 176 us (0.48)
  waiting for transfers between devices: 283 us -> 91.7 us
  matrix products: 49.6 us -> 21.9 us
  starting transfers between devices: 18.2 us -> 36.2 us
  local copies, waits for them, and re-layouts: 1.66 us -> 11.6 us
    all_to_all x4 -> x0, waiting for transfers between devices: 283 us -> none  [the longest x2 146 us: route_tokens(): lax.all_to_all(doubled, ('sec', 'dev'), split_axis=0, concat_axis=0, tile...]
    ppermute x0 -> x51, waiting for transfers between devices: none -> 91.7 us  [permutation(): return lambda a: lax.ppermute(a, AXES, pairs)]
    ppermute x0 -> x51, starting transfers between devices: none -> 36.2 us  [permutation(): return lambda a: lax.ppermute(a, AXES, pairs)]
    dot_general x12 -> x6, matrix products: 43 us -> 16.7 us  [the longest x2 7.64 us: project(): jnp.dot(rows_q, w[0, cut:], preferred_element_type=jnp.float32)]
    all_to_all x4 -> x0, starting transfers between devices: 18.2 us -> none  [the longest x2 11 us: route_tokens(): lax.all_to_all(doubled, ('sec', 'dev'), split_axis=0, concat_axis=0, tile...]
    reduce_sum x4 -> x1, other arithmetic: 7.9 us -> 0.11 us  [spread_coefs(): dense = jnp.sum(jnp.where(hot, gate_coef[:, :, None], 0.0), axis=1)]
    unnamed x10 -> x34, local copies, waits for them, and re-layouts: 0.03 us -> 7.54 us
    concatenate x4 -> x6, other arithmetic: 6.13 us -> 1.57 us  [the longest x1 0.7 us: routed_dense(): return jnp.concatenate([out_p, out_q], axis=1)]
  transfers between devices with their start and end apart: 4 -> 51, of which waited for: 4 -> 18; matrix products, arithmetic and copies ran while one was open for 14% -> 15% of each run, Pallas kernels for 0% -> 0%
where the time goes in v1:
time: 176 us; the launch traced here: 175 us
  waiting for transfers between devices  91.7 us (52%)
  starting transfers between devices  36.2 us (21%)
  matrix products  21.9 us (12%)
  other arithmetic  12.6 us (7%)
  local copies, waits for them, and re-layouts  11.6 us (7%)
    ppermute x51, waiting for transfers between devices, permutation(): return lambda a: lax.ppermute(a, AXES, pairs)  91.7 us
    ppermute x51, starting transfers between devices, permutation(): return lambda a: lax.ppermute(a, AXES, pairs)  36.2 us
    dot_general x2, matrix products, project(): jnp.dot(rows_q, w[0, cut:], preferred_element_type=jnp.float32)  7.64 us
    unnamed x34, local copies, waits for them, and re-layouts  7.54 us
    dot_general x2, matrix products, project(): jnp.dot(rows_p, w[0, :cut], preferred_element_type=jnp.float32)  4.71 us
    dot_general x1, matrix products, attend(): jnp.einsum('rhl,rlc->rhc', weights, kv_cache[:, :, :LAT], preferred_eleme...  4.49 us
    unnamed x5, other arithmetic  4.07 us
    convert_element_type x13, other arithmetic, plus(): return total.astype(jnp.bfloat16)  3.69 us
  transfers between devices with their start and end apart: 51, of which 18 were waited for; matrix products, arithmetic and copies ran while one was open for 15% of the time, Pallas kernels for 0%

profile of v1, /device:TPU:0, one launch (start us, length us, event | category | flops | bytes accessed | tf_op | source)
XLA Modules:
  0.0 175.3 jit_solution(8327337024755252626)
XLA Ops:
  1.7 3.0 %collective-permute-start = (bf16[16,2304]{1,0:T(8,128)(2,1)S(1)}, bf16[16,2304]{1,0:T(8,128)(2,1)S(1)}, u32[]{:S(2)}, u32[]{:S(2)}) collective-permute-start(bf16[16,2304]{1,0:T(8,128)(2,1)S(1)} %get-tuple-element.37), channel_id=1, source_target_pairs={{0,2},{1,17},{2,0},{3,19},{4,6},{5,21},{6,4},{7,23},{8,10},{9,25},... | collective-permute-start | bytes 221192 | tf_op jit(solution)/shard_map/ppermute | solution.py:112
  4.7 1.5 collective-permute-start.1
  11.1 3.3 %collective-permute-done.2 = bf16[16,2304]{1,0:T(8,128)(2,1)S(1)} collective-permute-done((bf16[16,2304]{1,0:T(8,128)(2,1)S(1)}, bf16[16,2304]{1,0:T(8,128)(2,1)S(1)}, u32[]{:S(2)}, u32[]{:S(2)}) %collective-permute-start.2) | collective-permute-done | bytes 73760 | tf_op jit(solution)/shard_map/ppermute | solution.py:112
  15.8 7.6 %collective-permute-done.14 = bf16[32,4992]{1,0:T(8,128)(2,1)S(1)} collective-permute-done((bf16[32,4992]{1,0:T(8,128)(2,1)S(1)}, bf16[32,4992]{1,0:T(8,128)(2,1)S(1)}, u32[]{:S(2)}, u32[]{:S(2)}) %collective-permute-start.14) | collective-permute-done | bytes 319520 | tf_op jit(solution)/shard_map/ppermute | solution.py:112
  24.7 7.6 %collective-permute-done.16 = bf16[32,4992]{1,0:T(8,128)(2,1)S(1)} collective-permute-done((bf16[32,4992]{1,0:T(8,128)(2,1)S(1)}, bf16[32,4992]{1,0:T(8,128)(2,1)S(1)}, u32[]{:S(2)}, u32[]{:S(2)}) %collective-permute-start.16) | collective-permute-done | bytes 319520 | tf_op jit(solution)/shard_map/ppermute | solution.py:112
  34.9 3.5 %collective-permute-start.15 = (bf16[16,4992]{1,0:T(8,128)(2,1)S(1)}, bf16[16,4992]{1,0:T(8,128)(2,1)S(1)}, u32[]{:S(2)}, u32[]{:S(2)}) collective-permute-start(bf16[16,4992]{1,0:T(8,128)(2,1)S(1)} %slice.236), channel_id=1, source_target_pairs={{0,1},{1,0},{2,3},{3,2},{4,5},{5,4},{6,7},{7,6},{8,9},{9,8},{10,11... | collective-permute-start | bytes 479240 | tf_op jit(solution)/shard_map/ppermute | solution.py:112
  38.4 2.6 %collective-permute-done.17 = bf16[32,4992]{1,0:T(8,128)(2,1)S(1)} collective-permute-done((bf16[32,4992]{1,0:T(8,128)(2,1)S(1)}, bf16[32,4992]{1,0:T(8,128)(2,1)S(1)}, u32[]{:S(2)}, u32[]{:S(2)}) %collective-permute-start.17) | collective-permute-done | bytes 319520 | tf_op jit(solution)/shard_map/ppermute | solution.py:112
  44.0 3.5 %collective-permute-done.7 = bf16[128,2304]{1,0:T(8,128)(2,1)} collective-permute-done((bf16[128,2304]{1,0:T(8,128)(2,1)S(1)}, bf16[128,2304]{1,0:T(8,128)(2,1)}, u32[]{:S(2)}, u32[]{:S(2)}) %collective-permute-start.7) | collective-permute-done | bytes 589856 | tf_op jit(solution)/shard_map/ppermute | solution.py:112
  48.9 1.7 constant_dynamic-update-slice_fusion.17
  50.6 1.6 constant_dynamic-update-slice_fusion.16
  54.0 5.5 %collective-permute-done.9 = bf16[128,2304]{1,0:T(8,128)(2,1)S(1)} collective-permute-done((bf16[128,2304]{1,0:T(8,128)(2,1)}, bf16[128,2304]{1,0:T(8,128)(2,1)S(1)}, u32[]{:S(2)}, u32[]{:S(2)}) %collective-permute-start.9) | collective-permute-done | bytes 589856 | tf_op jit(solution)/shard_map/ppermute | solution.py:112
  59.5 1.5 collective-permute-start.10
  61.1 9.0 %collective-permute-done.20 = bf16[64,4992]{1,0:T(8,128)(2,1)S(1)} collective-permute-done((bf16[64,4992]{1,0:T(8,128)(2,1)S(1)}, bf16[64,4992]{1,0:T(8,128)(2,1)S(1)}, u32[]{:S(2)}, u32[]{:S(2)}) %collective-permute-start.20) | collective-permute-done | bytes 639008 | tf_op jit(solution)/shard_map/ppermute | solution.py:112
  72.8 7.7 %collective-permute-done.22 = bf16[64,4992]{1,0:T(8,128)(2,1)S(1)} collective-permute-done((bf16[64,4992]{1,0:T(8,128)(2,1)S(1)}, bf16[64,4992]{1,0:T(8,128)(2,1)S(1)}, u32[]{:S(2)}, u32[]{:S(2)}) %collective-permute-start.22) | collective-permute-done | bytes 639008 | tf_op jit(solution)/shard_map/ppermute | solution.py:112
  84.1 1.6 select_select_fusion.2
  86.8 4.9 %fusion.2 = f32[512,512]{1,0:T(8,128)S(1)} fusion(bf16[1,7168,512]{2,1,0:T(8,128)(2,1)} %param.16, bf16[512,4992]{1,0:T(8,128)(2,1)S(1)} %constant_dynamic-update-slice_fusion.8), kind=kOutput, calls=%fused_computation.4 | convolution fusion | flops 2550136832 | bytes 11010048 | tf_op jit(solution)/shard_map/dot_general | solution.py:254
  91.8 2.7 %fusion.4 = f32[512,512]{1,0:T(8,128)S(1)} fusion(bf16[1,7168,512]{2,1,0:T(8,128)(2,1)S(1)} %bitcast.93, bf16[512,4992]{1,0:T(8,128)(2,1)S(1)} %constant_dynamic-update-slice_fusion.8), kind=kOutput, calls=%fused_computation.6 | convolution fusion | flops 2550136832 | bytes 11010048 | tf_op jit(solution)/shard_map/dot_general | solution.py:254
  95.9 3.3 %fusion.34 = bf16[512,512]{1,0:T(8,128)(2,1)S(1)} fusion(f32[512,512]{1,0:T(8,128)S(1)} %fusion.2, bf16[512,2304]{1,0:T(8,128)(2,1)S(1)} %bitcast.89, bf16[1,7168,512]{2,1,0:T(8,128)(2,1)} %param.16, f32[512,512]{1,0:T(8,128)S(1)} %fusion.25), kind=kOutput, calls=%fused_computation.29 | convolution fusion | flops 1209794560 | bytes 7340032 | tf_op jit(solution)/shard_map/dot_general | solution.py:254
  99.6 3.0 %multiply_convert_fusion = bf16[512,4864]{1,0:T(8,128)(2,1)S(1)} fusion(bf16[512,512]{1,0:T(8,128)(2,1)S(1)} %fusion.34, f32[512]{0:T(512)S(1)} %add_reduce_fusion, bf16[1,512,7168]{2,1,0:T(8,128)(2,1)S(1)} %bitcast.95), kind=kOutput, calls=%fused_computation.1 | convolution fusion | flops 2555117568 | bytes 10487808 | tf_op jit(solution)/shard_map/dot_general | solution.py:259
  102.6 1.4 fusion.9
  106.9 3.8 %collective-permute-done.28 = bf16[128,2304]{1,0:T(8,128)(2,1)S(1)} collective-permute-done((bf16[128,2304]{1,0:T(8,128)(2,1)S(1)}, bf16[128,2304]{1,0:T(8,128)(2,1)S(1)}, u32[]{:S(2)}, u32[]{:S(2)}) %collective-permute-start.28) | collective-permute-done | bytes 589856 | tf_op jit(solution)/shard_map/ppermute | solution.py:112
  112.9 2.0 %collective-permute-start.39 = (bf16[64,4864]{1,0:T(8,128)(2,1)S(1)}, bf16[64,4864]{1,0:T(8,128)(2,1)S(1)}, u32[]{:S(2)}, u32[]{:S(2)}) collective-permute-start(bf16[64,4864]{1,0:T(8,128)(2,1)S(1)} %get-tuple-element.12), channel_id=1, source_target_pairs={{0,16},{1,3},{2,18},{3,1},{4,20},{5,7},{6,22},{7,5},{8,24},{9,11},... | collective-permute-start | bytes 1867784 | tf_op jit(solution)/shard_map/ppermute | solution.py:112
  115.0 8.1 %collective-permute-done.42 = bf16[64,4864]{1,0:T(8,128)(2,1)S(1)} collective-permute-done((bf16[64,4864]{1,0:T(8,128)(2,1)S(1)}, bf16[64,4864]{1,0:T(8,128)(2,1)S(1)}, u32[]{:S(2)}, u32[]{:S(2)}) %collective-permute-start.42) | collective-permute-done | bytes 622624 | tf_op jit(solution)/shard_map/ppermute | solution.py:112
  125.3 5.8 %collective-permute-done.39 = bf16[64,4864]{1,0:T(8,128)(2,1)S(1)} collective-permute-done((bf16[64,4864]{1,0:T(8,128)(2,1)S(1)}, bf16[64,4864]{1,0:T(8,128)(2,1)S(1)}, u32[]{:S(2)}, u32[]{:S(2)}) %collective-permute-start.39) | collective-permute-done | bytes 622624 | tf_op jit(solution)/shard_map/ppermute | solution.py:112
  131.1 7.5 %collective-permute-done.43 = bf16[64,4864]{1,0:T(8,128)(2,1)S(1)} collective-permute-done((bf16[64,4864]{1,0:T(8,128)(2,1)S(1)}, bf16[64,4864]{1,0:T(8,128)(2,1)S(1)}, u32[]{:S(2)}, u32[]{:S(2)}) %collective-permute-start.43) | collective-permute-done | bytes 622624 | tf_op jit(solution)/shard_map/ppermute | solution.py:112
  139.3 1.5 collective-permute-start.32
  141.2 2.5 %collective-permute-start.45 = (bf16[16,4864]{1,0:T(8,128)(2,1)S(1)}, bf16[16,4864]{1,0:T(8,128)(2,1)S(1)}, u32[]{:S(2)}, u32[]{:S(2)}) collective-permute-start(bf16[16,4864]{1,0:T(8,128)(2,1)S(1)} %get-tuple-element.20), channel_id=1, source_target_pairs={{0,1},{1,0},{2,3},{3,2},{4,5},{5,4},{6,7},{7,6},{8,9},{9,8},{10,11... | collective-permute-start | bytes 466952 | tf_op jit(solution)/shard_map/ppermute | solution.py:112
  145.0 6.1 %collective-permute-done.32 = bf16[128,2304]{1,0:T(8,128)(2,1)S(1)} collective-permute-done((bf16[128,2304]{1,0:T(8,128)(2,1)S(1)}, bf16[128,2304]{1,0:T(8,128)(2,1)S(1)}, u32[]{:S(2)}, u32[]{:S(2)}) %collective-permute-start.32) | collective-permute-done | bytes 589856 | tf_op jit(solution)/shard_map/ppermute | solution.py:112
  151.4 3.0 %collective-permute-done.47 = bf16[32,4864]{1,0:T(8,128)(2,1)S(1)} collective-permute-done((bf16[32,4864]{1,0:T(8,128)(2,1)S(1)}, bf16[32,4864]{1,0:T(8,128)(2,1)S(1)}, u32[]{:S(2)}, u32[]{:S(2)}) %collective-permute-start.47) | collective-permute-done | bytes 311328 | tf_op jit(solution)/shard_map/ppermute | solution.py:112
  156.0 7.3 %collective-permute-done.48 = bf16[32,4864]{1,0:T(8,128)(2,1)S(1)} collective-permute-done((bf16[32,4864]{1,0:T(8,128)(2,1)S(1)}, bf16[32,4864]{1,0:T(8,128)(2,1)S(1)}, u32[]{:S(2)}, u32[]{:S(2)}) %collective-permute-start.48) | collective-permute-done | bytes 311328 | tf_op jit(solution)/shard_map/ppermute | solution.py:112
  166.0 4.5 %fusion.22 = bf16[16,64,512]{2,1,0:T(8,128)(2,1)} fusion(bf16[16,128,576]{1,2,0:T(8,128)(2,1)} %param.13, f32[16,64]{1,0:T(8,128)S(1)} %fusion.61, f32[16,64,128]{2,1,0:T(8,128)S(1)} %fusion.43), kind=kOutput, calls=%fused_computation.25 | convolution fusion | flops 135136384 | bytes 4202496 | tf_op jit(solution)/shard_map/rhl,rlc->rhc/dot_general | solution.py:27
  170.4 2.6 %collective-permute-done.49 = bf16[32,4864]{1,0:T(8,128)(2,1)S(1)} collective-permute-done((bf16[32,4864]{1,0:T(8,128)(2,1)}, bf16[32,4864]{1,0:T(8,128)(2,1)S(1)}, u32[]{:S(2)}, u32[]{:S(2)}) %collective-permute-start.49) | collective-permute-done | bytes 311328 | tf_op jit(solution)/shard_map/ppermute | solution.py:112
  (164 shorter events, 42.8 us)
Async XLA Ops:
  10.6 14.1 %collective-permute-start.5 = (bf16[16,2304]{1,0:T(8,128)(2,1)S(1)}, bf16[16,2304]{1,0:T(8,128)(2,1)S(1)}, u32[]{:S(2)}, u32[]{:S(2)}) collective-permute-start(bf16[16,2304]{1,0:T(8,128)(2,1)S(1)} %collective-permute-done.1), channel_id=1, source_target_pairs={{0,1},{1,0},{2,3},{3,2},{4,5},{5,4},{6,7},{7,6},{8,9},{9,8},{10,11... | collective-permute-start | bytes 221192 | tf_op jit(solution)/shard_map/ppermute | solution.py:112
  14.4 19.1 %collective-permute-start.6 = (bf16[16,2304]{1,0:T(8,128)(2,1)S(1)}, bf16[16,2304]{1,0:T(8,128)(2,1)S(1)}, u32[]{:S(2)}, u32[]{:S(2)}) collective-permute-start(bf16[16,2304]{1,0:T(8,128)(2,1)S(1)} %collective-permute-done.2), channel_id=1, source_target_pairs={{0,1},{1,0},{2,3},{3,2},{4,5},{5,4},{6,7},{7,6},{8,9},{9,8},{10,11... | collective-permute-start | bytes 221192 | tf_op jit(solution)/shard_map/ppermute | solution.py:112
  14.5 8.9 %collective-permute-start.14 = (bf16[32,4992]{1,0:T(8,128)(2,1)S(1)}, bf16[32,4992]{1,0:T(8,128)(2,1)S(1)}, u32[]{:S(2)}, u32[]{:S(2)}) collective-permute-start(bf16[32,4992]{1,0:T(8,128)(2,1)S(1)} %pad_maximum_fusion.5), channel_id=1, source_target_pairs={{1,5},{3,7},{4,0},{5,9},{6,2},{7,11},{8,4},{9,13},{10,6},{11,15},{... | collective-permute-start | bytes 958472 | tf_op jit(solution)/shard_map/ppermute | solution.py:112
  23.4 8.9 %collective-permute-start.16 = (bf16[32,4992]{1,0:T(8,128)(2,1)S(1)}, bf16[32,4992]{1,0:T(8,128)(2,1)S(1)}, u32[]{:S(2)}, u32[]{:S(2)}) collective-permute-start(bf16[32,4992]{1,0:T(8,128)(2,1)S(1)} %collective-permute-done.14), channel_id=1, source_target_pairs={{1,5},{3,7},{4,0},{5,9},{6,2},{7,11},{8,4},{9,13},{10,6},{11,15},{... | collective-permute-start | bytes 958472 | tf_op jit(solution)/shard_map/ppermute | solution.py:112
  32.2 8.9 %collective-permute-start.17 = (bf16[32,4992]{1,0:T(8,128)(2,1)S(1)}, bf16[32,4992]{1,0:T(8,128)(2,1)S(1)}, u32[]{:S(2)}, u32[]{:S(2)}) collective-permute-start(bf16[32,4992]{1,0:T(8,128)(2,1)S(1)} %collective-permute-done.16), channel_id=1, source_target_pairs={{1,5},{3,7},{4,0},{5,9},{6,2},{7,11},{8,4},{9,13},{10,6},{11,15},{... | collective-permute-start | bytes 958472 | tf_op jit(solution)/shard_map/ppermute | solution.py:112
  33.5 14.0 %collective-permute-start.7 = (bf16[128,2304]{1,0:T(8,128)(2,1)S(1)}, bf16[128,2304]{1,0:T(8,128)(2,1)}, u32[]{:S(2)}, u32[]{:S(2)}) collective-permute-start(bf16[128,2304]{1,0:T(8,128)(2,1)S(1)} %constant_dynamic-update-slice_fusion), channel_id=1, source_target_pairs={{1,5},{3,7},{4,0},{5,9},{6,2},{7,11},{8,4},{9,13},{10,6},{11,15},{... | collective-permute-start | bytes 1769480 | tf_op jit(solution)/shard_map/ppermute | solution.py:112
  34.9 13.9 %collective-permute-start.15 = (bf16[16,4992]{1,0:T(8,128)(2,1)S(1)}, bf16[16,4992]{1,0:T(8,128)(2,1)S(1)}, u32[]{:S(2)}, u32[]{:S(2)}) collective-permute-start(bf16[16,4992]{1,0:T(8,128)(2,1)S(1)} %slice.236), channel_id=1, source_target_pairs={{0,1},{1,0},{2,3},{3,2},{4,5},{5,4},{6,7},{7,6},{8,9},{9,8},{10,11... | collective-permute-start | bytes 479240 | tf_op jit(solution)/shard_map/ppermute | solution.py:112
  47.5 12.0 %collective-permute-start.9 = (bf16[128,2304]{1,0:T(8,128)(2,1)}, bf16[128,2304]{1,0:T(8,128)(2,1)S(1)}, u32[]{:S(2)}, u32[]{:S(2)}) collective-permute-start(bf16[128,2304]{1,0:T(8,128)(2,1)} %collective-permute-done.7), channel_id=1, source_target_pairs={{1,5},{3,7},{4,0},{5,9},{6,2},{7,11},{8,4},{9,13},{10,6},{11,15},{... | collective-permute-start | bytes 1769480 | tf_op jit(solution)/shard_map/ppermute | solution.py:112
  48.8 12.2 %collective-permute-start.8 = (bf16[128,2304]{1,0:T(8,128)(2,1)}, bf16[128,2304]{1,0:T(8,128)(2,1)S(1)}, u32[]{:S(2)}, u32[]{:S(2)}) collective-permute-start(bf16[128,2304]{1,0:T(8,128)(2,1)} %collective-permute-done.7), channel_id=1, source_target_pairs={{0,1},{1,0},{2,3},{3,2},{4,5},{5,4},{6,7},{7,6},{8,9},{9,8},{10,11... | collective-permute-start | bytes 1769480 | tf_op jit(solution)/shard_map/ppermute | solution.py:112
  53.0 17.1 %collective-permute-start.20 = (bf16[64,4992]{1,0:T(8,128)(2,1)S(1)}, bf16[64,4992]{1,0:T(8,128)(2,1)S(1)}, u32[]{:S(2)}, u32[]{:S(2)}) collective-permute-start(bf16[64,4992]{1,0:T(8,128)(2,1)S(1)} %pad_maximum_fusion.1), channel_id=1, source_target_pairs={{0,2},{1,17},{2,0},{3,19},{4,6},{5,21},{6,4},{7,23},{8,10},{9,25},... | collective-permute-start | bytes 1916936 | tf_op jit(solution)/shard_map/ppermute | solution.py:112
  53.6 17.4 %collective-permute-start.21 = (bf16[64,4992]{1,0:T(8,128)(2,1)S(1)}, bf16[64,4992]{1,0:T(8,128)(2,1)S(1)}, u32[]{:S(2)}, u32[]{:S(2)}) collective-permute-start(bf16[64,4992]{1,0:T(8,128)(2,1)S(1)} %pad_maximum_fusion.1), channel_id=1, source_target_pairs={{0,16},{1,3},{2,18},{3,1},{4,20},{5,7},{6,22},{7,5},{8,24},{9,11},... | collective-permute-start | bytes 1916936 | tf_op jit(solution)/shard_map/ppermute | solution.py:112
  54.0 27.4 %collective-permute-start.23 = (bf16[64,4992]{1,0:T(8,128)(2,1)S(1)}, bf16[64,4992]{1,0:T(8,128)(2,1)S(1)}, u32[]{:S(2)}, u32[]{:S(2)}) collective-permute-start(bf16[64,4992]{1,0:T(8,128)(2,1)S(1)} %pad_maximum_fusion.1), channel_id=1, source_target_pairs={{0,1},{1,0},{2,3},{3,2},{4,5},{5,4},{6,7},{7,6},{8,9},{9,8},{10,11... | collective-permute-start | bytes 1916936 | tf_op jit(solution)/shard_map/ppermute | solution.py:112
  59.5 12.4 %collective-permute-start.10 = (bf16[128,2304]{1,0:T(8,128)(2,1)S(1)}, bf16[128,2304]{1,0:T(8,128)(2,1)S(1)}, u32[]{:S(2)}, u32[]{:S(2)}) collective-permute-start(bf16[128,2304]{1,0:T(8,128)(2,1)S(1)} %collective-permute-done.9), channel_id=1, source_target_pairs={{1,5},{3,7},{4,0},{5,9},{6,2},{7,11},{8,4},{9,13},{10,6},{11,15},{... | collective-permute-start | bytes 1769480 | tf_op jit(solution)/shard_map/ppermute | solution.py:112
  61.0 11.5 %collective-permute-start.12 = (bf16[128,2304]{1,0:T(8,128)(2,1)S(1)}, bf16[128,2304]{1,0:T(8,128)(2,1)S(1)}, u32[]{:S(2)}, u32[]{:S(2)}) collective-permute-start(bf16[128,2304]{1,0:T(8,128)(2,1)S(1)} %collective-permute-done.9), channel_id=1, source_target_pairs={{0,1},{1,0},{2,3},{3,2},{4,5},{5,4},{6,7},{7,6},{8,9},{9,8},{10,11... | collective-permute-start | bytes 1769480 | tf_op jit(solution)/shard_map/ppermute | solution.py:112
  70.1 10.4 %collective-permute-start.22 = (bf16[64,4992]{1,0:T(8,128)(2,1)S(1)}, bf16[64,4992]{1,0:T(8,128)(2,1)S(1)}, u32[]{:S(2)}, u32[]{:S(2)}) collective-permute-start(bf16[64,4992]{1,0:T(8,128)(2,1)S(1)} %collective-permute-done.20), channel_id=1, source_target_pairs={{0,16},{1,3},{2,18},{3,1},{4,20},{5,7},{6,22},{7,5},{8,24},{9,11},... | collective-permute-start | bytes 1916936 | tf_op jit(solution)/shard_map/ppermute | solution.py:112
  71.0 11.2 %collective-permute-start.24 = (bf16[64,4992]{1,0:T(8,128)(2,1)S(1)}, bf16[64,4992]{1,0:T(8,128)(2,1)S(1)}, u32[]{:S(2)}, u32[]{:S(2)}) collective-permute-start(bf16[64,4992]{1,0:T(8,128)(2,1)S(1)} %collective-permute-done.20), channel_id=1, source_target_pairs={{0,1},{1,0},{2,3},{3,2},{4,5},{5,4},{6,7},{7,6},{8,9},{9,8},{10,11... | collective-permute-start | bytes 1916936 | tf_op jit(solution)/shard_map/ppermute | solution.py:112
  71.9 11.2 %collective-permute-start.25 = (bf16[64,4992]{1,0:T(8,128)(2,1)S(1)}, bf16[64,4992]{1,0:T(8,128)(2,1)S(1)}, u32[]{:S(2)}, u32[]{:S(2)}) collective-permute-start(bf16[64,4992]{1,0:T(8,128)(2,1)S(1)} %collective-permute-done.21), channel_id=1, source_target_pairs={{0,1},{1,0},{2,3},{3,2},{4,5},{5,4},{6,7},{7,6},{8,9},{9,8},{10,11... | collective-permute-start | bytes 1916936 | tf_op jit(solution)/shard_map/ppermute | solution.py:112
  72.4 11.6 %collective-permute-start.11 = (bf16[128,2304]{1,0:T(8,128)(2,1)S(1)}, bf16[128,2304]{1,0:T(8,128)(2,1)S(1)}, u32[]{:S(2)}, u32[]{:S(2)}) collective-permute-start(bf16[128,2304]{1,0:T(8,128)(2,1)S(1)} %collective-permute-done.10), channel_id=1, source_target_pairs={{0,1},{1,0},{2,3},{3,2},{4,5},{5,4},{6,7},{7,6},{8,9},{9,8},{10,11... | collective-permute-start | bytes 1769480 | tf_op jit(solution)/shard_map/ppermute | solution.py:112
  105.4 9.5 %collective-permute-start.40 = (bf16[64,4864]{1,0:T(8,128)(2,1)S(1)}, bf16[64,4864]{1,0:T(8,128)(2,1)S(1)}, u32[]{:S(2)}, u32[]{:S(2)}) collective-permute-start(bf16[64,4864]{1,0:T(8,128)(2,1)S(1)} %get-tuple-element.10), channel_id=1, source_target_pairs={{0,1},{1,0},{2,3},{3,2},{4,5},{5,4},{6,7},{7,6},{8,9},{9,8},{10,11... | collective-permute-start | bytes 1867784 | tf_op jit(solution)/shard_map/ppermute | solution.py:112
  105.5 19.8 %collective-permute-start.37 = (bf16[64,4864]{1,0:T(8,128)(2,1)S(1)}, bf16[64,4864]{1,0:T(8,128)(2,1)S(1)}, u32[]{:S(2)}, u32[]{:S(2)}) collective-permute-start(bf16[64,4864]{1,0:T(8,128)(2,1)S(1)} %get-tuple-element.8), channel_id=1, source_target_pairs={{0,1},{1,0},{2,3},{3,2},{4,5},{5,4},{6,7},{7,6},{8,9},{9,8},{10,11... | collective-permute-start | bytes 1867784 | tf_op jit(solution)/shard_map/ppermute | solution.py:112
  111.2 12.6 %collective-permute-start.30 = (bf16[128,2304]{1,0:T(8,128)(2,1)S(1)}, bf16[128,2304]{1,0:T(8,128)(2,1)S(1)}, u32[]{:S(2)}, u32[]{:S(2)}) collective-permute-start(bf16[128,2304]{1,0:T(8,128)(2,1)S(1)} %add_convert_fusion.4), channel_id=1, source_target_pairs={{1,5},{3,7},{4,0},{5,9},{6,2},{7,11},{8,4},{9,13},{10,6},{11,15},{... | collective-permute-start | bytes 1769480 | tf_op jit(solution)/shard_map/ppermute | solution.py:112
  112.8 10.3 %collective-permute-start.42 = (bf16[64,4864]{1,0:T(8,128)(2,1)S(1)}, bf16[64,4864]{1,0:T(8,128)(2,1)S(1)}, u32[]{:S(2)}, u32[]{:S(2)}) collective-permute-start(bf16[64,4864]{1,0:T(8,128)(2,1)S(1)} %get-tuple-element.13), channel_id=1, source_target_pairs={{0,16},{1,3},{2,18},{3,1},{4,20},{5,7},{6,22},{7,5},{8,24},{9,11},... | collective-permute-start | bytes 1867784 | tf_op jit(solution)/shard_map/ppermute | solution.py:112
  112.9 18.2 %collective-permute-start.39 = (bf16[64,4864]{1,0:T(8,128)(2,1)S(1)}, bf16[64,4864]{1,0:T(8,128)(2,1)S(1)}, u32[]{:S(2)}, u32[]{:S(2)}) collective-permute-start(bf16[64,4864]{1,0:T(8,128)(2,1)S(1)} %get-tuple-element.12), channel_id=1, source_target_pairs={{0,16},{1,3},{2,18},{3,1},{4,20},{5,7},{6,22},{7,5},{8,24},{9,11},... | collective-permute-start | bytes 1867784 | tf_op jit(solution)/shard_map/ppermute | solution.py:112
  123.3 15.3 %collective-permute-start.43 = (bf16[64,4864]{1,0:T(8,128)(2,1)S(1)}, bf16[64,4864]{1,0:T(8,128)(2,1)S(1)}, u32[]{:S(2)}, u32[]{:S(2)}) collective-permute-start(bf16[64,4864]{1,0:T(8,128)(2,1)S(1)} %add_convert_fusion.1), channel_id=1, source_target_pairs={{0,2},{1,17},{2,0},{3,19},{4,6},{5,21},{6,4},{7,23},{8,10},{9,25},... | collective-permute-start | bytes 1867784 | tf_op jit(solution)/shard_map/ppermute | solution.py:112
  124.0 15.0 %collective-permute-start.31 = (bf16[128,2304]{1,0:T(8,128)(2,1)S(1)}, bf16[128,2304]{1,0:T(8,128)(2,1)S(1)}, u32[]{:S(2)}, u32[]{:S(2)}) collective-permute-start(bf16[128,2304]{1,0:T(8,128)(2,1)S(1)} %add_convert_fusion.3), channel_id=1, source_target_pairs={{1,5},{3,7},{4,0},{5,9},{6,2},{7,11},{8,4},{9,13},{10,6},{11,15},{... | collective-permute-start | bytes 1769480 | tf_op jit(solution)/shard_map/ppermute | solution.py:112
  139.3 11.8 %collective-permute-start.32 = (bf16[128,2304]{1,0:T(8,128)(2,1)S(1)}, bf16[128,2304]{1,0:T(8,128)(2,1)S(1)}, u32[]{:S(2)}, u32[]{:S(2)}) collective-permute-start(bf16[128,2304]{1,0:T(8,128)(2,1)S(1)} %add_convert_fusion.2), channel_id=1, source_target_pairs={{1,5},{3,7},{4,0},{5,9},{6,2},{7,11},{8,4},{9,13},{10,6},{11,15},{... | collective-permute-start | bytes 1769480 | tf_op jit(solution)/shard_map/ppermute | solution.py:112
  141.2 10.2 %collective-permute-start.45 = (bf16[16,4864]{1,0:T(8,128)(2,1)S(1)}, bf16[16,4864]{1,0:T(8,128)(2,1)S(1)}, u32[]{:S(2)}, u32[]{:S(2)}) collective-permute-start(bf16[16,4864]{1,0:T(8,128)(2,1)S(1)} %get-tuple-element.20), channel_id=1, source_target_pairs={{0,1},{1,0},{2,3},{3,2},{4,5},{5,4},{6,7},{7,6},{8,9},{9,8},{10,11... | collective-permute-start | bytes 466952 | tf_op jit(solution)/shard_map/ppermute | solution.py:112
  143.6 12.4 %collective-permute-start.44 = (bf16[16,4864]{1,0:T(8,128)(2,1)S(1)}, bf16[16,4864]{1,0:T(8,128)(2,1)S(1)}, u32[]{:S(2)}, u32[]{:S(2)}) collective-permute-start(bf16[16,4864]{1,0:T(8,128)(2,1)S(1)} %get-tuple-element.22), channel_id=1, source_target_pairs={{0,1},{1,0},{2,3},{3,2},{4,5},{5,4},{6,7},{7,6},{8,9},{9,8},{10,11... | collective-permute-start | bytes 466952 | tf_op jit(solution)/shard_map/ppermute | solution.py:112
  143.7 10.7 %collective-permute-start.47 = (bf16[32,4864]{1,0:T(8,128)(2,1)S(1)}, bf16[32,4864]{1,0:T(8,128)(2,1)S(1)}, u32[]{:S(2)}, u32[]{:S(2)}) collective-permute-start(bf16[32,4864]{1,0:T(8,128)(2,1)S(1)} %pad_maximum_fusion.6), channel_id=1, source_target_pairs={{1,5},{3,7},{4,0},{5,9},{6,2},{7,11},{8,4},{9,13},{10,6},{11,15},{... | collective-permute-start | bytes 933896 | tf_op jit(solution)/shard_map/ppermute | solution.py:112
  154.5 8.8 %collective-permute-start.48 = (bf16[32,4864]{1,0:T(8,128)(2,1)S(1)}, bf16[32,4864]{1,0:T(8,128)(2,1)S(1)}, u32[]{:S(2)}, u32[]{:S(2)}) collective-permute-start(bf16[32,4864]{1,0:T(8,128)(2,1)S(1)} %add_convert_fusion.6), channel_id=1, source_target_pairs={{1,5},{3,7},{4,0},{5,9},{6,2},{7,11},{8,4},{9,13},{10,6},{11,15},{... | collective-permute-start | bytes 933896 | tf_op jit(solution)/shard_map/ppermute | solution.py:112
  155.9 9.6 %collective-permute-start.35 = (bf16[16,2304]{1,0:T(8,128)(2,1)S(1)}, bf16[16,2304]{1,0:T(8,128)(2,1)S(1)}, u32[]{:S(2)}, u32[]{:S(2)}) collective-permute-start(bf16[16,2304]{1,0:T(8,128)(2,1)S(1)} %get-tuple-element.36), channel_id=1, source_target_pairs={{0,16},{1,3},{2,18},{3,1},{4,20},{5,7},{6,22},{7,5},{8,24},{9,11},... | collective-permute-start | bytes 221192 | tf_op jit(solution)/shard_map/ppermute | solution.py:112
  164.1 9.0 %collective-permute-start.49 = (bf16[32,4864]{1,0:T(8,128)(2,1)}, bf16[32,4864]{1,0:T(8,128)(2,1)S(1)}, u32[]{:S(2)}, u32[]{:S(2)}) collective-permute-start(bf16[32,4864]{1,0:T(8,128)(2,1)} %add_convert_fusion.5), channel_id=1, source_target_pairs={{1,5},{3,7},{4,0},{5,9},{6,2},{7,11},{8,4},{9,13},{10,6},{11,15},{... | collective-permute-start | bytes 933896 | tf_op jit(solution)/shard_map/ppermute | solution.py:112
  (29 other events, 254.7 us)

commit v2 on v0

--- a/solution.py
+++ b/solution.py
@@ -1,13 +1,16 @@
+import functools
 import math
 
 import jax
 import jax.numpy as jnp
 from jax import lax
+from jax.experimental import pallas as pl
+from jax.experimental.pallas import tpu as pltpu
 from jax.sharding import PartitionSpec as P
 
 LAT = 512
 TOP = 8
-
+AXES = ("sec", "dev")
 
 score_scale = 1.0 / math.sqrt(192.0)
 
@@ -65,12 +68,12 @@
     section_count = lax.axis_size("sec")
     doubled = jnp.concatenate([send_buf] * section_count, axis=0)
     halves = expert_rows(
-        lax.all_to_all(doubled, ("sec", "dev"), split_axis=0, concat_axis=0, tiled=True),
+        lax.all_to_all(doubled, AXES, split_axis=0, concat_axis=0, tiled=True),
         gate_weight,
         up_weight,
         down_weight,
     )
-    returned = lax.all_to_all(halves, ("sec", "dev"), split_axis=0, concat_axis=0, tiled=True)
+    returned = lax.all_to_all(halves, AXES, split_axis=0, concat_axis=0, tiled=True)
     pieces = returned.reshape((section_count,) + send_buf.shape).astype(jnp.float32)
     return jnp.sum(pieces, axis=0).astype(jnp.bfloat16)
 
@@ -78,6 +81,179 @@
 def combine(returned, mixing):
     flat_back = returned.reshape(-1, returned.shape[-1]).astype(jnp.float32)
     return jnp.dot(mixing, flat_back, precision=lax.Precision.HIGHEST).astype(jnp.bfloat16)
+
+
+def routed_sparse(
+    hidden_in, expert_ids, gate_coef, gate_weight, up_weight, down_weight, half_rows, capacity
+):
+    model_width = hidden_in.shape[1]
+    expert_count = lax.axis_size("dev")
+    outs = []
+    for offset in (0, half_rows):
+        picker, mixing = routing_tables(
+            expert_ids[offset : offset + half_rows],
+            gate_coef[offset : offset + half_rows],
+            expert_count,
+            capacity,
+        )
+        gathered = jnp.dot(
+            picker, hidden_in[offset : offset + half_rows], preferred_element_type=jnp.float32
+        ).astype(jnp.bfloat16)
+        send_buf = gathered.reshape(expert_count, capacity, model_width)
+        outs.append(combine(route_tokens(send_buf, gate_weight, up_weight, down_weight), mixing))
+    return jnp.concatenate(outs, axis=0)
+
+
+def permutation(n_dev, move):
+    pairs = []
+    for y in range(2):
+        for d in range(n_dev):
+            there = move(y, d // 4, (d // 2) % 2, d % 2)
+            if there is not None:
+                ty, tz, tx, tc = there
+                pairs.append((y * n_dev + d, ty * n_dev + tz * 4 + tx * 2 + tc))
+    return lambda a: lax.ppermute(a, AXES, pairs)
+
+
+class Moves:
+    def __init__(self, n_dev):
+        line = n_dev // 4
+        self.line = line
+        self.core = permutation(n_dev, lambda y, z, x, c: (y, z, x, 1 - c))
+        self.first = permutation(
+            n_dev, lambda y, z, x, c: (1 - y, z, x, c) if c else (y, z, 1 - x, c)
+        )
+        self.second = permutation(
+            n_dev, lambda y, z, x, c: (y, z, 1 - x, c) if c else (1 - y, z, x, c)
+        )
+        self.ring = permutation(n_dev, lambda y, z, x, c: (y, (z + 1) % line, x, c))
+
+
+def plus(*terms):
+    total = terms[0].astype(jnp.float32)
+    for t in terms[1:]:
+        total = total + t.astype(jnp.float32)
+    return total.astype(jnp.bfloat16)
+
+
+def plane_gather(mv, block):
+    near = jnp.concatenate([block, mv.first(block)], axis=0)
+    far = mv.second(near)
+    return [near, far, mv.core(near), mv.core(far)]
+
+
+def plane_sum(mv, y, *more):
+    near, far, other_near, other_far = y
+    half = near.shape[0] // 2
+    crossed = mv.second(plus(far, mv.core(other_far)))
+    other = mv.core(other_near)
+    side = plus(near[half:], other[half:], crossed[half:])
+    return plus(near[:half], other[:half], crossed[:half], mv.first(side), *more)
+
+
+def spread_coefs(expert_ids, gate_coef, expert_count):
+    hot = expert_ids[:, :, None] == jnp.arange(expert_count, dtype=jnp.int32)[None, None, :]
+    dense = jnp.sum(jnp.where(hot, gate_coef[:, :, None], 0.0), axis=1)
+    high = lax.reduce_precision(dense, 8, 7)
+    parts = jnp.concatenate([high, dense - high], axis=1).astype(jnp.bfloat16)
+    pad = -parts.shape[1] % 128
+    return jnp.pad(parts, ((0, 0), (0, pad)))
+
+
+def expert_kernel(n_x, n_experts, steps, me, w_gate, w_up, w_down, *refs):
+    xs, outs = refs[:n_x], refs[n_x : 2 * n_x]
+    x, acc_gate, acc_up, hidden, coef, y, x_sem, y_sem = refs[2 * n_x :]
+    rows = xs[0].shape[0]
+    width = w_gate.shape[1]
+    chunk = width // steps
+    part = [pl.ds(k * chunk, chunk) for k in range(steps)]
+    group = [pl.ds(j * rows, rows) for j in range(n_x)]
+    x_in = [pltpu.make_async_copy(xs[j], x.at[group[j]], x_sem) for j in range(n_x)]
+    for c in x_in:
+        c.start()
+    for c in x_in:
+        c.wait()
+    tail = x[:, width:].astype(jnp.float32)
+    lane = lax.broadcasted_iota(jnp.int32, tail.shape, 1)
+    mine = (lane == me[0]) | (lane == me[0] + n_experts)
+    picked = jnp.sum(jnp.where(mine, tail, 0.0), axis=1, keepdims=True)
+    coef[...] = jnp.broadcast_to(picked, coef.shape)
+    for k in range(steps):
+        xk = x[:, part[k]]
+        g = jnp.dot(xk, w_gate[0, part[k], :], preferred_element_type=jnp.float32)
+        u = jnp.dot(xk, w_up[0, part[k], :], preferred_element_type=jnp.float32)
+        if k == 0:
+            acc_gate[...] = g
+            acc_up[...] = u
+        else:
+            acc_gate[...] += g
+            acc_up[...] += u
+    g = acc_gate[...]
+    hidden[...] = (g / (1.0 + jnp.exp(-g)) * acc_up[...]).astype(jnp.bfloat16)
+    y_out = []
+    for k in range(steps):
+        yk = jnp.dot(hidden[...], w_down[0, :, part[k]], preferred_element_type=jnp.float32)
+        y[:, part[k]] = (yk * coef[:, :1]).astype(jnp.bfloat16)
+        for j in range(n_x):
+            c = pltpu.make_async_copy(y.at[group[j], part[k]], outs[j].at[:, part[k]], y_sem)
+            c.start()
+            y_out.append(c)
+    for c in y_out:
+        c.wait()
+
+
+def expert_group(xs, gate_weight, up_weight, down_weight, n_experts):
+    rows, total = xs[0].shape
+    _, width, hidden_width = gate_weight.shape
+    chunk = max(c for c in range(128, 1025, 128) if width % c == 0)
+    steps = width // chunk
+    n_x = len(xs)
+    m = n_x * rows
+    me = lax.axis_index("dev").astype(jnp.int32).reshape(1)
+    anywhere = pl.BlockSpec(memory_space=pl.ANY)
+    held = pl.BlockSpec(memory_space=pltpu.VMEM)
+    return pl.pallas_call(
+        functools.partial(expert_kernel, n_x, n_experts, steps),
+        in_specs=[pl.BlockSpec(memory_space=pltpu.SMEM)] + [held] * 3 + [anywhere] * n_x,
+        out_specs=[anywhere] * n_x,
+        scratch_shapes=[
+            pltpu.VMEM((m, total), jnp.bfloat16),
+            pltpu.VMEM((m, hidden_width), jnp.float32),
+            pltpu.VMEM((m, hidden_width), jnp.float32),
+            pltpu.VMEM((m, hidden_width), jnp.bfloat16),
+            pltpu.VMEM((m, 128), jnp.float32),
+            pltpu.VMEM((m, width), jnp.bfloat16),
+            pltpu.SemaphoreType.DMA,
+            pltpu.SemaphoreType.DMA,
+        ],
+        out_shape=[jax.ShapeDtypeStruct((rows, width), jnp.bfloat16)] * n_x,
+        compiler_params=pltpu.CompilerParams(vmem_limit_bytes=14 * 2**20),
+        cost_estimate=pl.CostEstimate(
+            flops=6 * m * width * hidden_width,
+            bytes_accessed=6 * width * hidden_width + 4 * m * width,
+            transcendentals=m * hidden_width,
+        ),
+        name="experts",
+    )(me, gate_weight, up_weight, down_weight, *xs)
+
+
+def routed_dense(hidden_in, expert_ids, gate_coef, gate_weight, up_weight, down_weight):
+    n_dev = lax.axis_size("dev")
+    mv = Moves(n_dev)
+    coefs = spread_coefs(expert_ids, gate_coef, n_dev)
+    blocks = [jnp.concatenate([hidden_in, coefs], axis=1)]
+    for _ in range(mv.line - 1):
+        blocks.append(mv.ring(blocks[-1]))
+    gathered = [plane_gather(mv, b) for b in blocks]
+    half = mv.line // 2
+    sums = []
+    for group in (gathered[:half], gathered[half:]):
+        ys = expert_group(sum(group, []), gate_weight, up_weight, down_weight, n_dev)
+        sums += [ys[4 * k : 4 * k + 4] for k in range(len(group))]
+    acc = None
+    for y in sums[1:]:
+        acc = mv.ring(plane_sum(mv, y) if acc is None else plane_sum(mv, y, acc))
+    return plane_sum(mv, sums[0], acc)
 
 
 def per_device(
@@ -92,31 +268,16 @@
     down_weight,
 ):
     half_rows = hidden_in.shape[0] // 2
-    model_width = hidden_in.shape[1]
     expert_count = lax.axis_size("dev")
     capacity = max(2, 2 * TOP * half_rows // expert_count)
-    tables = []
-    send_bufs = []
-    for offset in (0, half_rows):
-        picker, mixing = routing_tables(
-            expert_ids[offset : offset + half_rows],
-            gate_coef[offset : offset + half_rows],
-            expert_count,
-            capacity,
-        )
-        tables.append(mixing)
-        gathered = jnp.dot(
-            picker, hidden_in[offset : offset + half_rows], preferred_element_type=jnp.float32
-        ).astype(jnp.bfloat16)
-        send_bufs.append(gathered.reshape(expert_count, capacity, model_width))
-    first_attention = attend(query_lat[:half_rows], kv_cache[:half_rows], cache_len[:half_rows])
-    first_back = route_tokens(send_bufs[0], gate_weight, up_weight, down_weight)
-    second_attention = attend(query_lat[half_rows:], kv_cache[half_rows:], cache_len[half_rows:])
-    second_back = route_tokens(send_bufs[1], gate_weight, up_weight, down_weight)
-    attention = jnp.concatenate([first_attention, second_attention], axis=0)
-    routed_out = jnp.concatenate(
-        [combine(first_back, tables[0]), combine(second_back, tables[1])], axis=0
-    )
+    weights = (gate_weight, up_weight, down_weight)
+    if capacity < half_rows:
+        routed_out = routed_sparse(
+            hidden_in, expert_ids, gate_coef, *weights, half_rows, capacity
+        )
+    else:
+        routed_out = routed_dense(hidden_in, expert_ids, gate_coef, *weights)
+    attention = attend(query_lat, kv_cache, cache_len)
     return (attention, routed_out)
 
 

time: 368 us -> 133 us (0.36)
  waiting for transfers between devices: 283 us -> 57.2 us
  matrix products: 49.6 us -> 6.85 us
  Pallas kernels: 0 us -> 21 us
  starting transfers between devices: 18.2 us -> 30.2 us
  local copies, waits for them, and re-layouts: 1.66 us -> 11 us
  other arithmetic: 14.6 us -> 6 us
    all_to_all x4 -> x0, waiting for transfers between devices: 283 us -> none  [the longest x2 146 us: route_tokens(): lax.all_to_all(doubled, ('sec', 'dev'), split_axis=0, concat_axis=0, tile...]
    ppermute x0 -> x38, waiting for transfers between devices: none -> 57.2 us  [permutation(): return lambda a: lax.ppermute(a, AXES, pairs)]
    dot_general x12 -> x0, matrix products: 43 us -> none  [the longest x2 24.3 us: expert_rows(): jnp.dot(hidden, down_weight[0], preferred_element_type=jnp.float32)]
    ppermute x0 -> x38, starting transfers between devices: none -> 30.2 us  [permutation(): return lambda a: lax.ppermute(a, AXES, pairs)]
    pallas_call x0 -> x2, Pallas kernels: none -> 21 us  [expert_group(): pl.pallas_call(functools.partial(expert_kernel, n_x, n_experts, steps), i...]
    all_to_all x4 -> x0, starting transfers between devices: 18.2 us -> none  [the longest x2 11 us: route_tokens(): lax.all_to_all(doubled, ('sec', 'dev'), split_axis=0, concat_axis=0, tile...]
    unnamed x10 -> x15, local copies, waits for them, and re-layouts: 0.03 us -> 10.9 us
    reduce_sum x4 -> x1, other arithmetic: 7.9 us -> 0.11 us  [spread_coefs(): dense = jnp.sum(jnp.where(hot, gate_coef[:, :, None], 0.0), axis=1)]
  transfers between devices with their start and end apart: 4 -> 38, of which waited for: 4 -> 14; matrix products, arithmetic and copies ran while one was open for 14% -> 7% of each run, Pallas kernels for 0% -> 16%
where the time goes in v2:
time: 133 us
  waiting for transfers between devices  57.2 us (43%)
  starting transfers between devices  30.2 us (23%)
  Pallas kernels  21 us (16%)
  local copies, waits for them, and re-layouts  11 us (8%)
  matrix products  6.85 us (5%)
  other arithmetic  6 us (5%)
    ppermute x38, waiting for transfers between devices, permutation(): return lambda a: lax.ppermute(a, AXES, pairs)  57.2 us
    ppermute x38, starting transfers between devices, permutation(): return lambda a: lax.ppermute(a, AXES, pairs)  30.2 us
    pallas_call x2, Pallas kernels, expert_group(): pl.pallas_call(functools.partial(expert_kernel, n_x, n_experts, steps), i...  21 us
    unnamed x15, local copies, waits for them, and re-layouts  10.9 us
    dot_general x1, matrix products, attend(): jnp.einsum('rhl,rlc->rhc', weights, kv_cache[:, :, :LAT], preferred_eleme...  4.49 us
    convert_element_type x12, other arithmetic, plus(): return total.astype(jnp.bfloat16)  3.75 us
  transfers between devices with their start and end apart: 38, of which 14 were waited for; matrix products, arithmetic and copies ran while one was open for 7% of the time, Pallas kernels for 16%

profile of v2, /device:TPU:0, one launch (start us, length us, event | category | flops | bytes accessed | tf_op | source)
XLA Modules:
  0.0 133.1 jit_solution(5191102111764638830)
XLA Ops:
  3.4 3.0 %collective-permute-start = (bf16[16,7296]{1,0:T(8,128)(2,1)S(1)}, bf16[16,7296]{1,0:T(8,128)(2,1)S(1)}, u32[]{:S(2)}, u32[]{:S(2)}) collective-permute-start(bf16[16,7296]{1,0:T(8,128)(2,1)S(1)} %pad_maximum_fusion.1), channel_id=1, source_target_pairs={{0,2},{1,17},{2,0},{3,19},{4,6},{5,21},{6,4},{7,23},{8,10},{9,25},... | collective-permute-start | bytes 700424 | tf_op jit(solution)/shard_map/ppermute | solution.py:115
  6.4 1.6 %collective-permute-start.4 = (bf16[16,7296]{1,0:T(8,128)(2,1)S(1)}, bf16[16,7296]{1,0:T(8,128)(2,1)S(1)}, u32[]{:S(2)}, u32[]{:S(2)}) collective-permute-start(bf16[16,7296]{1,0:T(8,128)(2,1)S(1)} %pad_maximum_fusion.1), channel_id=1, source_target_pairs={{0,4},{1,5},{2,6},{3,7},{4,8},{5,9},{6,10},{7,11},{8,12},{9,13},{1... | collective-permute-start | bytes 700424 | tf_op jit(solution)/shard_map/ppermute | solution.py:115
  8.7 2.4 %fusion.8 = f32[16,64,128]{2,1,0:T(8,128)S(1)} fusion(bf16[16,64,576]{2,1,0:T(8,128)(2,1)S(1)} %copy-done, bf16[16,128,576]{1,2,0:T(8,128)(2,1)} %param.13, pred[16,128]{1,0:T(8,128)(4,1)S(1)} %iota_compare_fusion.2), kind=kOutput, calls=%fused_computation.7 | convolution fusion | flops 151257088 | bytes 4065280 | tf_op jit(solution)/shard_map/rhk,rlk->rhl/dot_general | solution.py:20
  11.5 1.6 %collective-permute-start.1 = (bf16[32,7296]{1,0:T(8,128)(2,1)S(1)}, bf16[32,7296]{1,0:T(8,128)(2,1)S(1)}, u32[]{:S(2)}, u32[]{:S(2)}) collective-permute-start(bf16[32,7296]{1,0:T(8,128)(2,1)S(1)} %pad_maximum_fusion.refs_0_), channel_id=1, source_target_pairs={{0,16},{1,3},{2,18},{3,1},{4,20},{5,7},{6,22},{7,5},{8,24},{9,11},... | collective-permute-start | bytes 1400840 | tf_op jit(solution)/shard_map/ppermute | solution.py:115
  13.1 2.4 %collective-permute-done.4 = bf16[16,7296]{1,0:T(8,128)(2,1)S(1)} collective-permute-done((bf16[16,7296]{1,0:T(8,128)(2,1)S(1)}, bf16[16,7296]{1,0:T(8,128)(2,1)S(1)}, u32[]{:S(2)}, u32[]{:S(2)}) %collective-permute-start.4) | collective-permute-done | bytes 233504 | tf_op jit(solution)/shard_map/ppermute | solution.py:115
  15.5 1.5 %collective-permute-start.5 = (bf16[16,7296]{1,0:T(8,128)(2,1)S(1)}, bf16[16,7296]{1,0:T(8,128)(2,1)S(1)}, u32[]{:S(2)}, u32[]{:S(2)}) collective-permute-start(bf16[16,7296]{1,0:T(8,128)(2,1)S(1)} %collective-permute-done.4), channel_id=1, source_target_pairs={{0,2},{1,17},{2,0},{3,19},{4,6},{5,21},{6,4},{7,23},{8,10},{9,25},... | collective-permute-start | bytes 700424 | tf_op jit(solution)/shard_map/ppermute | solution.py:115
  17.0 4.5 %collective-permute-done.5 = bf16[16,7296]{1,0:T(8,128)(2,1)S(1)} collective-permute-done((bf16[16,7296]{1,0:T(8,128)(2,1)S(1)}, bf16[16,7296]{1,0:T(8,128)(2,1)S(1)}, u32[]{:S(2)}, u32[]{:S(2)}) %collective-permute-start.5) | collective-permute-done | bytes 233504 | tf_op jit(solution)/shard_map/ppermute | solution.py:115
  22.1 1.5 %collective-permute-start.7 = (bf16[32,7296]{1,0:T(8,128)(2,1)S(1)}, bf16[32,7296]{1,0:T(8,128)(2,1)S(1)}, u32[]{:S(2)}, u32[]{:S(2)}) collective-permute-start(bf16[32,7296]{1,0:T(8,128)(2,1)S(1)} %constant_dynamic-update-slice_fusion.refs_4_), channel_id=1, source_target_pairs={{0,1},{1,0},{2,3},{3,2},{4,5},{5,4},{6,7},{7,6},{8,9},{9,8},{10,11... | collective-permute-start | bytes 1400840 | tf_op jit(solution)/shard_map/ppermute | solution.py:115
  23.6 1.3 collective-permute-done.13
  24.9 1.5 %collective-permute-start.14 = (bf16[16,7296]{1,0:T(8,128)(2,1)S(1)}, bf16[16,7296]{1,0:T(8,128)(2,1)S(1)}, u32[]{:S(2)}, u32[]{:S(2)}) collective-permute-start(bf16[16,7296]{1,0:T(8,128)(2,1)S(1)} %collective-permute-done.13), channel_id=1, source_target_pairs={{0,2},{1,17},{2,0},{3,19},{4,6},{5,21},{6,4},{7,23},{8,10},{9,25},... | collective-permute-start | bytes 700424 | tf_op jit(solution)/shard_map/ppermute | solution.py:115
  26.4 5.8 %collective-permute-done.14 = bf16[16,7296]{1,0:T(8,128)(2,1)S(1)} collective-permute-done((bf16[16,7296]{1,0:T(8,128)(2,1)S(1)}, bf16[16,7296]{1,0:T(8,128)(2,1)S(1)}, u32[]{:S(2)}, u32[]{:S(2)}) %collective-permute-start.14) | collective-permute-done | bytes 233504 | tf_op jit(solution)/shard_map/ppermute | solution.py:115
  33.5 7.2 %collective-permute-done.18 = bf16[16,7296]{1,0:T(8,128)(2,1)S(1)} collective-permute-done((bf16[16,7296]{1,0:T(8,128)(2,1)S(1)}, bf16[16,7296]{1,0:T(8,128)(2,1)S(1)}, u32[]{:S(2)}, u32[]{:S(2)}) %collective-permute-start.18) | collective-permute-done | bytes 233504 | tf_op jit(solution)/shard_map/ppermute | solution.py:115
  41.3 2.7 %collective-permute-start.19 = (bf16[16,7296]{1,0:T(8,128)(2,1)S(1)}, bf16[16,7296]{1,0:T(8,128)(2,1)S(1)}, u32[]{:S(2)}, u32[]{:S(2)}) collective-permute-start(bf16[16,7296]{1,0:T(8,128)(2,1)S(1)} %collective-permute-done.18), channel_id=1, source_target_pairs={{0,2},{1,17},{2,0},{3,19},{4,6},{5,21},{6,4},{7,23},{8,10},{9,25},... | collective-permute-start | bytes 700424 | tf_op jit(solution)/shard_map/ppermute | solution.py:115
  44.1 3.1 %copy-done.1 = bf16[1,7168,512]{2,1,0:T(8,128)(2,1)S(1)} copy-done((bf16[1,7168,512]{2,1,0:T(8,128)(2,1)S(1)}, bf16[1,7168,512]{2,1,0:T(8,128)(2,1)}, u32[]{:S(2)}) %copy-start.1) | copy-done | bytes 7340056
  47.2 3.1 %copy-done.2 = bf16[1,7168,512]{2,1,0:T(8,128)(2,1)S(1)} copy-done((bf16[1,7168,512]{2,1,0:T(8,128)(2,1)S(1)}, bf16[1,7168,512]{2,1,0:T(8,128)(2,1)}, u32[]{:S(2)}) %copy-start.2) | copy-done | bytes 7340056
  50.3 3.1 %copy-done.3 = bf16[1,512,7168]{2,1,0:T(8,128)(2,1)S(1)} copy-done((bf16[1,512,7168]{2,1,0:T(8,128)(2,1)S(1)}, bf16[1,512,7168]{2,1,0:T(8,128)(2,1)}, u32[]{:S(2)}) %copy-start.3) | copy-done | bytes 7340056
  53.3 10.4 %experts.2 = (bf16[32,7168]{1,0:T(8,128)(2,1)S(1)}, bf16[32,7168]{1,0:T(8,128)(2,1)S(1)}, bf16[32,7168]{1,0:T(8,128)(2,1)S(1)}, bf16[32,7168]{1,0:T(8,128)(2,1)S...) custom-call(s32[1]{0:T(128)} %bitcast.me, ...), custom_call_target="tpu_custom_call" | custom-call | flops 5637144576 | bytes 29360128 | tf_op jit(solution)/shard_map/experts/pallas_call | solution.py:215
  66.5 5.9 %collective-permute-done.20.refs_5_ = bf16[32,7296]{1,0:T(8,128)(2,1)S(1)} collective-permute-done((bf16[32,7296]{1,0:T(8,128)(2,1)S(1)}, bf16[32,7296]{1,0:T(8,128)(2,1)S(1)}, u32[]{:S(2)}, u32[]{:S(2)}) %collective-permute-start.20) | collective-permute-done | bytes 466976 | tf_op jit(solution)/shard_map/ppermute | solution.py:115
  74.1 1.2 collective-permute-start.11
  75.3 10.6 %experts.3 = (bf16[32,7168]{1,0:T(8,128)(2,1)S(1)}, bf16[32,7168]{1,0:T(8,128)(2,1)S(1)}, bf16[32,7168]{1,0:T(8,128)(2,1)S(1)}, bf16[32,7168]{1,0:T(8,128)(2,1)S...) custom-call(s32[1]{0:T(128)} %bitcast.me, ...), custom_call_target="tpu_custom_call" | custom-call | flops 5637144576 | bytes 29360128 | tf_op jit(solution)/shard_map/experts/pallas_call | solution.py:215
  89.1 1.9 %collective-permute-start.34 = (bf16[16,7168]{1,0:T(8,128)(2,1)S(1)}, bf16[16,7168]{1,0:T(8,128)(2,1)S(1)}, u32[]{:S(2)}, u32[]{:S(2)}) collective-permute-start(bf16[16,7168]{1,0:T(8,128)(2,1)S(1)} %add_convert_fusion.8), channel_id=1, source_target_pairs={{0,2},{1,17},{2,0},{3,19},{4,6},{5,21},{6,4},{7,23},{8,10},{9,25},... | collective-permute-start | bytes 688136 | tf_op jit(solution)/shard_map/ppermute | solution.py:115
  91.1 4.0 %collective-permute-done.34 = bf16[16,7168]{1,0:T(8,128)(2,1)S(1)} collective-permute-done((bf16[16,7168]{1,0:T(8,128)(2,1)S(1)}, bf16[16,7168]{1,0:T(8,128)(2,1)S(1)}, u32[]{:S(2)}, u32[]{:S(2)}) %collective-permute-start.34) | collective-permute-done | bytes 229408 | tf_op jit(solution)/shard_map/ppermute | solution.py:115
  96.0 1.3 collective-permute-start.25
  97.3 6.3 %collective-permute-done.29 = bf16[32,7168]{1,0:T(8,128)(2,1)S(1)} collective-permute-done((bf16[32,7168]{1,0:T(8,128)(2,1)S(1)}, bf16[32,7168]{1,0:T(8,128)(2,1)S(1)}, u32[]{:S(2)}, u32[]{:S(2)}) %collective-permute-start.29) | collective-permute-done | bytes 458784 | tf_op jit(solution)/shard_map/ppermute | solution.py:115
  103.7 2.0 %collective-permute-start.30 = (bf16[16,7168]{1,0:T(8,128)(2,1)S(1)}, bf16[16,7168]{1,0:T(8,128)(2,1)S(1)}, u32[]{:S(2)}, u32[]{:S(2)}) collective-permute-start(bf16[16,7168]{1,0:T(8,128)(2,1)S(1)} %add_convert_fusion.9), channel_id=1, source_target_pairs={{0,2},{1,17},{2,0},{3,19},{4,6},{5,21},{6,4},{7,23},{8,10},{9,25},... | collective-permute-start | bytes 688136 | tf_op jit(solution)/shard_map/ppermute | solution.py:115
  105.6 6.3 %collective-permute-done.25 = bf16[32,7168]{1,0:T(8,128)(2,1)S(1)} collective-permute-done((bf16[32,7168]{1,0:T(8,128)(2,1)S(1)}, bf16[32,7168]{1,0:T(8,128)(2,1)S(1)}, u32[]{:S(2)}, u32[]{:S(2)}) %collective-permute-start.25) | collective-permute-done | bytes 458784 | tf_op jit(solution)/shard_map/ppermute | solution.py:115
  112.1 2.1 %collective-permute-start.26 = (bf16[16,7168]{1,0:T(8,128)(2,1)S(1)}, bf16[16,7168]{1,0:T(8,128)(2,1)S(1)}, u32[]{:S(2)}, u32[]{:S(2)}) collective-permute-start(bf16[16,7168]{1,0:T(8,128)(2,1)S(1)} %add_convert_fusion.10), channel_id=1, source_target_pairs={{0,2},{1,17},{2,0},{3,19},{4,6},{5,21},{6,4},{7,23},{8,10},{9,25},... | collective-permute-start | bytes 688136 | tf_op jit(solution)/shard_map/ppermute | solution.py:115
  114.6 3.6 %collective-permute-done.26 = bf16[16,7168]{1,0:T(8,128)(2,1)S(1)} collective-permute-done((bf16[16,7168]{1,0:T(8,128)(2,1)S(1)}, bf16[16,7168]{1,0:T(8,128)(2,1)S(1)}, u32[]{:S(2)}, u32[]{:S(2)}) %collective-permute-start.26) | collective-permute-done | bytes 229408 | tf_op jit(solution)/shard_map/ppermute | solution.py:115
  118.2 4.0 %collective-permute-done.36 = bf16[16,7168]{1,0:T(8,128)(2,1)S(1)} collective-permute-done((bf16[16,7168]{1,0:T(8,128)(2,1)S(1)}, bf16[16,7168]{1,0:T(8,128)(2,1)S(1)}, u32[]{:S(2)}, u32[]{:S(2)}) %collective-permute-start.36) | collective-permute-done | bytes 229408 | tf_op jit(solution)/shard_map/ppermute | solution.py:115
  123.1 4.5 %fusion.3 = bf16[16,64,512]{2,1,0:T(8,128)(2,1)} fusion(bf16[16,128,576]{1,2,0:T(8,128)(2,1)} %param.13, f32[16,64]{1,0:T(8,128)S(1)} %fusion.15, f32[16,64,128]{2,1,0:T(8,128)S(1)} %fusion.8), kind=kOutput, calls=%fused_computation.3 | convolution fusion | flops 135136384 | bytes 4202496 | tf_op jit(solution)/shard_map/rhl,rlc->rhc/dot_general | solution.py:30
  127.6 3.6 %collective-permute-done.37 = bf16[16,7168]{1,0:T(8,128)(2,1)} collective-permute-done((bf16[16,7168]{1,0:T(8,128)(2,1)}, bf16[16,7168]{1,0:T(8,128)(2,1)}, u32[]{:S(2)}, u32[]{:S(2)}) %collective-permute-start.37) | collective-permute-done | bytes 229408 | tf_op jit(solution)/shard_map/ppermute | solution.py:115
  131.2 1.9 %add_convert_fusion.4 = bf16[16,7168]{1,0:T(8,128)(2,1)} fusion(bf16[16,7168]{1,0:T(8,128)(2,1)} %collective-permute-done.37, bf16[16,7168]{1,0:T(8,128)(2,1)} %collective-permute-done.12, bf16[32,7168]{1,0:T(8,128)(2,1)S(1)} %collective-permute-done.11, bf16[32,7168]{1,0:T(8,128)(2,1)S(1)} %collective-permute-done.9, bf16[32,7168]{1,0:T(8,128)(2,1)S(1)} %get-tuple-element.18), kind=kLoop, calls=%fused_computation.14 | loop fusion | flops 1146880 | bytes 1376256 | tf_op jit(solution)/shard_map/convert_element_type | solution.py:136
  (85 shorter events, 16.5 us)
Async XLA Ops:
  3.4 8.0 %collective-permute-start = (bf16[16,7296]{1,0:T(8,128)(2,1)S(1)}, bf16[16,7296]{1,0:T(8,128)(2,1)S(1)}, u32[]{:S(2)}, u32[]{:S(2)}) collective-permute-start(bf16[16,7296]{1,0:T(8,128)(2,1)S(1)} %pad_maximum_fusion.1), channel_id=1, source_target_pairs={{0,2},{1,17},{2,0},{3,19},{4,6},{5,21},{6,4},{7,23},{8,10},{9,25},... | collective-permute-start | bytes 700424 | tf_op jit(solution)/shard_map/ppermute | solution.py:115
  6.4 9.0 %collective-permute-start.4 = (bf16[16,7296]{1,0:T(8,128)(2,1)S(1)}, bf16[16,7296]{1,0:T(8,128)(2,1)S(1)}, u32[]{:S(2)}, u32[]{:S(2)}) collective-permute-start(bf16[16,7296]{1,0:T(8,128)(2,1)S(1)} %pad_maximum_fusion.1), channel_id=1, source_target_pairs={{0,4},{1,5},{2,6},{3,7},{4,8},{5,9},{6,10},{7,11},{8,12},{9,13},{1... | collective-permute-start | bytes 700424 | tf_op jit(solution)/shard_map/ppermute | solution.py:115
  11.5 21.1 %collective-permute-start.1 = (bf16[32,7296]{1,0:T(8,128)(2,1)S(1)}, bf16[32,7296]{1,0:T(8,128)(2,1)S(1)}, u32[]{:S(2)}, u32[]{:S(2)}) collective-permute-start(bf16[32,7296]{1,0:T(8,128)(2,1)S(1)} %pad_maximum_fusion.refs_0_), channel_id=1, source_target_pairs={{0,16},{1,3},{2,18},{3,1},{4,20},{5,7},{6,22},{7,5},{8,24},{9,11},... | collective-permute-start | bytes 1400840 | tf_op jit(solution)/shard_map/ppermute | solution.py:115
  13.1 28.1 %collective-permute-start.2 = (bf16[32,7296]{1,0:T(8,128)(2,1)S(1)}, bf16[32,7296]{1,0:T(8,128)(2,1)S(1)}, u32[]{:S(2)}, u32[]{:S(2)}) collective-permute-start(bf16[32,7296]{1,0:T(8,128)(2,1)S(1)} %pad_maximum_fusion.refs_0_), channel_id=1, source_target_pairs={{0,1},{1,0},{2,3},{3,2},{4,5},{5,4},{6,7},{7,6},{8,9},{9,8},{10,11... | collective-permute-start | bytes 1400840 | tf_op jit(solution)/shard_map/ppermute | solution.py:115
  15.5 6.1 %collective-permute-start.5 = (bf16[16,7296]{1,0:T(8,128)(2,1)S(1)}, bf16[16,7296]{1,0:T(8,128)(2,1)S(1)}, u32[]{:S(2)}, u32[]{:S(2)}) collective-permute-start(bf16[16,7296]{1,0:T(8,128)(2,1)S(1)} %collective-permute-done.4), channel_id=1, source_target_pairs={{0,2},{1,17},{2,0},{3,19},{4,6},{5,21},{6,4},{7,23},{8,10},{9,25},... | collective-permute-start | bytes 700424 | tf_op jit(solution)/shard_map/ppermute | solution.py:115
  17.0 7.9 %collective-permute-start.13 = (bf16[16,7296]{1,0:T(8,128)(2,1)S(1)}, bf16[16,7296]{1,0:T(8,128)(2,1)S(1)}, u32[]{:S(2)}, u32[]{:S(2)}) collective-permute-start(bf16[16,7296]{1,0:T(8,128)(2,1)S(1)} %collective-permute-done.4), channel_id=1, source_target_pairs={{0,4},{1,5},{2,6},{3,7},{4,8},{5,9},{6,10},{7,11},{8,12},{9,13},{1... | collective-permute-start | bytes 700424 | tf_op jit(solution)/shard_map/ppermute | solution.py:115
  21.6 19.2 %collective-permute-start.6 = (bf16[32,7296]{1,0:T(8,128)(2,1)S(1)}, bf16[32,7296]{1,0:T(8,128)(2,1)S(1)}, u32[]{:S(2)}, u32[]{:S(2)}) collective-permute-start(bf16[32,7296]{1,0:T(8,128)(2,1)S(1)} %constant_dynamic-update-slice_fusion.refs_4_), channel_id=1, source_target_pairs={{0,16},{1,3},{2,18},{3,1},{4,20},{5,7},{6,22},{7,5},{8,24},{9,11},... | collective-permute-start | bytes 1400840 | tf_op jit(solution)/shard_map/ppermute | solution.py:115
  22.1 19.2 %collective-permute-start.7 = (bf16[32,7296]{1,0:T(8,128)(2,1)S(1)}, bf16[32,7296]{1,0:T(8,128)(2,1)S(1)}, u32[]{:S(2)}, u32[]{:S(2)}) collective-permute-start(bf16[32,7296]{1,0:T(8,128)(2,1)S(1)} %constant_dynamic-update-slice_fusion.refs_4_), channel_id=1, source_target_pairs={{0,1},{1,0},{2,3},{3,2},{4,5},{5,4},{6,7},{7,6},{8,9},{9,8},{10,11... | collective-permute-start | bytes 1400840 | tf_op jit(solution)/shard_map/ppermute | solution.py:115
  24.9 7.3 %collective-permute-start.14 = (bf16[16,7296]{1,0:T(8,128)(2,1)S(1)}, bf16[16,7296]{1,0:T(8,128)(2,1)S(1)}, u32[]{:S(2)}, u32[]{:S(2)}) collective-permute-start(bf16[16,7296]{1,0:T(8,128)(2,1)S(1)} %collective-permute-done.13), channel_id=1, source_target_pairs={{0,2},{1,17},{2,0},{3,19},{4,6},{5,21},{6,4},{7,23},{8,10},{9,25},... | collective-permute-start | bytes 700424 | tf_op jit(solution)/shard_map/ppermute | solution.py:115
  32.2 8.5 %collective-permute-start.18 = (bf16[16,7296]{1,0:T(8,128)(2,1)S(1)}, bf16[16,7296]{1,0:T(8,128)(2,1)S(1)}, u32[]{:S(2)}, u32[]{:S(2)}) collective-permute-start(bf16[16,7296]{1,0:T(8,128)(2,1)S(1)} %collective-permute-done.13), channel_id=1, source_target_pairs={{0,4},{1,5},{2,6},{3,7},{4,8},{5,9},{6,10},{7,11},{8,12},{9,13},{1... | collective-permute-start | bytes 700424 | tf_op jit(solution)/shard_map/ppermute | solution.py:115
  32.7 33.2 %collective-permute-start.15 = (bf16[32,7296]{1,0:T(8,128)(2,1)S(1)}, bf16[32,7296]{1,0:T(8,128)(2,1)S(1)}, u32[]{:S(2)}, u32[]{:S(2)}) collective-permute-start(bf16[32,7296]{1,0:T(8,128)(2,1)S(1)} %constant_dynamic-update-slice_fusion.2.refs_0_), channel_id=1, source_target_pairs={{0,16},{1,3},{2,18},{3,1},{4,20},{5,7},{6,22},{7,5},{8,24},{9,11},... | collective-permute-start | bytes 1400840 | tf_op jit(solution)/shard_map/ppermute | solution.py:115
  41.3 31.9 %collective-permute-start.16 = (bf16[32,7296]{1,0:T(8,128)(2,1)S(1)}, bf16[32,7296]{1,0:T(8,128)(2,1)S(1)}, u32[]{:S(2)}, u32[]{:S(2)}) collective-permute-start(bf16[32,7296]{1,0:T(8,128)(2,1)S(1)} %constant_dynamic-update-slice_fusion.2.refs_0_), channel_id=1, source_target_pairs={{0,1},{1,0},{2,3},{3,2},{4,5},{5,4},{6,7},{7,6},{8,9},{9,8},{10,11... | collective-permute-start | bytes 1400840 | tf_op jit(solution)/shard_map/ppermute | solution.py:115
  41.3 22.5 %collective-permute-start.19 = (bf16[16,7296]{1,0:T(8,128)(2,1)S(1)}, bf16[16,7296]{1,0:T(8,128)(2,1)S(1)}, u32[]{:S(2)}, u32[]{:S(2)}) collective-permute-start(bf16[16,7296]{1,0:T(8,128)(2,1)S(1)} %collective-permute-done.18), channel_id=1, source_target_pairs={{0,2},{1,17},{2,0},{3,19},{4,6},{5,21},{6,4},{7,23},{8,10},{9,25},... | collective-permute-start | bytes 700424 | tf_op jit(solution)/shard_map/ppermute | solution.py:115
  63.8 8.6 %collective-permute-start.20 = (bf16[32,7296]{1,0:T(8,128)(2,1)S(1)}, bf16[32,7296]{1,0:T(8,128)(2,1)S(1)}, u32[]{:S(2)}, u32[]{:S(2)}) collective-permute-start(bf16[32,7296]{1,0:T(8,128)(2,1)S(1)} %constant_dynamic-update-slice_fusion.4.refs_4_), channel_id=1, source_target_pairs={{0,16},{1,3},{2,18},{3,1},{4,20},{5,7},{6,22},{7,5},{8,24},{9,11},... | collective-permute-start | bytes 1400840 | tf_op jit(solution)/shard_map/ppermute | solution.py:115
  64.7 8.5 %collective-permute-start.21 = (bf16[32,7296]{1,0:T(8,128)(2,1)S(1)}, bf16[32,7296]{1,0:T(8,128)(2,1)S(1)}, u32[]{:S(2)}, u32[]{:S(2)}) collective-permute-start(bf16[32,7296]{1,0:T(8,128)(2,1)S(1)} %constant_dynamic-update-slice_fusion.4.refs_4_), channel_id=1, source_target_pairs={{0,1},{1,0},{2,3},{3,2},{4,5},{5,4},{6,7},{7,6},{8,9},{9,8},{10,11... | collective-permute-start | bytes 1400840 | tf_op jit(solution)/shard_map/ppermute | solution.py:115
  65.9 8.2 %collective-permute-start.17 = (bf16[32,7296]{1,0:T(8,128)(2,1)S(1)}, bf16[32,7296]{1,0:T(8,128)(2,1)S(1)}, u32[]{:S(2)}, u32[]{:S(2)}) collective-permute-start(bf16[32,7296]{1,0:T(8,128)(2,1)S(1)} %collective-permute-done.15.refs_1_), channel_id=1, source_target_pairs={{0,1},{1,0},{2,3},{3,2},{4,5},{5,4},{6,7},{7,6},{8,9},{9,8},{10,11... | collective-permute-start | bytes 1400840 | tf_op jit(solution)/shard_map/ppermute | solution.py:115
  65.9 6.6 %collective-permute-start.10 = (bf16[32,7168]{1,0:T(8,128)(2,1)S(1)}, bf16[32,7168]{1,0:T(8,128)(2,1)S(1)}, u32[]{:S(2)}, u32[]{:S(2)}) collective-permute-start(bf16[32,7168]{1,0:T(8,128)(2,1)S(1)} %get-tuple-element.21), channel_id=1, source_target_pairs={{0,1},{1,0},{2,3},{3,2},{4,5},{5,4},{6,7},{7,6},{8,9},{9,8},{10,11... | collective-permute-start | bytes 1376264 | tf_op jit(solution)/shard_map/ppermute | solution.py:115
  72.5 13.6 %collective-permute-start.31 = (bf16[32,7168]{1,0:T(8,128)(2,1)S(1)}, bf16[32,7168]{1,0:T(8,128)(2,1)S(1)}, u32[]{:S(2)}, u32[]{:S(2)}) collective-permute-start(bf16[32,7168]{1,0:T(8,128)(2,1)S(1)} %get-tuple-element.31), channel_id=1, source_target_pairs={{0,1},{1,0},{2,3},{3,2},{4,5},{5,4},{6,7},{7,6},{8,9},{9,8},{10,11... | collective-permute-start | bytes 1376264 | tf_op jit(solution)/shard_map/ppermute | solution.py:115
  73.1 41.3 %collective-permute-start.9 = (bf16[32,7168]{1,0:T(8,128)(2,1)S(1)}, bf16[32,7168]{1,0:T(8,128)(2,1)S(1)}, u32[]{:S(2)}, u32[]{:S(2)}) collective-permute-start(bf16[32,7168]{1,0:T(8,128)(2,1)S(1)} %get-tuple-element.19), channel_id=1, source_target_pairs={{0,1},{1,0},{2,3},{3,2},{4,5},{5,4},{6,7},{7,6},{8,9},{9,8},{10,11... | collective-permute-start | bytes 1376264 | tf_op jit(solution)/shard_map/ppermute | solution.py:115
  73.2 13.3 %collective-permute-start.33 = (bf16[32,7168]{1,0:T(8,128)(2,1)S(1)}, bf16[32,7168]{1,0:T(8,128)(2,1)S(1)}, u32[]{:S(2)}, u32[]{:S(2)}) collective-permute-start(bf16[32,7168]{1,0:T(8,128)(2,1)S(1)} %add_convert_fusion), channel_id=1, source_target_pairs={{0,16},{1,3},{2,18},{3,1},{4,20},{5,7},{6,22},{7,5},{8,24},{9,11},... | collective-permute-start | bytes 1376264 | tf_op jit(solution)/shard_map/ppermute | solution.py:115
  74.1 40.3 %collective-permute-start.11 = (bf16[32,7168]{1,0:T(8,128)(2,1)S(1)}, bf16[32,7168]{1,0:T(8,128)(2,1)S(1)}, u32[]{:S(2)}, u32[]{:S(2)}) collective-permute-start(bf16[32,7168]{1,0:T(8,128)(2,1)S(1)} %add_convert_fusion.3), channel_id=1, source_target_pairs={{0,16},{1,3},{2,18},{3,1},{4,20},{5,7},{6,22},{7,5},{8,24},{9,11},... | collective-permute-start | bytes 1376264 | tf_op jit(solution)/shard_map/ppermute | solution.py:115
  86.0 10.0 %collective-permute-start.27 = (bf16[32,7168]{1,0:T(8,128)(2,1)S(1)}, bf16[32,7168]{1,0:T(8,128)(2,1)S(1)}, u32[]{:S(2)}, u32[]{:S(2)}) collective-permute-start(bf16[32,7168]{1,0:T(8,128)(2,1)S(1)} %get-tuple-element.27), channel_id=1, source_target_pairs={{0,1},{1,0},{2,3},{3,2},{4,5},{5,4},{6,7},{7,6},{8,9},{9,8},{10,11... | collective-permute-start | bytes 1376264 | tf_op jit(solution)/shard_map/ppermute | solution.py:115
  87.8 15.9 %collective-permute-start.23 = (bf16[32,7168]{1,0:T(8,128)(2,1)S(1)}, bf16[32,7168]{1,0:T(8,128)(2,1)S(1)}, u32[]{:S(2)}, u32[]{:S(2)}) collective-permute-start(bf16[32,7168]{1,0:T(8,128)(2,1)S(1)} %get-tuple-element.23), channel_id=1, source_target_pairs={{0,1},{1,0},{2,3},{3,2},{4,5},{5,4},{6,7},{7,6},{8,9},{9,8},{10,11... | collective-permute-start | bytes 1376264 | tf_op jit(solution)/shard_map/ppermute | solution.py:115
  89.1 6.0 %collective-permute-start.34 = (bf16[16,7168]{1,0:T(8,128)(2,1)S(1)}, bf16[16,7168]{1,0:T(8,128)(2,1)S(1)}, u32[]{:S(2)}, u32[]{:S(2)}) collective-permute-start(bf16[16,7168]{1,0:T(8,128)(2,1)S(1)} %add_convert_fusion.8), channel_id=1, source_target_pairs={{0,2},{1,17},{2,0},{3,19},{4,6},{5,21},{6,4},{7,23},{8,10},{9,25},... | collective-permute-start | bytes 688136 | tf_op jit(solution)/shard_map/ppermute | solution.py:115
  95.1 8.5 %collective-permute-start.29 = (bf16[32,7168]{1,0:T(8,128)(2,1)S(1)}, bf16[32,7168]{1,0:T(8,128)(2,1)S(1)}, u32[]{:S(2)}, u32[]{:S(2)}) collective-permute-start(bf16[32,7168]{1,0:T(8,128)(2,1)S(1)} %add_convert_fusion.1), channel_id=1, source_target_pairs={{0,16},{1,3},{2,18},{3,1},{4,20},{5,7},{6,22},{7,5},{8,24},{9,11},... | collective-permute-start | bytes 1376264 | tf_op jit(solution)/shard_map/ppermute | solution.py:115
  96.0 15.9 %collective-permute-start.25 = (bf16[32,7168]{1,0:T(8,128)(2,1)S(1)}, bf16[32,7168]{1,0:T(8,128)(2,1)S(1)}, u32[]{:S(2)}, u32[]{:S(2)}) collective-permute-start(bf16[32,7168]{1,0:T(8,128)(2,1)S(1)} %add_convert_fusion.2), channel_id=1, source_target_pairs={{0,16},{1,3},{2,18},{3,1},{4,20},{5,7},{6,22},{7,5},{8,24},{9,11},... | collective-permute-start | bytes 1376264 | tf_op jit(solution)/shard_map/ppermute | solution.py:115
  103.6 10.6 %collective-permute-start.35 = (bf16[16,7168]{1,0:T(8,128)(2,1)S(1)}, bf16[16,7168]{1,0:T(8,128)(2,1)S(1)}, u32[]{:S(2)}, u32[]{:S(2)}) collective-permute-start(bf16[16,7168]{1,0:T(8,128)(2,1)S(1)} %add_convert_fusion.7), channel_id=1, source_target_pairs={{0,4},{1,5},{2,6},{3,7},{4,8},{5,9},{6,10},{7,11},{8,12},{9,13},{1... | collective-permute-start | bytes 688136 | tf_op jit(solution)/shard_map/ppermute | solution.py:115
  103.7 10.5 %collective-permute-start.30 = (bf16[16,7168]{1,0:T(8,128)(2,1)S(1)}, bf16[16,7168]{1,0:T(8,128)(2,1)S(1)}, u32[]{:S(2)}, u32[]{:S(2)}) collective-permute-start(bf16[16,7168]{1,0:T(8,128)(2,1)S(1)} %add_convert_fusion.9), channel_id=1, source_target_pairs={{0,2},{1,17},{2,0},{3,19},{4,6},{5,21},{6,4},{7,23},{8,10},{9,25},... | collective-permute-start | bytes 688136 | tf_op jit(solution)/shard_map/ppermute | solution.py:115
  112.1 6.1 %collective-permute-start.26 = (bf16[16,7168]{1,0:T(8,128)(2,1)S(1)}, bf16[16,7168]{1,0:T(8,128)(2,1)S(1)}, u32[]{:S(2)}, u32[]{:S(2)}) collective-permute-start(bf16[16,7168]{1,0:T(8,128)(2,1)S(1)} %add_convert_fusion.10), channel_id=1, source_target_pairs={{0,2},{1,17},{2,0},{3,19},{4,6},{5,21},{6,4},{7,23},{8,10},{9,25},... | collective-permute-start | bytes 688136 | tf_op jit(solution)/shard_map/ppermute | solution.py:115
  114.4 7.9 %collective-permute-start.36 = (bf16[16,7168]{1,0:T(8,128)(2,1)S(1)}, bf16[16,7168]{1,0:T(8,128)(2,1)S(1)}, u32[]{:S(2)}, u32[]{:S(2)}) collective-permute-start(bf16[16,7168]{1,0:T(8,128)(2,1)S(1)} %add_convert_fusion.6), channel_id=1, source_target_pairs={{0,4},{1,5},{2,6},{3,7},{4,8},{5,9},{6,10},{7,11},{8,12},{9,13},{1... | collective-permute-start | bytes 688136 | tf_op jit(solution)/shard_map/ppermute | solution.py:115
  114.5 13.0 %collective-permute-start.12 = (bf16[16,7168]{1,0:T(8,128)(2,1)S(1)}, bf16[16,7168]{1,0:T(8,128)(2,1)}, u32[]{:S(2)}, u32[]{:S(2)}) collective-permute-start(bf16[16,7168]{1,0:T(8,128)(2,1)S(1)} %add_convert_fusion.11), channel_id=1, source_target_pairs={{0,2},{1,17},{2,0},{3,19},{4,6},{5,21},{6,4},{7,23},{8,10},{9,25},... | collective-permute-start | bytes 688136 | tf_op jit(solution)/shard_map/ppermute | solution.py:115
  123.1 8.1 %collective-permute-start.37 = (bf16[16,7168]{1,0:T(8,128)(2,1)}, bf16[16,7168]{1,0:T(8,128)(2,1)}, u32[]{:S(2)}, u32[]{:S(2)}) collective-permute-start(bf16[16,7168]{1,0:T(8,128)(2,1)} %add_convert_fusion.5), channel_id=1, source_target_pairs={{0,4},{1,5},{2,6},{3,7},{4,8},{5,9},{6,10},{7,11},{8,12},{9,13},{1... | collective-permute-start | bytes 688136 | tf_op jit(solution)/shard_map/ppermute | solution.py:115
  (11 other events, 36.3 us)

commit v3 on v2

--- a/solution.py
+++ b/solution.py
@@ -136,52 +136,75 @@
     return total.astype(jnp.bfloat16)
 
 
-def plane_gather(mv, block):
-    near = jnp.concatenate([block, mv.first(block)], axis=0)
-    far = mv.second(near)
-    return [near, far, mv.core(near), mv.core(far)]
-
-
-def plane_sum(mv, y, *more):
-    near, far, other_near, other_far = y
-    half = near.shape[0] // 2
-    crossed = mv.second(plus(far, mv.core(other_far)))
-    other = mv.core(other_near)
-    side = plus(near[half:], other[half:], crossed[half:])
-    return plus(near[:half], other[:half], crossed[:half], mv.first(side), *more)
-
-
-def spread_coefs(expert_ids, gate_coef, expert_count):
-    hot = expert_ids[:, :, None] == jnp.arange(expert_count, dtype=jnp.int32)[None, None, :]
-    dense = jnp.sum(jnp.where(hot, gate_coef[:, :, None], 0.0), axis=1)
-    high = lax.reduce_precision(dense, 8, 7)
-    parts = jnp.concatenate([high, dense - high], axis=1).astype(jnp.bfloat16)
-    pad = -parts.shape[1] % 128
-    return jnp.pad(parts, ((0, 0), (0, pad)))
-
-
-def expert_kernel(n_x, n_experts, steps, me, w_gate, w_up, w_down, *refs):
-    xs, outs = refs[:n_x], refs[n_x : 2 * n_x]
-    x, acc_gate, acc_up, hidden, coef, y, x_sem, y_sem = refs[2 * n_x :]
-    rows = xs[0].shape[0]
-    width = w_gate.shape[1]
+ANYWHERE = pl.BlockSpec(memory_space=pl.ANY)
+FAR = pl.BlockSpec(memory_space=pltpu.HBM)
+HELD = pl.BlockSpec(memory_space=pltpu.VMEM)
+SCALARS = pl.BlockSpec(memory_space=pltpu.SMEM)
+
+
+def pack_kernel(n_experts, ids, coefs, x, out):
+    rows, width = x.shape
+    hot = lax.broadcasted_iota(jnp.int32, (n_experts, rows), 0)
+    dense = jnp.zeros((n_experts, rows), jnp.float32)
+    for k in range(ids.shape[0]):
+        dense += jnp.where(hot == ids[k : k + 1, :], coefs[k : k + 1, :], 0.0)
+    high = dense.astype(jnp.bfloat16)
+    low = (dense - high.astype(jnp.float32)).astype(jnp.bfloat16)
+    rest = jnp.zeros((out.shape[1] - width - 2 * n_experts, rows), jnp.bfloat16)
+    parts = jnp.concatenate([high, low, rest], axis=0)
+    same = lax.broadcasted_iota(jnp.int32, (rows, rows), 0) == lax.broadcasted_iota(
+        jnp.int32, (rows, rows), 1
+    )
+    turned = lax.dot_general(
+        same.astype(jnp.bfloat16),
+        parts,
+        (((1,), (1,)), ((), ())),
+        preferred_element_type=jnp.float32,
+    )
+    out[:, :width] = x[...]
+    out[:, width:] = turned.astype(jnp.bfloat16)
+
+
+def pack_rows(hidden_in, expert_ids, gate_coef, n_experts):
+    rows, width = hidden_in.shape
+    tail = 2 * n_experts + -2 * n_experts % 128
+    return pl.pallas_call(
+        functools.partial(pack_kernel, n_experts),
+        in_specs=[HELD] * 3,
+        out_specs=HELD,
+        out_shape=jax.ShapeDtypeStruct((rows, width + tail), jnp.bfloat16),
+        name="pack",
+    )(expert_ids.T, gate_coef.T, hidden_in)
+
+
+def expert_kernel(sizes, sizes_out, n_experts, steps, me, gate, up, down, *refs):
+    xs = refs[: len(sizes)]
+    outs = refs[-10 - len(sizes_out) : -10]
+    w_gate, w_up, w_down, acc_gate, acc_up, hidden, coef = refs[-10:-3]
+    gate_sem, up_sem, down_sem = refs[-3:]
+    width = w_gate.shape[0]
     chunk = width // steps
+    copy = pltpu.make_async_copy
     part = [pl.ds(k * chunk, chunk) for k in range(steps)]
-    group = [pl.ds(j * rows, rows) for j in range(n_x)]
-    x_in = [pltpu.make_async_copy(xs[j], x.at[group[j]], x_sem) for j in range(n_x)]
-    for c in x_in:
+    gate_in = [copy(gate.at[0, p], w_gate.at[p], gate_sem.at[k]) for k, p in enumerate(part)]
+    up_in = [copy(up.at[0, p], w_up.at[p], up_sem.at[k]) for k, p in enumerate(part)]
+    down_in = [copy(down.at[0, :, p], w_down.at[:, p], down_sem.at[k]) for k, p in enumerate(part)]
+    for k in range(steps):
+        gate_in[k].start()
+        up_in[k].start()
+    for c in down_in:
         c.start()
-    for c in x_in:
-        c.wait()
-    tail = x[:, width:].astype(jnp.float32)
+    tail = jnp.concatenate([x[:, width:] for x in xs], axis=0).astype(jnp.float32)
     lane = lax.broadcasted_iota(jnp.int32, tail.shape, 1)
     mine = (lane == me[0]) | (lane == me[0] + n_experts)
     picked = jnp.sum(jnp.where(mine, tail, 0.0), axis=1, keepdims=True)
     coef[...] = jnp.broadcast_to(picked, coef.shape)
     for k in range(steps):
-        xk = x[:, part[k]]
-        g = jnp.dot(xk, w_gate[0, part[k], :], preferred_element_type=jnp.float32)
-        u = jnp.dot(xk, w_up[0, part[k], :], preferred_element_type=jnp.float32)
+        gate_in[k].wait()
+        up_in[k].wait()
+        xk = jnp.concatenate([x[:, part[k]] for x in xs], axis=0)
+        g = jnp.dot(xk, w_gate[part[k], :], preferred_element_type=jnp.float32)
+        u = jnp.dot(xk, w_up[part[k], :], preferred_element_type=jnp.float32)
         if k == 0:
             acc_gate[...] = g
             acc_up[...] = u
@@ -190,70 +213,84 @@
             acc_up[...] += u
     g = acc_gate[...]
     hidden[...] = (g / (1.0 + jnp.exp(-g)) * acc_up[...]).astype(jnp.bfloat16)
-    y_out = []
     for k in range(steps):
-        yk = jnp.dot(hidden[...], w_down[0, :, part[k]], preferred_element_type=jnp.float32)
-        y[:, part[k]] = (yk * coef[:, :1]).astype(jnp.bfloat16)
-        for j in range(n_x):
-            c = pltpu.make_async_copy(y.at[group[j], part[k]], outs[j].at[:, part[k]], y_sem)
-            c.start()
-            y_out.append(c)
-    for c in y_out:
-        c.wait()
-
-
-def expert_group(xs, gate_weight, up_weight, down_weight, n_experts):
-    rows, total = xs[0].shape
+        down_in[k].wait()
+        yk = jnp.dot(hidden[...], w_down[:, part[k]], preferred_element_type=jnp.float32)
+        yk = (yk * coef[:, :1]).astype(jnp.bfloat16)
+        row = 0
+        for out in outs:
+            out[:, part[k]] = yk[row : row + out.shape[0]]
+            row += out.shape[0]
+
+
+def expert_group(xs, slots, gate_weight, up_weight, down_weight, n_experts, *after):
+    sizes = [x.shape[0] for x in xs]
+    m = sum(sizes)
     _, width, hidden_width = gate_weight.shape
     chunk = max(c for c in range(128, 1025, 128) if width % c == 0)
     steps = width // chunk
-    n_x = len(xs)
-    m = n_x * rows
+    quarter = m // slots // 4
+    outs = [quarter] * (2 * slots) + [2 * quarter] * slots
     me = lax.axis_index("dev").astype(jnp.int32).reshape(1)
-    anywhere = pl.BlockSpec(memory_space=pl.ANY)
-    held = pl.BlockSpec(memory_space=pltpu.VMEM)
     return pl.pallas_call(
-        functools.partial(expert_kernel, n_x, n_experts, steps),
-        in_specs=[pl.BlockSpec(memory_space=pltpu.SMEM)] + [held] * 3 + [anywhere] * n_x,
-        out_specs=[anywhere] * n_x,
+        functools.partial(expert_kernel, sizes, outs, n_experts, steps),
+        in_specs=[SCALARS] + [FAR] * 3 + [HELD] * len(xs) + [ANYWHERE] * len(after),
+        out_specs=[HELD] * len(outs),
         scratch_shapes=[
-            pltpu.VMEM((m, total), jnp.bfloat16),
+            pltpu.VMEM((width, hidden_width), jnp.bfloat16),
+            pltpu.VMEM((width, hidden_width), jnp.bfloat16),
+            pltpu.VMEM((hidden_width, width), jnp.bfloat16),
             pltpu.VMEM((m, hidden_width), jnp.float32),
             pltpu.VMEM((m, hidden_width), jnp.float32),
             pltpu.VMEM((m, hidden_width), jnp.bfloat16),
             pltpu.VMEM((m, 128), jnp.float32),
-            pltpu.VMEM((m, width), jnp.bfloat16),
-            pltpu.SemaphoreType.DMA,
-            pltpu.SemaphoreType.DMA,
+            pltpu.SemaphoreType.DMA((steps,)),
+            pltpu.SemaphoreType.DMA((steps,)),
+            pltpu.SemaphoreType.DMA((steps,)),
         ],
-        out_shape=[jax.ShapeDtypeStruct((rows, width), jnp.bfloat16)] * n_x,
-        compiler_params=pltpu.CompilerParams(vmem_limit_bytes=14 * 2**20),
+        out_shape=[jax.ShapeDtypeStruct((r, width), jnp.bfloat16) for r in outs],
+        compiler_params=pltpu.CompilerParams(vmem_limit_bytes=28 * 2**20),
         cost_estimate=pl.CostEstimate(
             flops=6 * m * width * hidden_width,
-            bytes_accessed=6 * width * hidden_width + 4 * m * width,
+            bytes_accessed=1,
             transcendentals=m * hidden_width,
         ),
         name="experts",
-    )(me, gate_weight, up_weight, down_weight, *xs)
+    )(me, gate_weight, up_weight, down_weight, *xs, *after)
 
 
 def routed_dense(hidden_in, expert_ids, gate_coef, gate_weight, up_weight, down_weight):
     n_dev = lax.axis_size("dev")
     mv = Moves(n_dev)
-    coefs = spread_coefs(expert_ids, gate_coef, n_dev)
-    blocks = [jnp.concatenate([hidden_in, coefs], axis=1)]
-    for _ in range(mv.line - 1):
-        blocks.append(mv.ring(blocks[-1]))
-    gathered = [plane_gather(mv, b) for b in blocks]
-    half = mv.line // 2
-    sums = []
-    for group in (gathered[:half], gathered[half:]):
-        ys = expert_group(sum(group, []), gate_weight, up_weight, down_weight, n_dev)
-        sums += [ys[4 * k : 4 * k + 4] for k in range(len(group))]
-    acc = None
-    for y in sums[1:]:
-        acc = mv.ring(plane_sum(mv, y) if acc is None else plane_sum(mv, y, acc))
-    return plane_sum(mv, sums[0], acc)
+    weights = (gate_weight, up_weight, down_weight)
+    n = mv.line
+    half = n // 2
+    cat = lambda *a: jnp.concatenate(a, axis=0)
+    block = [pack_rows(hidden_in, expert_ids, gate_coef, n_dev)]
+    for _ in range(n - 1):
+        block.append(mv.ring(block[-1]))
+    near = [cat(b, mv.first(b)) for b in block]
+    far = [mv.second(a) for a in near]
+    pairs = [a for k in range(n) for a in (near[k], far[k])]
+    own = cat(*pairs[: 2 * half])
+    early = expert_group([own, mv.core(own)], half, *weights, n_dev)
+    late = []
+    for k in range(half, n - 1):
+        late.append(cat(near[k], far[k]))
+    late += pairs[2 * n - 2 :]
+    late = expert_group(late + [mv.core(a) for a in late], n - half, *weights, n_dev, early[0])
+    y_near = early[0 : 2 * half : 2] + late[0 : 2 * (n - half) : 2]
+    y_far = early[1 : 2 * half : 2] + late[1 : 2 * (n - half) : 2]
+    mine = [mv.core(a) for a in early[2 * half :] + late[2 * (n - half) :]]
+    rows = block[0].shape[0]
+    acc = ()
+    for k in list(range(1, n)) + [0]:
+        crossed = mv.second(plus(y_far[k], mine[k][2 * rows :]))
+        side = mv.first(plus(y_near[k][rows:], mine[k][rows : 2 * rows], crossed[rows:]))
+        total = plus(y_near[k][:rows], mine[k][:rows], crossed[:rows], side, *acc)
+        if k:
+            acc = (mv.ring(total),)
+    return total
 
 
 def per_device(

time: 133 us -> 118 us (0.89)
  waiting for transfers between devices: 57.2 us -> 51.2 us
  local copies, waits for them, and re-layouts: 11 us -> 5.3 us
  Pallas kernels: 21 us -> 19.3 us
  matrix products: 6.85 us -> 5.19 us
    ppermute x38 -> x30, waiting for transfers between devices: 57.2 us -> 51.2 us  [permutation(): return lambda a: lax.ppermute(a, AXES, pairs)]
    unnamed x15 -> x22, local copies, waits for them, and re-layouts: 10.9 us -> 5.2 us
    dot_general x1, matrix products: 2.36 us -> 0.65 us  [attend(): jnp.einsum('rhk,rlk->rhl', query_lat, kv_cache, preferred_element_type=jn...]
    pallas_call x2 -> x3, Pallas kernels: 21 us -> 19.3 us  [the longest x2 17.4 us: expert_group(): pl.pallas_call(functools.partial(expert_kernel, sizes, outs, n_experts, s...]
    ppermute x38 -> x30, starting transfers between devices: 30.2 us -> 30.1 us  [permutation(): return lambda a: lax.ppermute(a, AXES, pairs)]
  transfers between devices with their start and end apart: 38 -> 30, of which waited for: 14 -> 16; matrix products, arithmetic and copies ran while one was open for 7% -> 10% of each run, Pallas kernels for 16% -> 15%
where the time goes in v3:
time: 118 us
  waiting for transfers between devices  51.2 us (43%)
  starting transfers between devices  30.1 us (26%)
  Pallas kernels  19.3 us (16%)
  other arithmetic  6.08 us (5%)
  local copies, waits for them, and re-layouts  5.3 us (4%)
  matrix products  5.19 us (4%)
    ppermute x30, waiting for transfers between devices, permutation(): return lambda a: lax.ppermute(a, AXES, pairs)  51.2 us
    ppermute x30, starting transfers between devices, permutation(): return lambda a: lax.ppermute(a, AXES, pairs)  30.1 us
    pallas_call x2, Pallas kernels, expert_group(): pl.pallas_call(functools.partial(expert_kernel, sizes, outs, n_experts, s...  17.4 us
    unnamed x22, local copies, waits for them, and re-layouts  5.2 us
    dot_general x1, matrix products, attend(): jnp.einsum('rhl,rlc->rhc', weights, kv_cache[:, :, :LAT], preferred_eleme...  4.54 us
    convert_element_type x12, other arithmetic, plus(): return total.astype(jnp.bfloat16)  3.86 us
  transfers between devices with their start and end apart: 30, of which 16 were waited for; matrix products, arithmetic and copies ran while one was open for 10% of the time, Pallas kernels for 15%

profile of v3, /device:TPU:0, one launch (start us, length us, event | category | flops | bytes accessed | tf_op | source)
XLA Modules:
  0.0 118.0 jit_solution(9667342353951401444)
XLA Ops:
  0.6 1.9 %pack.1 = bf16[16,7296]{1,0:T(8,128)(2,1)} custom-call(s32[8,16]{1,0:T(8,128)} %bitcast.7, f32[8,16]{1,0:T(8,128)} %bitcast.8, bf16[16,7168]{1,0:T(8,128)(2,1)} %x.1), custom_call_target="tpu_custom_call" | custom-call | tf_op jit(solution)/shard_map/pack/pallas_call | solution.py:171
  2.5 2.9 %collective-permute-start = (bf16[16,7296]{1,0:T(8,128)(2,1)}, bf16[16,7296]{1,0:T(8,128)(2,1)}, u32[]{:S(2)}, u32[]{:S(2)}) collective-permute-start(bf16[16,7296]{1,0:T(8,128)(2,1)} %pack.1), channel_id=1, source_target_pairs={{0,2},{1,17},{2,0},{3,19},{4,6},{5,21},{6,4},{7,23},{8,10},{9,25},... | collective-permute-start | bytes 700424 | tf_op jit(solution)/shard_map/ppermute | solution.py:115
  5.5 1.6 %collective-permute-start.2 = (bf16[16,7296]{1,0:T(8,128)(2,1)}, bf16[16,7296]{1,0:T(8,128)(2,1)S(1)}, u32[]{:S(2)}, u32[]{:S(2)}) collective-permute-start(bf16[16,7296]{1,0:T(8,128)(2,1)} %pack.1), channel_id=1, source_target_pairs={{0,4},{1,5},{2,6},{3,7},{4,8},{5,9},{6,10},{7,11},{8,12},{9,13},{1... | collective-permute-start | bytes 700424 | tf_op jit(solution)/shard_map/ppermute | solution.py:115
  10.9 2.1 %collective-permute-start.1 = (bf16[32,7296]{1,0:T(8,128)(2,1)S(1)}, bf16[32,7296]{1,0:T(8,128)(2,1)S(1)}, u32[]{:S(2)}, u32[]{:S(2)}) collective-permute-start(bf16[32,7296]{1,0:T(8,128)(2,1)S(1)} %pad_maximum_fusion), channel_id=1, source_target_pairs={{0,16},{1,3},{2,18},{3,1},{4,20},{5,7},{6,22},{7,5},{8,24},{9,11},... | collective-permute-start | bytes 1400840 | tf_op jit(solution)/shard_map/ppermute | solution.py:115
  13.0 1.7 %collective-permute-done.2 = bf16[16,7296]{1,0:T(8,128)(2,1)S(1)} collective-permute-done((bf16[16,7296]{1,0:T(8,128)(2,1)}, bf16[16,7296]{1,0:T(8,128)(2,1)S(1)}, u32[]{:S(2)}, u32[]{:S(2)}) %collective-permute-start.2) | collective-permute-done | bytes 233504 | tf_op jit(solution)/shard_map/ppermute | solution.py:115
  14.8 1.5 %collective-permute-start.3 = (bf16[16,7296]{1,0:T(8,128)(2,1)S(1)}, bf16[16,7296]{1,0:T(8,128)(2,1)S(1)}, u32[]{:S(2)}, u32[]{:S(2)}) collective-permute-start(bf16[16,7296]{1,0:T(8,128)(2,1)S(1)} %collective-permute-done.2), channel_id=1, source_target_pairs={{0,2},{1,17},{2,0},{3,19},{4,6},{5,21},{6,4},{7,23},{8,10},{9,25},... | collective-permute-start | bytes 700424 | tf_op jit(solution)/shard_map/ppermute | solution.py:115
  17.2 3.6 %collective-permute-done.3 = bf16[16,7296]{1,0:T(8,128)(2,1)S(1)} collective-permute-done((bf16[16,7296]{1,0:T(8,128)(2,1)S(1)}, bf16[16,7296]{1,0:T(8,128)(2,1)S(1)}, u32[]{:S(2)}, u32[]{:S(2)}) %collective-permute-start.3) | collective-permute-done | bytes 233504 | tf_op jit(solution)/shard_map/ppermute | solution.py:115
  20.9 1.4 %collective-permute-start.4 = (bf16[32,7296]{1,0:T(8,128)(2,1)S(1)}, bf16[32,7296]{1,0:T(8,128)(2,1)S(1)}, u32[]{:S(2)}, u32[]{:S(2)}) collective-permute-start(bf16[32,7296]{1,0:T(8,128)(2,1)S(1)} %pad_maximum_fusion.1), channel_id=1, source_target_pairs={{0,16},{1,3},{2,18},{3,1},{4,20},{5,7},{6,22},{7,5},{8,24},{9,11},... | collective-permute-start | bytes 1400840 | tf_op jit(solution)/shard_map/ppermute | solution.py:115
  22.2 1.9 %collective-permute-done.9 = bf16[16,7296]{1,0:T(8,128)(2,1)S(1)} collective-permute-done((bf16[16,7296]{1,0:T(8,128)(2,1)S(1)}, bf16[16,7296]{1,0:T(8,128)(2,1)S(1)}, u32[]{:S(2)}, u32[]{:S(2)}) %collective-permute-start.9) | collective-permute-done | bytes 233504 | tf_op jit(solution)/shard_map/ppermute | solution.py:115
  24.1 1.5 %collective-permute-start.10 = (bf16[16,7296]{1,0:T(8,128)(2,1)S(1)}, bf16[16,7296]{1,0:T(8,128)(2,1)S(1)}, u32[]{:S(2)}, u32[]{:S(2)}) collective-permute-start(bf16[16,7296]{1,0:T(8,128)(2,1)S(1)} %collective-permute-done.9), channel_id=1, source_target_pairs={{0,2},{1,17},{2,0},{3,19},{4,6},{5,21},{6,4},{7,23},{8,10},{9,25},... | collective-permute-start | bytes 700424 | tf_op jit(solution)/shard_map/ppermute | solution.py:115
  25.7 6.8 %collective-permute-done.10 = bf16[16,7296]{1,0:T(8,128)(2,1)S(1)} collective-permute-done((bf16[16,7296]{1,0:T(8,128)(2,1)S(1)}, bf16[16,7296]{1,0:T(8,128)(2,1)S(1)}, u32[]{:S(2)}, u32[]{:S(2)}) %collective-permute-start.10) | collective-permute-done | bytes 233504 | tf_op jit(solution)/shard_map/ppermute | solution.py:115
  33.6 2.8 %collective-permute-start.13 = (bf16[16,7296]{1,0:T(8,128)(2,1)S(1)}, bf16[16,7296]{1,0:T(8,128)(2,1)S(1)}, u32[]{:S(2)}, u32[]{:S(2)}) collective-permute-start(bf16[16,7296]{1,0:T(8,128)(2,1)S(1)} %collective-permute-done.12), channel_id=1, source_target_pairs={{0,2},{1,17},{2,0},{3,19},{4,6},{5,21},{6,4},{7,23},{8,10},{9,25},... | collective-permute-start | bytes 700424 | tf_op jit(solution)/shard_map/ppermute | solution.py:115
  36.6 5.1 %collective-permute-done.13 = bf16[16,7296]{1,0:T(8,128)(2,1)S(1)} collective-permute-done((bf16[16,7296]{1,0:T(8,128)(2,1)S(1)}, bf16[16,7296]{1,0:T(8,128)(2,1)S(1)}, u32[]{:S(2)}, u32[]{:S(2)}) %collective-permute-start.13) | collective-permute-done | bytes 233504 | tf_op jit(solution)/shard_map/ppermute | solution.py:115
  41.8 1.6 %collective-permute-start.14 = (bf16[32,7296]{1,0:T(8,128)(2,1)S(1)}, bf16[32,7296]{1,0:T(8,128)(2,1)S(1)}, u32[]{:S(2)}, u32[]{:S(2)}) collective-permute-start(bf16[32,7296]{1,0:T(8,128)(2,1)S(1)} %constant_dynamic-update-slice_fusion.9.refs_1_), channel_id=1, source_target_pairs={{0,16},{1,3},{2,18},{3,1},{4,20},{5,7},{6,22},{7,5},{8,24},{9,11},... | collective-permute-start | bytes 1400840 | tf_op jit(solution)/shard_map/ppermute | solution.py:115
  44.1 6.4 %collective-permute-done.14.refs_2_ = bf16[32,7296]{1,0:T(8,128)(2,1)S(1)} collective-permute-done((bf16[32,7296]{1,0:T(8,128)(2,1)S(1)}, bf16[32,7296]{1,0:T(8,128)(2,1)S(1)}, u32[]{:S(2)}, u32[]{:S(2)}) %collective-permute-start.14) | collective-permute-done | bytes 466976 | tf_op jit(solution)/shard_map/ppermute | solution.py:115
  50.5 3.1 %copy-done.2 = bf16[1,7168,512]{2,1,0:T(8,128)(2,1)S(1)} copy-done((bf16[1,7168,512]{2,1,0:T(8,128)(2,1)S(1)}, bf16[1,7168,512]{2,1,0:T(8,128)(2,1)}, u32[]{:S(2)}) %copy-start.2) | copy-done | bytes 7340056
  53.6 8.7 %experts.2 = (bf16[32,7168]{1,0:T(8,128)(2,1)S(1)}, bf16[32,7168]{1,0:T(8,128)(2,1)S(1)}, bf16[32,7168]{1,0:T(8,128)(2,1)S(1)}, bf16[32,7168]{1,0:T(8,128)(2,1)S...) custom-call(s32[1]{0:T(128)} %bitcast.me, bf16[1,7168,512]{2,1,0:T(8,128)(2,1)S(1)} %copy-done.1, ...), custom_call_target="tpu_custom_call" | custom-call | flops 5637144576 | bytes 1 | tf_op jit(solution)/shard_map/experts/pallas_call | solution.py:235
  63.9 8.7 %experts.3 = (bf16[32,7168]{1,0:T(8,128)(2,1)S(1)}, bf16[32,7168]{1,0:T(8,128)(2,1)S(1)}, bf16[32,7168]{1,0:T(8,128)(2,1)S(1)}, bf16[32,7168]{1,0:T(8,128)(2,1)S...) custom-call(s32[1]{0:T(128)} %bitcast.me, bf16[1,7168,512]{2,1,0:T(8,128)(2,1)S(1)} %copy-done.1, ...), custom_call_target="tpu_custom_call" | custom-call | flops 5637144576 | bytes 1 | tf_op jit(solution)/shard_map/experts/pallas_call | solution.py:235
  73.3 1.6 %collective-permute-start.25 = (bf16[32,7168]{1,0:T(8,128)(2,1)S(1)}, bf16[32,7168]{1,0:T(8,128)(2,1)S(1)}, u32[]{:S(2)}, u32[]{:S(2)}) collective-permute-start(bf16[32,7168]{1,0:T(8,128)(2,1)S(1)} %add_convert_fusion), channel_id=1, source_target_pairs={{0,16},{1,3},{2,18},{3,1},{4,20},{5,7},{6,22},{7,5},{8,24},{9,11},... | collective-permute-start | bytes 1376264 | tf_op jit(solution)/shard_map/ppermute | solution.py:115
  75.2 1.6 %collective-permute-start.22 = (bf16[32,7168]{1,0:T(8,128)(2,1)S(1)}, bf16[32,7168]{1,0:T(8,128)(2,1)S(1)}, u32[]{:S(2)}, u32[]{:S(2)}) collective-permute-start(bf16[32,7168]{1,0:T(8,128)(2,1)S(1)} %add_convert_fusion.1), channel_id=1, source_target_pairs={{0,16},{1,3},{2,18},{3,1},{4,20},{5,7},{6,22},{7,5},{8,24},{9,11},... | collective-permute-start | bytes 1376264 | tf_op jit(solution)/shard_map/ppermute | solution.py:115
  79.5 2.4 %collective-permute-done.25 = bf16[32,7168]{1,0:T(8,128)(2,1)S(1)} collective-permute-done((bf16[32,7168]{1,0:T(8,128)(2,1)S(1)}, bf16[32,7168]{1,0:T(8,128)(2,1)S(1)}, u32[]{:S(2)}, u32[]{:S(2)}) %collective-permute-start.25) | collective-permute-done | bytes 458784 | tf_op jit(solution)/shard_map/ppermute | solution.py:115
  82.0 1.7 %collective-permute-start.26 = (bf16[16,7168]{1,0:T(8,128)(2,1)S(1)}, bf16[16,7168]{1,0:T(8,128)(2,1)S(1)}, u32[]{:S(2)}, u32[]{:S(2)}) collective-permute-start(bf16[16,7168]{1,0:T(8,128)(2,1)S(1)} %add_convert_fusion.8), channel_id=1, source_target_pairs={{0,2},{1,17},{2,0},{3,19},{4,6},{5,21},{6,4},{7,23},{8,10},{9,25},... | collective-permute-start | bytes 688136 | tf_op jit(solution)/shard_map/ppermute | solution.py:115
  83.6 5.6 %collective-permute-done.22 = bf16[32,7168]{1,0:T(8,128)(2,1)S(1)} collective-permute-done((bf16[32,7168]{1,0:T(8,128)(2,1)S(1)}, bf16[32,7168]{1,0:T(8,128)(2,1)S(1)}, u32[]{:S(2)}, u32[]{:S(2)}) %collective-permute-start.22) | collective-permute-done | bytes 458784 | tf_op jit(solution)/shard_map/ppermute | solution.py:115
  89.3 1.7 %collective-permute-start.23 = (bf16[16,7168]{1,0:T(8,128)(2,1)S(1)}, bf16[16,7168]{1,0:T(8,128)(2,1)S(1)}, u32[]{:S(2)}, u32[]{:S(2)}) collective-permute-start(bf16[16,7168]{1,0:T(8,128)(2,1)S(1)} %add_convert_fusion.9), channel_id=1, source_target_pairs={{0,2},{1,17},{2,0},{3,19},{4,6},{5,21},{6,4},{7,23},{8,10},{9,25},... | collective-permute-start | bytes 688136 | tf_op jit(solution)/shard_map/ppermute | solution.py:115
  91.2 5.4 %collective-permute-done.19 = bf16[32,7168]{1,0:T(8,128)(2,1)S(1)} collective-permute-done((bf16[32,7168]{1,0:T(8,128)(2,1)S(1)}, bf16[32,7168]{1,0:T(8,128)(2,1)S(1)}, u32[]{:S(2)}, u32[]{:S(2)}) %collective-permute-start.19) | collective-permute-done | bytes 458784 | tf_op jit(solution)/shard_map/ppermute | solution.py:115
  96.7 1.7 %collective-permute-start.20 = (bf16[16,7168]{1,0:T(8,128)(2,1)S(1)}, bf16[16,7168]{1,0:T(8,128)(2,1)S(1)}, u32[]{:S(2)}, u32[]{:S(2)}) collective-permute-start(bf16[16,7168]{1,0:T(8,128)(2,1)S(1)} %add_convert_fusion.10), channel_id=1, source_target_pairs={{0,2},{1,17},{2,0},{3,19},{4,6},{5,21},{6,4},{7,23},{8,10},{9,25},... | collective-permute-start | bytes 688136 | tf_op jit(solution)/shard_map/ppermute | solution.py:115
  99.2 4.8 %collective-permute-done.7 = bf16[32,7168]{1,0:T(8,128)(2,1)S(1)} collective-permute-done((bf16[32,7168]{1,0:T(8,128)(2,1)S(1)}, bf16[32,7168]{1,0:T(8,128)(2,1)S(1)}, u32[]{:S(2)}, u32[]{:S(2)}) %collective-permute-start.7) | collective-permute-done | bytes 458784 | tf_op jit(solution)/shard_map/ppermute | solution.py:115
  104.1 1.7 %collective-permute-start.8 = (bf16[16,7168]{1,0:T(8,128)(2,1)S(1)}, bf16[16,7168]{1,0:T(8,128)(2,1)}, u32[]{:S(2)}, u32[]{:S(2)}) collective-permute-start(bf16[16,7168]{1,0:T(8,128)(2,1)S(1)} %add_convert_fusion.11), channel_id=1, source_target_pairs={{0,2},{1,17},{2,0},{3,19},{4,6},{5,21},{6,4},{7,23},{8,10},{9,25},... | collective-permute-start | bytes 688136 | tf_op jit(solution)/shard_map/ppermute | solution.py:115
  105.8 1.3 %collective-permute-done.28 = bf16[16,7168]{1,0:T(8,128)(2,1)S(1)} collective-permute-done((bf16[16,7168]{1,0:T(8,128)(2,1)S(1)}, bf16[16,7168]{1,0:T(8,128)(2,1)S(1)}, u32[]{:S(2)}, u32[]{:S(2)}) %collective-permute-start.28) | collective-permute-done | bytes 229408 | tf_op jit(solution)/shard_map/ppermute | solution.py:115
  107.9 4.5 %fusion.3 = bf16[16,64,512]{2,1,0:T(8,128)(2,1)} fusion(bf16[16,128,576]{1,2,0:T(8,128)(2,1)} %param.13, f32[16,64]{1,0:T(8,128)S(1)} %fusion.11, f32[16,64,128]{2,1,0:T(8,128)S(1)} %fusion.8), kind=kOutput, calls=%fused_computation.3 | convolution fusion | flops 135136384 | bytes 4202496 | tf_op jit(solution)/shard_map/rhl,rlc->rhc/dot_general | solution.py:30
  112.4 3.6 %collective-permute-done.29 = bf16[16,7168]{1,0:T(8,128)(2,1)} collective-permute-done((bf16[16,7168]{1,0:T(8,128)(2,1)}, bf16[16,7168]{1,0:T(8,128)(2,1)}, u32[]{:S(2)}, u32[]{:S(2)}) %collective-permute-start.29) | collective-permute-done | bytes 229408 | tf_op jit(solution)/shard_map/ppermute | solution.py:115
  116.0 2.0 %add_convert_fusion.4 = bf16[16,7168]{1,0:T(8,128)(2,1)} fusion(bf16[16,7168]{1,0:T(8,128)(2,1)} %collective-permute-done.29, bf16[16,7168]{1,0:T(8,128)(2,1)} %collective-permute-done.8, bf16[32,7168]{1,0:T(8,128)(2,1)} %copy-done.6, bf16[64,7168]{1,0:T(8,128)(2,1)S(1)} %collective-permute-done.6, bf16[32,7168]{1,0:T(8,128)(2,1)S(1)} %copy-done.4), kind=kLoop, calls=%fused_computation.16 | loop fusion | flops 1146880 | bytes 1376256 | tf_op jit(solution)/shard_map/convert_element_type | solution.py:136
  (75 shorter events, 14.3 us)
Async XLA Ops:
  0.6 62.2 %copy-start = (bf16[16,64,576]{2,1,0:T(8,128)(2,1)S(1)}, bf16[16,64,576]{2,1,0:T(8,128)(2,1)}, u32[]{:S(2)}) copy-start(bf16[16,64,576]{2,1,0:T(8,128)(2,1)} %param.12) | copy-start | bytes 3538948
  2.5 7.3 %collective-permute-start = (bf16[16,7296]{1,0:T(8,128)(2,1)}, bf16[16,7296]{1,0:T(8,128)(2,1)}, u32[]{:S(2)}, u32[]{:S(2)}) collective-permute-start(bf16[16,7296]{1,0:T(8,128)(2,1)} %pack.1), channel_id=1, source_target_pairs={{0,2},{1,17},{2,0},{3,19},{4,6},{5,21},{6,4},{7,23},{8,10},{9,25},... | collective-permute-start | bytes 700424 | tf_op jit(solution)/shard_map/ppermute | solution.py:115
  5.5 9.3 %collective-permute-start.2 = (bf16[16,7296]{1,0:T(8,128)(2,1)}, bf16[16,7296]{1,0:T(8,128)(2,1)S(1)}, u32[]{:S(2)}, u32[]{:S(2)}) collective-permute-start(bf16[16,7296]{1,0:T(8,128)(2,1)} %pack.1), channel_id=1, source_target_pairs={{0,4},{1,5},{2,6},{3,7},{4,8},{5,9},{6,10},{7,11},{8,12},{9,13},{1... | collective-permute-start | bytes 700424 | tf_op jit(solution)/shard_map/ppermute | solution.py:115
  10.9 25.4 %collective-permute-start.1 = (bf16[32,7296]{1,0:T(8,128)(2,1)S(1)}, bf16[32,7296]{1,0:T(8,128)(2,1)S(1)}, u32[]{:S(2)}, u32[]{:S(2)}) collective-permute-start(bf16[32,7296]{1,0:T(8,128)(2,1)S(1)} %pad_maximum_fusion), channel_id=1, source_target_pairs={{0,16},{1,3},{2,18},{3,1},{4,20},{5,7},{6,22},{7,5},{8,24},{9,11},... | collective-permute-start | bytes 1400840 | tf_op jit(solution)/shard_map/ppermute | solution.py:115
  14.8 6.1 %collective-permute-start.3 = (bf16[16,7296]{1,0:T(8,128)(2,1)S(1)}, bf16[16,7296]{1,0:T(8,128)(2,1)S(1)}, u32[]{:S(2)}, u32[]{:S(2)}) collective-permute-start(bf16[16,7296]{1,0:T(8,128)(2,1)S(1)} %collective-permute-done.2), channel_id=1, source_target_pairs={{0,2},{1,17},{2,0},{3,19},{4,6},{5,21},{6,4},{7,23},{8,10},{9,25},... | collective-permute-start | bytes 700424 | tf_op jit(solution)/shard_map/ppermute | solution.py:115
  16.3 7.9 %collective-permute-start.9 = (bf16[16,7296]{1,0:T(8,128)(2,1)S(1)}, bf16[16,7296]{1,0:T(8,128)(2,1)S(1)}, u32[]{:S(2)}, u32[]{:S(2)}) collective-permute-start(bf16[16,7296]{1,0:T(8,128)(2,1)S(1)} %collective-permute-done.2), channel_id=1, source_target_pairs={{0,4},{1,5},{2,6},{3,7},{4,8},{5,9},{6,10},{7,11},{8,12},{9,13},{1... | collective-permute-start | bytes 700424 | tf_op jit(solution)/shard_map/ppermute | solution.py:115
  20.9 15.6 %collective-permute-start.4 = (bf16[32,7296]{1,0:T(8,128)(2,1)S(1)}, bf16[32,7296]{1,0:T(8,128)(2,1)S(1)}, u32[]{:S(2)}, u32[]{:S(2)}) collective-permute-start(bf16[32,7296]{1,0:T(8,128)(2,1)S(1)} %pad_maximum_fusion.1), channel_id=1, source_target_pairs={{0,16},{1,3},{2,18},{3,1},{4,20},{5,7},{6,22},{7,5},{8,24},{9,11},... | collective-permute-start | bytes 1400840 | tf_op jit(solution)/shard_map/ppermute | solution.py:115
  24.1 8.3 %collective-permute-start.10 = (bf16[16,7296]{1,0:T(8,128)(2,1)S(1)}, bf16[16,7296]{1,0:T(8,128)(2,1)S(1)}, u32[]{:S(2)}, u32[]{:S(2)}) collective-permute-start(bf16[16,7296]{1,0:T(8,128)(2,1)S(1)} %collective-permute-done.9), channel_id=1, source_target_pairs={{0,2},{1,17},{2,0},{3,19},{4,6},{5,21},{6,4},{7,23},{8,10},{9,25},... | collective-permute-start | bytes 700424 | tf_op jit(solution)/shard_map/ppermute | solution.py:115
  25.6 7.9 %collective-permute-start.12 = (bf16[16,7296]{1,0:T(8,128)(2,1)S(1)}, bf16[16,7296]{1,0:T(8,128)(2,1)S(1)}, u32[]{:S(2)}, u32[]{:S(2)}) collective-permute-start(bf16[16,7296]{1,0:T(8,128)(2,1)S(1)} %collective-permute-done.9), channel_id=1, source_target_pairs={{0,4},{1,5},{2,6},{3,7},{4,8},{5,9},{6,10},{7,11},{8,12},{9,13},{1... | collective-permute-start | bytes 700424 | tf_op jit(solution)/shard_map/ppermute | solution.py:115
  32.5 11.3 %collective-permute-start.11 = (bf16[32,7296]{1,0:T(8,128)(2,1)S(1)}, bf16[32,7296]{1,0:T(8,128)(2,1)S(1)}, u32[]{:S(2)}, u32[]{:S(2)}) collective-permute-start(bf16[32,7296]{1,0:T(8,128)(2,1)S(1)} %pad_maximum_fusion.2), channel_id=1, source_target_pairs={{0,16},{1,3},{2,18},{3,1},{4,20},{5,7},{6,22},{7,5},{8,24},{9,11},... | collective-permute-start | bytes 1400840 | tf_op jit(solution)/shard_map/ppermute | solution.py:115
  33.6 8.2 %collective-permute-start.13 = (bf16[16,7296]{1,0:T(8,128)(2,1)S(1)}, bf16[16,7296]{1,0:T(8,128)(2,1)S(1)}, u32[]{:S(2)}, u32[]{:S(2)}) collective-permute-start(bf16[16,7296]{1,0:T(8,128)(2,1)S(1)} %collective-permute-done.12), channel_id=1, source_target_pairs={{0,2},{1,17},{2,0},{3,19},{4,6},{5,21},{6,4},{7,23},{8,10},{9,25},... | collective-permute-start | bytes 700424 | tf_op jit(solution)/shard_map/ppermute | solution.py:115
  36.5 13.9 %collective-permute-start.5 = (bf16[128,7296]{1,0:T(8,128)(2,1)S(1)}, bf16[128,7296]{1,0:T(8,128)(2,1)S(1)}, u32[]{:S(2)}, u32[]{:S(2)}) collective-permute-start(bf16[128,7296]{1,0:T(8,128)(2,1)S(1)} %constant_dynamic-update-slice_fusion.refs_0_), channel_id=1, source_target_pairs={{0,1},{1,0},{2,3},{3,2},{4,5},{5,4},{6,7},{7,6},{8,9},{9,8},{10,11... | collective-permute-start | bytes 5603336 | tf_op jit(solution)/shard_map/ppermute | solution.py:115
  41.8 8.6 %collective-permute-start.14 = (bf16[32,7296]{1,0:T(8,128)(2,1)S(1)}, bf16[32,7296]{1,0:T(8,128)(2,1)S(1)}, u32[]{:S(2)}, u32[]{:S(2)}) collective-permute-start(bf16[32,7296]{1,0:T(8,128)(2,1)S(1)} %constant_dynamic-update-slice_fusion.9.refs_1_), channel_id=1, source_target_pairs={{0,16},{1,3},{2,18},{3,1},{4,20},{5,7},{6,22},{7,5},{8,24},{9,11},... | collective-permute-start | bytes 1400840 | tf_op jit(solution)/shard_map/ppermute | solution.py:115
  43.5 20.4 %collective-permute-start.16 = (bf16[32,7296]{1,0:T(8,128)(2,1)S(1)}, bf16[32,7296]{1,0:T(8,128)(2,1)S(1)}, u32[]{:S(2)}, u32[]{:S(2)}) collective-permute-start(bf16[32,7296]{1,0:T(8,128)(2,1)S(1)} %constant_dynamic-update-slice_fusion.9.refs_1_), channel_id=1, source_target_pairs={{0,1},{1,0},{2,3},{3,2},{4,5},{5,4},{6,7},{7,6},{8,9},{9,8},{10,11... | collective-permute-start | bytes 1400840 | tf_op jit(solution)/shard_map/ppermute | solution.py:115
  43.8 20.1 %collective-permute-start.15 = (bf16[64,7296]{1,0:T(8,128)(2,1)S(1)}, bf16[64,7296]{1,0:T(8,128)(2,1)S(1)}, u32[]{:S(2)}, u32[]{:S(2)}) collective-permute-start(bf16[64,7296]{1,0:T(8,128)(2,1)S(1)} %constant_dynamic-update-slice_fusion.6.refs_0_), channel_id=1, source_target_pairs={{0,1},{1,0},{2,3},{3,2},{4,5},{5,4},{6,7},{7,6},{8,9},{9,8},{10,11... | collective-permute-start | bytes 2801672 | tf_op jit(solution)/shard_map/ppermute | solution.py:115
  50.5 13.4 %collective-permute-start.17 = (bf16[32,7296]{1,0:T(8,128)(2,1)S(1)}, bf16[32,7296]{1,0:T(8,128)(2,1)S(1)}, u32[]{:S(2)}, u32[]{:S(2)}) collective-permute-start(bf16[32,7296]{1,0:T(8,128)(2,1)S(1)} %collective-permute-done.14.refs_2_), channel_id=1, source_target_pairs={{0,1},{1,0},{2,3},{3,2},{4,5},{5,4},{6,7},{7,6},{8,9},{9,8},{10,11... | collective-permute-start | bytes 1400840 | tf_op jit(solution)/shard_map/ppermute | solution.py:115
  62.2 41.7 %copy-start.3 = (bf16[32,7168]{1,0:T(8,128)(2,1)}, bf16[32,7168]{1,0:T(8,128)(2,1)S(1)}, u32[]{:S(2)}) copy-start(bf16[32,7168]{1,0:T(8,128)(2,1)S(1)} %get-tuple-element.14.refs_6_) | copy-start | bytes 1376260
  62.2 11.0 %collective-permute-start.24 = (bf16[64,7168]{1,0:T(8,128)(2,1)S(1)}, bf16[64,7168]{1,0:T(8,128)(2,1)S(1)}, u32[]{:S(2)}, u32[]{:S(2)}) collective-permute-start(bf16[64,7168]{1,0:T(8,128)(2,1)S(1)} %get-tuple-element.24), channel_id=1, source_target_pairs={{0,1},{1,0},{2,3},{3,2},{4,5},{5,4},{6,7},{7,6},{8,9},{9,8},{10,11... | collective-permute-start | bytes 2752520 | tf_op jit(solution)/shard_map/ppermute | solution.py:115
  72.6 2.5 %collective-permute-start.21 = (bf16[64,7168]{1,0:T(8,128)(2,1)S(1)}, bf16[64,7168]{1,0:T(8,128)(2,1)S(1)}, u32[]{:S(2)}, u32[]{:S(2)}) collective-permute-start(bf16[64,7168]{1,0:T(8,128)(2,1)S(1)} %get-tuple-element.21), channel_id=1, source_target_pairs={{0,1},{1,0},{2,3},{3,2},{4,5},{5,4},{6,7},{7,6},{8,9},{9,8},{10,11... | collective-permute-start | bytes 2752520 | tf_op jit(solution)/shard_map/ppermute | solution.py:115
  72.6 4.2 %collective-permute-start.18 = (bf16[64,7168]{1,0:T(8,128)(2,1)S(1)}, bf16[64,7168]{1,0:T(8,128)(2,1)S(1)}, u32[]{:S(2)}, u32[]{:S(2)}) collective-permute-start(bf16[64,7168]{1,0:T(8,128)(2,1)S(1)} %get-tuple-element.18), channel_id=1, source_target_pairs={{0,1},{1,0},{2,3},{3,2},{4,5},{5,4},{6,7},{7,6},{8,9},{9,8},{10,11... | collective-permute-start | bytes 2752520 | tf_op jit(solution)/shard_map/ppermute | solution.py:115
  73.1 5.0 %collective-permute-start.6 = (bf16[64,7168]{1,0:T(8,128)(2,1)S(1)}, bf16[64,7168]{1,0:T(8,128)(2,1)S(1)}, u32[]{:S(2)}, u32[]{:S(2)}) collective-permute-start(bf16[64,7168]{1,0:T(8,128)(2,1)S(1)} %get-tuple-element.15), channel_id=1, source_target_pairs={{0,1},{1,0},{2,3},{3,2},{4,5},{5,4},{6,7},{7,6},{8,9},{9,8},{10,11... | collective-permute-start | bytes 2752520 | tf_op jit(solution)/shard_map/ppermute | solution.py:115
  73.3 8.5 %collective-permute-start.25 = (bf16[32,7168]{1,0:T(8,128)(2,1)S(1)}, bf16[32,7168]{1,0:T(8,128)(2,1)S(1)}, u32[]{:S(2)}, u32[]{:S(2)}) collective-permute-start(bf16[32,7168]{1,0:T(8,128)(2,1)S(1)} %add_convert_fusion), channel_id=1, source_target_pairs={{0,16},{1,3},{2,18},{3,1},{4,20},{5,7},{6,22},{7,5},{8,24},{9,11},... | collective-permute-start | bytes 1376264 | tf_op jit(solution)/shard_map/ppermute | solution.py:115
  75.2 14.0 %collective-permute-start.22 = (bf16[32,7168]{1,0:T(8,128)(2,1)S(1)}, bf16[32,7168]{1,0:T(8,128)(2,1)S(1)}, u32[]{:S(2)}, u32[]{:S(2)}) collective-permute-start(bf16[32,7168]{1,0:T(8,128)(2,1)S(1)} %add_convert_fusion.1), channel_id=1, source_target_pairs={{0,16},{1,3},{2,18},{3,1},{4,20},{5,7},{6,22},{7,5},{8,24},{9,11},... | collective-permute-start | bytes 1376264 | tf_op jit(solution)/shard_map/ppermute | solution.py:115
  77.0 19.7 %collective-permute-start.19 = (bf16[32,7168]{1,0:T(8,128)(2,1)S(1)}, bf16[32,7168]{1,0:T(8,128)(2,1)S(1)}, u32[]{:S(2)}, u32[]{:S(2)}) collective-permute-start(bf16[32,7168]{1,0:T(8,128)(2,1)S(1)} %add_convert_fusion.2), channel_id=1, source_target_pairs={{0,16},{1,3},{2,18},{3,1},{4,20},{5,7},{6,22},{7,5},{8,24},{9,11},... | collective-permute-start | bytes 1376264 | tf_op jit(solution)/shard_map/ppermute | solution.py:115
  78.3 25.7 %collective-permute-start.7 = (bf16[32,7168]{1,0:T(8,128)(2,1)S(1)}, bf16[32,7168]{1,0:T(8,128)(2,1)S(1)}, u32[]{:S(2)}, u32[]{:S(2)}) collective-permute-start(bf16[32,7168]{1,0:T(8,128)(2,1)S(1)} %add_convert_fusion.3), channel_id=1, source_target_pairs={{0,16},{1,3},{2,18},{3,1},{4,20},{5,7},{6,22},{7,5},{8,24},{9,11},... | collective-permute-start | bytes 1376264 | tf_op jit(solution)/shard_map/ppermute | solution.py:115
  82.0 9.0 %collective-permute-start.26 = (bf16[16,7168]{1,0:T(8,128)(2,1)S(1)}, bf16[16,7168]{1,0:T(8,128)(2,1)S(1)}, u32[]{:S(2)}, u32[]{:S(2)}) collective-permute-start(bf16[16,7168]{1,0:T(8,128)(2,1)S(1)} %add_convert_fusion.8), channel_id=1, source_target_pairs={{0,2},{1,17},{2,0},{3,19},{4,6},{5,21},{6,4},{7,23},{8,10},{9,25},... | collective-permute-start | bytes 688136 | tf_op jit(solution)/shard_map/ppermute | solution.py:115
  89.3 9.0 %collective-permute-start.23 = (bf16[16,7168]{1,0:T(8,128)(2,1)S(1)}, bf16[16,7168]{1,0:T(8,128)(2,1)S(1)}, u32[]{:S(2)}, u32[]{:S(2)}) collective-permute-start(bf16[16,7168]{1,0:T(8,128)(2,1)S(1)} %add_convert_fusion.9), channel_id=1, source_target_pairs={{0,2},{1,17},{2,0},{3,19},{4,6},{5,21},{6,4},{7,23},{8,10},{9,25},... | collective-permute-start | bytes 688136 | tf_op jit(solution)/shard_map/ppermute | solution.py:115
  91.1 7.9 %collective-permute-start.27 = (bf16[16,7168]{1,0:T(8,128)(2,1)S(1)}, bf16[16,7168]{1,0:T(8,128)(2,1)S(1)}, u32[]{:S(2)}, u32[]{:S(2)}) collective-permute-start(bf16[16,7168]{1,0:T(8,128)(2,1)S(1)} %add_convert_fusion.7), channel_id=1, source_target_pairs={{0,4},{1,5},{2,6},{3,7},{4,8},{5,9},{6,10},{7,11},{8,12},{9,13},{1... | collective-permute-start | bytes 688136 | tf_op jit(solution)/shard_map/ppermute | solution.py:115
  96.7 9.1 %collective-permute-start.20 = (bf16[16,7168]{1,0:T(8,128)(2,1)S(1)}, bf16[16,7168]{1,0:T(8,128)(2,1)S(1)}, u32[]{:S(2)}, u32[]{:S(2)}) collective-permute-start(bf16[16,7168]{1,0:T(8,128)(2,1)S(1)} %add_convert_fusion.10), channel_id=1, source_target_pairs={{0,2},{1,17},{2,0},{3,19},{4,6},{5,21},{6,4},{7,23},{8,10},{9,25},... | collective-permute-start | bytes 688136 | tf_op jit(solution)/shard_map/ppermute | solution.py:115
  99.1 7.9 %collective-permute-start.28 = (bf16[16,7168]{1,0:T(8,128)(2,1)S(1)}, bf16[16,7168]{1,0:T(8,128)(2,1)S(1)}, u32[]{:S(2)}, u32[]{:S(2)}) collective-permute-start(bf16[16,7168]{1,0:T(8,128)(2,1)S(1)} %add_convert_fusion.6), channel_id=1, source_target_pairs={{0,4},{1,5},{2,6},{3,7},{4,8},{5,9},{6,10},{7,11},{8,12},{9,13},{1... | collective-permute-start | bytes 688136 | tf_op jit(solution)/shard_map/ppermute | solution.py:115
  104.1 8.3 %collective-permute-start.8 = (bf16[16,7168]{1,0:T(8,128)(2,1)S(1)}, bf16[16,7168]{1,0:T(8,128)(2,1)}, u32[]{:S(2)}, u32[]{:S(2)}) collective-permute-start(bf16[16,7168]{1,0:T(8,128)(2,1)S(1)} %add_convert_fusion.11), channel_id=1, source_target_pairs={{0,2},{1,17},{2,0},{3,19},{4,6},{5,21},{6,4},{7,23},{8,10},{9,25},... | collective-permute-start | bytes 688136 | tf_op jit(solution)/shard_map/ppermute | solution.py:115
  107.9 8.1 %collective-permute-start.29 = (bf16[16,7168]{1,0:T(8,128)(2,1)}, bf16[16,7168]{1,0:T(8,128)(2,1)}, u32[]{:S(2)}, u32[]{:S(2)}) collective-permute-start(bf16[16,7168]{1,0:T(8,128)(2,1)} %add_convert_fusion.5), channel_id=1, source_target_pairs={{0,4},{1,5},{2,6},{3,7},{4,8},{5,9},{6,10},{7,11},{8,12},{9,13},{1... | collective-permute-start | bytes 688136 | tf_op jit(solution)/shard_map/ppermute | solution.py:115
  (5 other events, 54.0 us)

commit v4 on v3

--- a/solution.py
+++ b/solution.py
@@ -134,6 +134,10 @@
     for t in terms[1:]:
         total = total + t.astype(jnp.float32)
     return total.astype(jnp.bfloat16)
+
+
+def after(a, other):
+    return a + other[:1, :1] * 0
 
 
 ANYWHERE = pl.BlockSpec(memory_space=pl.ANY)
@@ -249,7 +253,7 @@
             pltpu.SemaphoreType.DMA((steps,)),
         ],
         out_shape=[jax.ShapeDtypeStruct((r, width), jnp.bfloat16) for r in outs],
-        compiler_params=pltpu.CompilerParams(vmem_limit_bytes=28 * 2**20),
+        compiler_params=pltpu.CompilerParams(vmem_limit_bytes=33 * 2**20),
         cost_estimate=pl.CostEstimate(
             flops=6 * m * width * hidden_width,
             bytes_accessed=1,
@@ -274,20 +278,26 @@
     pairs = [a for k in range(n) for a in (near[k], far[k])]
     own = cat(*pairs[: 2 * half])
     early = expert_group([own, mv.core(own)], half, *weights, n_dev)
-    late = []
-    for k in range(half, n - 1):
-        late.append(cat(near[k], far[k]))
-    late += pairs[2 * n - 2 :]
-    late = expert_group(late + [mv.core(a) for a in late], n - half, *weights, n_dev, early[0])
-    y_near = early[0 : 2 * half : 2] + late[0 : 2 * (n - half) : 2]
-    y_far = early[1 : 2 * half : 2] + late[1 : 2 * (n - half) : 2]
-    mine = [mv.core(a) for a in early[2 * half :] + late[2 * (n - half) :]]
     rows = block[0].shape[0]
+    y_near, y_far = early[0 : 2 * half : 2], early[1 : 2 * half : 2]
+    order = list(range(1, n)) + [0]
+    mine, crossed, back = {}, {}, []
+    for k in [k for k in order if k < half]:
+        mine[k] = mv.core(early[2 * half + k])
+        back.append(plus(y_far[k], mine[k][2 * rows :]))
+        crossed[k] = mv.second(back[-1])
+    late = [cat(near[k], far[k]) for k in range(half, n - 1)] + pairs[2 * n - 2 :]
+    theirs = [mv.core(a) for a in late[:-1]] + [mv.core(after(late[-1], early[-1]))]
+    late = expert_group(late + theirs, n - half, *weights, n_dev, *back)
+    y_near, y_far = y_near + late[0 : 2 * (n - half) : 2], y_far + late[1 : 2 * (n - half) : 2]
     acc = ()
-    for k in list(range(1, n)) + [0]:
-        crossed = mv.second(plus(y_far[k], mine[k][2 * rows :]))
-        side = mv.first(plus(y_near[k][rows:], mine[k][rows : 2 * rows], crossed[rows:]))
-        total = plus(y_near[k][:rows], mine[k][:rows], crossed[:rows], side, *acc)
+    for k in order:
+        if k >= half:
+            mine[k] = mv.core(late[2 * (n - half) + k - half])
+            back = plus(y_far[k], mine[k][2 * rows :])
+            crossed[k] = mv.second(after(back, crossed[k - 1]) if k > half else back)
+        side = mv.first(plus(y_near[k][rows:], mine[k][rows : 2 * rows], crossed[k][rows:]))
+        total = plus(y_near[k][:rows], mine[k][:rows], crossed[k][:rows], side, *acc)
         if k:
             acc = (mv.ring(total),)
     return total

time: 118 us -> 110 us (0.932)
  waiting for transfers between devices: 51.2 us -> 37 us
  matrix products: 5.19 us -> 7.97 us
  other arithmetic: 6.08 us -> 8.28 us
  between operations: 0.87 us -> 2.21 us
    ppermute x30, waiting for transfers between devices: 51.2 us -> 37 us  [permutation(): return lambda a: lax.ppermute(a, AXES, pairs)]
    dot_general x1, matrix products: 0.65 us -> 3.15 us  [attend(): jnp.einsum('rhk,rlk->rhl', query_lat, kv_cache, preferred_element_type=jn...]
    unnamed x22 -> x18, local copies, waits for them, and re-layouts: 5.2 us -> 3.06 us
    sub x1, other arithmetic: 0.34 us -> 1.58 us  [attend(): exponent = jnp.exp(scores - top_score)]
    convert_element_type x12 -> x11, other arithmetic: 3.86 us -> 3.64 us  [plus(): return total.astype(jnp.bfloat16)]
  transfers between devices with their start and end apart: 30 -> 30, of which waited for: 16 -> 14; matrix products, arithmetic and copies ran while one was open for 10% -> 17% of each run, Pallas kernels for 15% -> 17%
where the time goes in v4:
time: 110 us; the launch traced here: 109 us
  waiting for transfers between devices  37 us (34%)
  starting transfers between devices  29.3 us (27%)
  Pallas kernels  20.1 us (18%)
  other arithmetic  8.28 us (8%)
  matrix products  7.97 us (7%)
  local copies, waits for them, and re-layouts  4.22 us (4%)
  between operations  2.21 us (2%)
    ppermute x30, waiting for transfers between devices, permutation(): return lambda a: lax.ppermute(a, AXES, pairs)  37 us
    ppermute x30, starting transfers between devices, permutation(): return lambda a: lax.ppermute(a, AXES, pairs)  29.3 us
    pallas_call x2, Pallas kernels, expert_group(): pl.pallas_call(functools.partial(expert_kernel, sizes, outs, n_experts, s...  18.2 us
    dot_general x1, matrix products, attend(): jnp.einsum('rhl,rlc->rhc', weights, kv_cache[:, :, :LAT], preferred_eleme...  4.82 us
    convert_element_type x11, other arithmetic, plus(): return total.astype(jnp.bfloat16)  3.64 us
    dot_general x1, matrix products, attend(): jnp.einsum('rhk,rlk->rhl', query_lat, kv_cache, preferred_element_type=jn...  3.15 us
    unnamed x18, local copies, waits for them, and re-layouts  3.06 us
  transfers between devices with their start and end apart: 30, of which 14 were waited for; matrix products, arithmetic and copies ran while one was open for 17% of the time, Pallas kernels for 17%

profile of v4, /device:TPU:0, one launch (start us, length us, event | category | flops | bytes accessed | tf_op | source)
XLA Modules:
  0.0 109.1 jit_solution(7085762834475819473)
XLA Ops:
  0.6 1.9 %pack.1 = bf16[16,7296]{1,0:T(8,128)(2,1)} custom-call(s32[8,16]{1,0:T(8,128)} %bitcast.9, f32[8,16]{1,0:T(8,128)} %bitcast.10, bf16[16,7168]{1,0:T(8,128)(2,1)} %x.1), custom_call_target="tpu_custom_call" | custom-call | tf_op jit(solution)/shard_map/pack/pallas_call | solution.py:175
  2.5 2.9 %collective-permute-start = (bf16[16,7296]{1,0:T(8,128)(2,1)}, bf16[16,7296]{1,0:T(8,128)(2,1)}, u32[]{:S(2)}, u32[]{:S(2)}) collective-permute-start(bf16[16,7296]{1,0:T(8,128)(2,1)} %pack.1), channel_id=1, source_target_pairs={{0,2},{1,17},{2,0},{3,19},{4,6},{5,21},{6,4},{7,23},{8,10},{9,25},... | collective-permute-start | bytes 700424 | tf_op jit(solution)/shard_map/ppermute | solution.py:115
  5.5 1.6 %collective-permute-start.2 = (bf16[16,7296]{1,0:T(8,128)(2,1)}, bf16[16,7296]{1,0:T(8,128)(2,1)}, u32[]{:S(2)}, u32[]{:S(2)}) collective-permute-start(bf16[16,7296]{1,0:T(8,128)(2,1)} %pack.1), channel_id=1, source_target_pairs={{0,4},{1,5},{2,6},{3,7},{4,8},{5,9},{6,10},{7,11},{8,12},{9,13},{1... | collective-permute-start | bytes 700424 | tf_op jit(solution)/shard_map/ppermute | solution.py:115
  8.8 3.2 %fusion.8 = f32[16,64,128]{2,1,0:T(8,128)} fusion(bf16[16,64,576]{2,1,0:T(8,128)(2,1)S(1)} %copy-done, bf16[16,128,576]{1,2,0:T(8,128)(2,1)} %param.13, pred[16,128]{1,0:T(8,128)(4,1)S(1)} %iota_compare_fusion), kind=kOutput, calls=%fused_computation.7 | convolution fusion | flops 151257088 | bytes 4065280 | tf_op jit(solution)/shard_map/rhk,rlk->rhl/dot_general | solution.py:20
  11.9 1.6 %fusion.12 = f32[16,64]{1,0:T(8,128)S(1)} fusion(f32[16,64,128]{2,1,0:T(8,128)} %fusion.8), kind=kOutput, calls=%fused_computation.40 | output fusion | flops 262271 | bytes 528384 | tf_op jit(solution)/shard_map/sub | solution.py:27
  14.5 1.6 %collective-permute-start.1 = (bf16[32,7296]{1,0:T(8,128)(2,1)S(1)}, bf16[32,7296]{1,0:T(8,128)(2,1)S(1)}, u32[]{:S(2)}, u32[]{:S(2)}) collective-permute-start(bf16[32,7296]{1,0:T(8,128)(2,1)S(1)} %pad_maximum_fusion), channel_id=1, source_target_pairs={{0,16},{1,3},{2,18},{3,1},{4,20},{5,7},{6,22},{7,5},{8,24},{9,11},... | collective-permute-start | bytes 1400840 | tf_op jit(solution)/shard_map/ppermute | solution.py:115
  16.7 1.6 %collective-permute-start.9 = (bf16[16,7296]{1,0:T(8,128)(2,1)}, bf16[16,7296]{1,0:T(8,128)(2,1)S(1)}, u32[]{:S(2)}, u32[]{:S(2)}) collective-permute-start(bf16[16,7296]{1,0:T(8,128)(2,1)} %collective-permute-done.2), channel_id=1, source_target_pairs={{0,4},{1,5},{2,6},{3,7},{4,8},{5,9},{6,10},{7,11},{8,12},{9,13},{1... | collective-permute-start | bytes 700424 | tf_op jit(solution)/shard_map/ppermute | solution.py:115
  19.2 4.8 %collective-permute-done.3 = bf16[16,7296]{1,0:T(8,128)(2,1)S(1)} collective-permute-done((bf16[16,7296]{1,0:T(8,128)(2,1)}, bf16[16,7296]{1,0:T(8,128)(2,1)S(1)}, u32[]{:S(2)}, u32[]{:S(2)}) %collective-permute-start.3) | collective-permute-done | bytes 233504 | tf_op jit(solution)/shard_map/ppermute | solution.py:115
  24.0 1.1 %pad_maximum_fusion.1 = bf16[32,7296]{1,0:T(8,128)(2,1)S(1)} fusion(bf16[16,7296]{1,0:T(8,128)(2,1)S(1)} %collective-permute-done.3, bf16[16,7296]{1,0:T(8,128)(2,1)} %collective-permute-done.2), kind=kLoop, calls=%fused_computation.14 | loop fusion | flops 933888 | bytes 933888 | tf_op jit(solution)/shard_map/concatenate | solution.py:272
  25.7 1.5 %collective-permute-start.10 = (bf16[16,7296]{1,0:T(8,128)(2,1)S(1)}, bf16[16,7296]{1,0:T(8,128)(2,1)S(1)}, u32[]{:S(2)}, u32[]{:S(2)}) collective-permute-start(bf16[16,7296]{1,0:T(8,128)(2,1)S(1)} %collective-permute-done.9), channel_id=1, source_target_pairs={{0,2},{1,17},{2,0},{3,19},{4,6},{5,21},{6,4},{7,23},{8,10},{9,25},... | collective-permute-start | bytes 700424 | tf_op jit(solution)/shard_map/ppermute | solution.py:115
  27.2 1.6 %collective-permute-start.12 = (bf16[16,7296]{1,0:T(8,128)(2,1)S(1)}, bf16[16,7296]{1,0:T(8,128)(2,1)S(1)}, u32[]{:S(2)}, u32[]{:S(2)}) collective-permute-start(bf16[16,7296]{1,0:T(8,128)(2,1)S(1)} %collective-permute-done.9), channel_id=1, source_target_pairs={{0,4},{1,5},{2,6},{3,7},{4,8},{5,9},{6,10},{7,11},{8,12},{9,13},{1... | collective-permute-start | bytes 700424 | tf_op jit(solution)/shard_map/ppermute | solution.py:115
  28.8 5.2 %collective-permute-done.10 = bf16[16,7296]{1,0:T(8,128)(2,1)S(1)} collective-permute-done((bf16[16,7296]{1,0:T(8,128)(2,1)S(1)}, bf16[16,7296]{1,0:T(8,128)(2,1)S(1)}, u32[]{:S(2)}, u32[]{:S(2)}) %collective-permute-start.10) | collective-permute-done | bytes 233504 | tf_op jit(solution)/shard_map/ppermute | solution.py:115
  37.2 6.1 %collective-permute-done.13 = bf16[16,7296]{1,0:T(8,128)(2,1)S(1)} collective-permute-done((bf16[16,7296]{1,0:T(8,128)(2,1)S(1)}, bf16[16,7296]{1,0:T(8,128)(2,1)S(1)}, u32[]{:S(2)}, u32[]{:S(2)}) %collective-permute-start.13) | collective-permute-done | bytes 233504 | tf_op jit(solution)/shard_map/ppermute | solution.py:115
  44.1 9.1 %experts.2 = (bf16[32,7168]{1,0:T(8,128)(2,1)S(1)}, bf16[32,7168]{1,0:T(8,128)(2,1)S(1)}, bf16[32,7168]{1,0:T(8,128)(2,1)S(1)}, bf16[32,7168]{1,0:T(8,128)(2,1)S...) custom-call(s32[1]{0:T(128)} %bitcast.me, bf16[1,7168,512]{2,1,0:T(8,128)(2,1)S(1)} %copy-done.1, ...), custom_call_target="tpu_custom_call" | custom-call | flops 5637144576 | bytes 1 | tf_op jit(solution)/shard_map/experts/pallas_call | solution.py:239
  55.9 2.0 %collective-permute-start.25 = (bf16[32,7168]{1,0:T(8,128)(2,1)S(1)}, bf16[32,7168]{1,0:T(8,128)(2,1)S(1)}, u32[]{:S(2)}, u32[]{:S(2)}) collective-permute-start(bf16[32,7168]{1,0:T(8,128)(2,1)S(1)} %add_convert_fusion.2.refs_6_), channel_id=1, source_target_pairs={{0,16},{1,3},{2,18},{3,1},{4,20},{5,7},{6,22},{7,5},{8,24},{9,11},... | collective-permute-start | bytes 1376264 | tf_op jit(solution)/shard_map/ppermute | solution.py:115
  58.0 2.0 %collective-permute-start.7 = (bf16[32,7168]{1,0:T(8,128)(2,1)S(1)}, bf16[32,7168]{1,0:T(8,128)(2,1)S(1)}, u32[]{:S(2)}, u32[]{:S(2)}) collective-permute-start(bf16[32,7168]{1,0:T(8,128)(2,1)S(1)} %add_convert_fusion.3.refs_7_), channel_id=1, source_target_pairs={{0,16},{1,3},{2,18},{3,1},{4,20},{5,7},{6,22},{7,5},{8,24},{9,11},... | collective-permute-start | bytes 1376264 | tf_op jit(solution)/shard_map/ppermute | solution.py:115
  60.0 9.1 %experts.3 = (bf16[32,7168]{1,0:T(8,128)(2,1)S(1)}, bf16[32,7168]{1,0:T(8,128)(2,1)S(1)}, bf16[32,7168]{1,0:T(8,128)(2,1)S(1)}, bf16[32,7168]{1,0:T(8,128)(2,1)S...) custom-call(s32[1]{0:T(128)} %bitcast.me, bf16[1,7168,512]{2,1,0:T(8,128)(2,1)S(1)} %copy-done.1, ...), custom_call_target="tpu_custom_call" | custom-call | flops 5637144576 | bytes 1 | tf_op jit(solution)/shard_map/experts/pallas_call | solution.py:239
  69.8 1.0 collective-permute-start.26
  72.6 4.6 %collective-permute-done.26 = bf16[16,7168]{1,0:T(8,128)(2,1)S(1)} collective-permute-done((bf16[16,7168]{1,0:T(8,128)(2,1)S(1)}, bf16[16,7168]{1,0:T(8,128)(2,1)S(1)}, u32[]{:S(2)}, u32[]{:S(2)}) %collective-permute-start.26) | collective-permute-done | bytes 229408 | tf_op jit(solution)/shard_map/ppermute | solution.py:115
  77.3 1.6 %collective-permute-start.27 = (bf16[16,7168]{1,0:T(8,128)(2,1)S(1)}, bf16[16,7168]{1,0:T(8,128)(2,1)S(1)}, u32[]{:S(2)}, u32[]{:S(2)}) collective-permute-start(bf16[16,7168]{1,0:T(8,128)(2,1)S(1)} %add_convert_fusion.7), channel_id=1, source_target_pairs={{0,4},{1,5},{2,6},{3,7},{4,8},{5,9},{6,10},{7,11},{8,12},{9,13},{1... | collective-permute-start | bytes 688136 | tf_op jit(solution)/shard_map/ppermute | solution.py:115
  79.0 1.4 %collective-permute-done.21 = bf16[32,7168]{1,0:T(8,128)(2,1)S(1)} collective-permute-done((bf16[32,7168]{1,0:T(8,128)(2,1)S(1)}, bf16[32,7168]{1,0:T(8,128)(2,1)S(1)}, u32[]{:S(2)}, u32[]{:S(2)}) %collective-permute-start.21) | collective-permute-done | bytes 458784 | tf_op jit(solution)/shard_map/ppermute | solution.py:115
  80.4 1.0 collective-permute-start.24
  83.6 1.5 %collective-permute-done.27 = bf16[16,7168]{1,0:T(8,128)(2,1)S(1)} collective-permute-done((bf16[16,7168]{1,0:T(8,128)(2,1)S(1)}, bf16[16,7168]{1,0:T(8,128)(2,1)S(1)}, u32[]{:S(2)}, u32[]{:S(2)}) %collective-permute-start.27) | collective-permute-done | bytes 229408 | tf_op jit(solution)/shard_map/ppermute | solution.py:115
  85.2 2.7 %collective-permute-done.24 = bf16[16,7168]{1,0:T(8,128)(2,1)S(1)} collective-permute-done((bf16[16,7168]{1,0:T(8,128)(2,1)S(1)}, bf16[16,7168]{1,0:T(8,128)(2,1)S(1)}, u32[]{:S(2)}, u32[]{:S(2)}) %collective-permute-start.24) | collective-permute-done | bytes 229408 | tf_op jit(solution)/shard_map/ppermute | solution.py:115
  88.0 1.9 %collective-permute-start.28 = (bf16[16,7168]{1,0:T(8,128)(2,1)S(1)}, bf16[16,7168]{1,0:T(8,128)(2,1)S(1)}, u32[]{:S(2)}, u32[]{:S(2)}) collective-permute-start(bf16[16,7168]{1,0:T(8,128)(2,1)S(1)} %add_convert_fusion.6), channel_id=1, source_target_pairs={{0,4},{1,5},{2,6},{3,7},{4,8},{5,9},{6,10},{7,11},{8,12},{9,13},{1... | collective-permute-start | bytes 688136 | tf_op jit(solution)/shard_map/ppermute | solution.py:115
  90.0 1.4 %collective-permute-done.22 = bf16[32,7168]{1,0:T(8,128)(2,1)S(1)} collective-permute-done((bf16[32,7168]{1,0:T(8,128)(2,1)S(1)}, bf16[32,7168]{1,0:T(8,128)(2,1)S(1)}, u32[]{:S(2)}, u32[]{:S(2)}) %collective-permute-start.22) | collective-permute-done | bytes 458784 | tf_op jit(solution)/shard_map/ppermute | solution.py:115
  91.4 1.1 %collective-permute-start.23 = (bf16[16,7168]{1,0:T(8,128)(2,1)S(1)}, bf16[16,7168]{1,0:T(8,128)(2,1)S(1)}, u32[]{:S(2)}, u32[]{:S(2)}) collective-permute-start(bf16[16,7168]{1,0:T(8,128)(2,1)S(1)} %add_convert_fusion.10), channel_id=1, source_target_pairs={{0,2},{1,17},{2,0},{3,19},{4,6},{5,21},{6,4},{7,23},{8,10},{9,25},... | collective-permute-start | bytes 688136 | tf_op jit(solution)/shard_map/ppermute | solution.py:115
  93.7 2.2 %collective-permute-done.28 = bf16[16,7168]{1,0:T(8,128)(2,1)S(1)} collective-permute-done((bf16[16,7168]{1,0:T(8,128)(2,1)S(1)}, bf16[16,7168]{1,0:T(8,128)(2,1)S(1)}, u32[]{:S(2)}, u32[]{:S(2)}) %collective-permute-start.28) | collective-permute-done | bytes 229408 | tf_op jit(solution)/shard_map/ppermute | solution.py:115
  95.9 1.6 %collective-permute-done.23 = bf16[16,7168]{1,0:T(8,128)(2,1)S(1)} collective-permute-done((bf16[16,7168]{1,0:T(8,128)(2,1)S(1)}, bf16[16,7168]{1,0:T(8,128)(2,1)S(1)}, u32[]{:S(2)}, u32[]{:S(2)}) %collective-permute-start.23) | collective-permute-done | bytes 229408 | tf_op jit(solution)/shard_map/ppermute | solution.py:115
  99.4 4.8 %fusion.3 = bf16[16,64,512]{2,1,0:T(8,128)(2,1)} fusion(bf16[16,128,576]{1,2,0:T(8,128)(2,1)} %param.13, f32[16,64]{1,0:T(8,128)S(1)} %fusion.12, f32[16,64,128]{2,1,0:T(8,128)} %fusion.8), kind=kOutput, calls=%fused_computation.3 | convolution fusion | flops 135136384 | bytes 4198400 | tf_op jit(solution)/shard_map/rhl,rlc->rhc/dot_general | solution.py:30
  104.2 3.0 %collective-permute-done.29 = bf16[16,7168]{1,0:T(8,128)(2,1)} collective-permute-done((bf16[16,7168]{1,0:T(8,128)(2,1)}, bf16[16,7168]{1,0:T(8,128)(2,1)}, u32[]{:S(2)}, u32[]{:S(2)}) %collective-permute-start.29) | collective-permute-done | bytes 229408 | tf_op jit(solution)/shard_map/ppermute | solution.py:115
  107.2 1.9 %add_convert_fusion.4 = bf16[16,7168]{1,0:T(8,128)(2,1)} fusion(bf16[16,7168]{1,0:T(8,128)(2,1)} %collective-permute-done.29, bf16[16,7168]{1,0:T(8,128)(2,1)} %collective-permute-done.8, bf16[32,7168]{1,0:T(8,128)(2,1)S(1)} %collective-permute-done.7, bf16[64,7168]{1,0:T(8,128)(2,1)S(1)} %collective-permute-done.6, bf16[32,7168]{1,0:T(8,128)(2,1)S(1)} %copy-done.3), kind=kLoop, calls=%fused_computation.17 | loop fusion | flops 1146880 | bytes 1376256 | tf_op jit(solution)/shard_map/convert_element_type | solution.py:136
  (74 shorter events, 18.0 us)
Async XLA Ops:
  2.5 11.0 %collective-permute-start = (bf16[16,7296]{1,0:T(8,128)(2,1)}, bf16[16,7296]{1,0:T(8,128)(2,1)}, u32[]{:S(2)}, u32[]{:S(2)}) collective-permute-start(bf16[16,7296]{1,0:T(8,128)(2,1)} %pack.1), channel_id=1, source_target_pairs={{0,2},{1,17},{2,0},{3,19},{4,6},{5,21},{6,4},{7,23},{8,10},{9,25},... | collective-permute-start | bytes 700424 | tf_op jit(solution)/shard_map/ppermute | solution.py:115
  5.5 10.6 %collective-permute-start.2 = (bf16[16,7296]{1,0:T(8,128)(2,1)}, bf16[16,7296]{1,0:T(8,128)(2,1)}, u32[]{:S(2)}, u32[]{:S(2)}) collective-permute-start(bf16[16,7296]{1,0:T(8,128)(2,1)} %pack.1), channel_id=1, source_target_pairs={{0,4},{1,5},{2,6},{3,7},{4,8},{5,9},{6,10},{7,11},{8,12},{9,13},{1... | collective-permute-start | bytes 700424 | tf_op jit(solution)/shard_map/ppermute | solution.py:115
  14.5 21.5 %collective-permute-start.1 = (bf16[32,7296]{1,0:T(8,128)(2,1)S(1)}, bf16[32,7296]{1,0:T(8,128)(2,1)S(1)}, u32[]{:S(2)}, u32[]{:S(2)}) collective-permute-start(bf16[32,7296]{1,0:T(8,128)(2,1)S(1)} %pad_maximum_fusion), channel_id=1, source_target_pairs={{0,16},{1,3},{2,18},{3,1},{4,20},{5,7},{6,22},{7,5},{8,24},{9,11},... | collective-permute-start | bytes 1400840 | tf_op jit(solution)/shard_map/ppermute | solution.py:115
  16.1 7.9 %collective-permute-start.3 = (bf16[16,7296]{1,0:T(8,128)(2,1)}, bf16[16,7296]{1,0:T(8,128)(2,1)S(1)}, u32[]{:S(2)}, u32[]{:S(2)}) collective-permute-start(bf16[16,7296]{1,0:T(8,128)(2,1)} %collective-permute-done.2), channel_id=1, source_target_pairs={{0,2},{1,17},{2,0},{3,19},{4,6},{5,21},{6,4},{7,23},{8,10},{9,25},... | collective-permute-start | bytes 700424 | tf_op jit(solution)/shard_map/ppermute | solution.py:115
  16.7 9.0 %collective-permute-start.9 = (bf16[16,7296]{1,0:T(8,128)(2,1)}, bf16[16,7296]{1,0:T(8,128)(2,1)S(1)}, u32[]{:S(2)}, u32[]{:S(2)}) collective-permute-start(bf16[16,7296]{1,0:T(8,128)(2,1)} %collective-permute-done.2), channel_id=1, source_target_pairs={{0,4},{1,5},{2,6},{3,7},{4,8},{5,9},{6,10},{7,11},{8,12},{9,13},{1... | collective-permute-start | bytes 700424 | tf_op jit(solution)/shard_map/ppermute | solution.py:115
  24.0 20.1 %copy-start.1 = (bf16[1,7168,512]{2,1,0:T(8,128)(2,1)S(1)}, bf16[1,7168,512]{2,1,0:T(8,128)(2,1)}, u32[]{:S(2)}) copy-start(bf16[1,7168,512]{2,1,0:T(8,128)(2,1)} %gate.3) | copy-start | bytes 22020100
  25.1 12.0 %collective-permute-start.4 = (bf16[32,7296]{1,0:T(8,128)(2,1)S(1)}, bf16[32,7296]{1,0:T(8,128)(2,1)S(1)}, u32[]{:S(2)}, u32[]{:S(2)}) collective-permute-start(bf16[32,7296]{1,0:T(8,128)(2,1)S(1)} %pad_maximum_fusion.1), channel_id=1, source_target_pairs={{0,16},{1,3},{2,18},{3,1},{4,20},{5,7},{6,22},{7,5},{8,24},{9,11},... | collective-permute-start | bytes 1400840 | tf_op jit(solution)/shard_map/ppermute | solution.py:115
  25.7 8.4 %collective-permute-start.10 = (bf16[16,7296]{1,0:T(8,128)(2,1)S(1)}, bf16[16,7296]{1,0:T(8,128)(2,1)S(1)}, u32[]{:S(2)}, u32[]{:S(2)}) collective-permute-start(bf16[16,7296]{1,0:T(8,128)(2,1)S(1)} %collective-permute-done.9), channel_id=1, source_target_pairs={{0,2},{1,17},{2,0},{3,19},{4,6},{5,21},{6,4},{7,23},{8,10},{9,25},... | collective-permute-start | bytes 700424 | tf_op jit(solution)/shard_map/ppermute | solution.py:115
  27.2 7.9 %collective-permute-start.12 = (bf16[16,7296]{1,0:T(8,128)(2,1)S(1)}, bf16[16,7296]{1,0:T(8,128)(2,1)S(1)}, u32[]{:S(2)}, u32[]{:S(2)}) collective-permute-start(bf16[16,7296]{1,0:T(8,128)(2,1)S(1)} %collective-permute-done.9), channel_id=1, source_target_pairs={{0,4},{1,5},{2,6},{3,7},{4,8},{5,9},{6,10},{7,11},{8,12},{9,13},{1... | collective-permute-start | bytes 700424 | tf_op jit(solution)/shard_map/ppermute | solution.py:115
  34.1 9.4 %collective-permute-start.11 = (bf16[32,7296]{1,0:T(8,128)(2,1)S(1)}, bf16[32,7296]{1,0:T(8,128)(2,1)S(1)}, u32[]{:S(2)}, u32[]{:S(2)}) collective-permute-start(bf16[32,7296]{1,0:T(8,128)(2,1)S(1)} %pad_maximum_fusion.2), channel_id=1, source_target_pairs={{0,16},{1,3},{2,18},{3,1},{4,20},{5,7},{6,22},{7,5},{8,24},{9,11},... | collective-permute-start | bytes 1400840 | tf_op jit(solution)/shard_map/ppermute | solution.py:115
  35.1 8.2 %collective-permute-start.13 = (bf16[16,7296]{1,0:T(8,128)(2,1)S(1)}, bf16[16,7296]{1,0:T(8,128)(2,1)S(1)}, u32[]{:S(2)}, u32[]{:S(2)}) collective-permute-start(bf16[16,7296]{1,0:T(8,128)(2,1)S(1)} %collective-permute-done.12), channel_id=1, source_target_pairs={{0,2},{1,17},{2,0},{3,19},{4,6},{5,21},{6,4},{7,23},{8,10},{9,25},... | collective-permute-start | bytes 700424 | tf_op jit(solution)/shard_map/ppermute | solution.py:115
  37.1 7.0 %collective-permute-start.5 = (bf16[128,7296]{1,0:T(8,128)(2,1)S(1)}, bf16[128,7296]{1,0:T(8,128)(2,1)S(1)}, u32[]{:S(2)}, u32[]{:S(2)}) collective-permute-start(bf16[128,7296]{1,0:T(8,128)(2,1)S(1)} %constant_dynamic-update-slice_fusion.refs_0_), channel_id=1, source_target_pairs={{0,1},{1,0},{2,3},{3,2},{4,5},{5,4},{6,7},{7,6},{8,9},{9,8},{10,11... | collective-permute-start | bytes 5603336 | tf_op jit(solution)/shard_map/ppermute | solution.py:115
  43.3 11.2 %collective-permute-start.14 = (bf16[32,7296]{1,0:T(8,128)(2,1)S(1)}, bf16[32,7296]{1,0:T(8,128)(2,1)S(1)}, u32[]{:S(2)}, u32[]{:S(2)}) collective-permute-start(bf16[32,7296]{1,0:T(8,128)(2,1)S(1)} %constant_dynamic-update-slice_fusion.9.refs_1_), channel_id=1, source_target_pairs={{0,16},{1,3},{2,18},{3,1},{4,20},{5,7},{6,22},{7,5},{8,24},{9,11},... | collective-permute-start | bytes 1400840 | tf_op jit(solution)/shard_map/ppermute | solution.py:115
  43.4 16.6 %collective-permute-start.16 = (bf16[32,7296]{1,0:T(8,128)(2,1)S(1)}, bf16[32,7296]{1,0:T(8,128)(2,1)S(1)}, u32[]{:S(2)}, u32[]{:S(2)}) collective-permute-start(bf16[32,7296]{1,0:T(8,128)(2,1)S(1)} %constant_dynamic-update-slice_fusion.9.refs_1_), channel_id=1, source_target_pairs={{0,1},{1,0},{2,3},{3,2},{4,5},{5,4},{6,7},{7,6},{8,9},{9,8},{10,11... | collective-permute-start | bytes 1400840 | tf_op jit(solution)/shard_map/ppermute | solution.py:115
  43.6 16.5 %collective-permute-start.15 = (bf16[64,7296]{1,0:T(8,128)(2,1)S(1)}, bf16[64,7296]{1,0:T(8,128)(2,1)S(1)}, u32[]{:S(2)}, u32[]{:S(2)}) collective-permute-start(bf16[64,7296]{1,0:T(8,128)(2,1)S(1)} %constant_dynamic-update-slice_fusion.6.refs_0_), channel_id=1, source_target_pairs={{0,1},{1,0},{2,3},{3,2},{4,5},{5,4},{6,7},{7,6},{8,9},{9,8},{10,11... | collective-permute-start | bytes 2801672 | tf_op jit(solution)/shard_map/ppermute | solution.py:115
  53.2 39.3 %copy-start.2 = (bf16[32,7168]{1,0:T(8,128)(2,1)}, bf16[32,7168]{1,0:T(8,128)(2,1)S(1)}, u32[]{:S(2)}) copy-start(bf16[32,7168]{1,0:T(8,128)(2,1)S(1)} %get-tuple-element.14) | copy-start | bytes 1376260
  53.2 2.5 %collective-permute-start.18 = (bf16[64,7168]{1,0:T(8,128)(2,1)S(1)}, bf16[64,7168]{1,0:T(8,128)(2,1)S(1)}, u32[]{:S(2)}, u32[]{:S(2)}) collective-permute-start(bf16[64,7168]{1,0:T(8,128)(2,1)S(1)} %get-tuple-element.17), channel_id=1, source_target_pairs={{0,1},{1,0},{2,3},{3,2},{4,5},{5,4},{6,7},{7,6},{8,9},{9,8},{10,11... | collective-permute-start | bytes 2752520 | tf_op jit(solution)/shard_map/ppermute | solution.py:115
  54.6 5.4 %collective-permute-start.17 = (bf16[32,7296]{1,0:T(8,128)(2,1)S(1)}, bf16[32,7296]{1,0:T(8,128)(2,1)S(1)}, u32[]{:S(2)}, u32[]{:S(2)}) collective-permute-start(bf16[32,7296]{1,0:T(8,128)(2,1)S(1)} %broadcast_add_fusion), channel_id=1, source_target_pairs={{0,1},{1,0},{2,3},{3,2},{4,5},{5,4},{6,7},{7,6},{8,9},{9,8},{10,11... | collective-permute-start | bytes 1400840 | tf_op jit(solution)/shard_map/ppermute | solution.py:115
  55.1 2.8 %collective-permute-start.6 = (bf16[64,7168]{1,0:T(8,128)(2,1)S(1)}, bf16[64,7168]{1,0:T(8,128)(2,1)S(1)}, u32[]{:S(2)}, u32[]{:S(2)}) collective-permute-start(bf16[64,7168]{1,0:T(8,128)(2,1)S(1)} %get-tuple-element.15), channel_id=1, source_target_pairs={{0,1},{1,0},{2,3},{3,2},{4,5},{5,4},{6,7},{7,6},{8,9},{9,8},{10,11... | collective-permute-start | bytes 2752520 | tf_op jit(solution)/shard_map/ppermute | solution.py:115
  55.9 13.8 %collective-permute-start.25 = (bf16[32,7168]{1,0:T(8,128)(2,1)S(1)}, bf16[32,7168]{1,0:T(8,128)(2,1)S(1)}, u32[]{:S(2)}, u32[]{:S(2)}) collective-permute-start(bf16[32,7168]{1,0:T(8,128)(2,1)S(1)} %add_convert_fusion.2.refs_6_), channel_id=1, source_target_pairs={{0,16},{1,3},{2,18},{3,1},{4,20},{5,7},{6,22},{7,5},{8,24},{9,11},... | collective-permute-start | bytes 1376264 | tf_op jit(solution)/shard_map/ppermute | solution.py:115
  58.0 34.5 %collective-permute-start.7 = (bf16[32,7168]{1,0:T(8,128)(2,1)S(1)}, bf16[32,7168]{1,0:T(8,128)(2,1)S(1)}, u32[]{:S(2)}, u32[]{:S(2)}) collective-permute-start(bf16[32,7168]{1,0:T(8,128)(2,1)S(1)} %add_convert_fusion.3.refs_7_), channel_id=1, source_target_pairs={{0,16},{1,3},{2,18},{3,1},{4,20},{5,7},{6,22},{7,5},{8,24},{9,11},... | collective-permute-start | bytes 1376264 | tf_op jit(solution)/shard_map/ppermute | solution.py:115
  69.1 2.5 %collective-permute-start.20 = (bf16[64,7168]{1,0:T(8,128)(2,1)S(1)}, bf16[64,7168]{1,0:T(8,128)(2,1)S(1)}, u32[]{:S(2)}, u32[]{:S(2)}) collective-permute-start(bf16[64,7168]{1,0:T(8,128)(2,1)S(1)} %get-tuple-element.23), channel_id=1, source_target_pairs={{0,1},{1,0},{2,3},{3,2},{4,5},{5,4},{6,7},{7,6},{8,9},{9,8},{10,11... | collective-permute-start | bytes 2752520 | tf_op jit(solution)/shard_map/ppermute | solution.py:115
  69.2 13.4 %collective-permute-start.19 = (bf16[64,7168]{1,0:T(8,128)(2,1)S(1)}, bf16[64,7168]{1,0:T(8,128)(2,1)S(1)}, u32[]{:S(2)}, u32[]{:S(2)}) collective-permute-start(bf16[64,7168]{1,0:T(8,128)(2,1)S(1)} %get-tuple-element.20), channel_id=1, source_target_pairs={{0,1},{1,0},{2,3},{3,2},{4,5},{5,4},{6,7},{7,6},{8,9},{9,8},{10,11... | collective-permute-start | bytes 2752520 | tf_op jit(solution)/shard_map/ppermute | solution.py:115
  69.8 7.4 %collective-permute-start.26 = (bf16[16,7168]{1,0:T(8,128)(2,1)S(1)}, bf16[16,7168]{1,0:T(8,128)(2,1)S(1)}, u32[]{:S(2)}, u32[]{:S(2)}) collective-permute-start(bf16[16,7168]{1,0:T(8,128)(2,1)S(1)} %add_convert_fusion.8), channel_id=1, source_target_pairs={{0,2},{1,17},{2,0},{3,19},{4,6},{5,21},{6,4},{7,23},{8,10},{9,25},... | collective-permute-start | bytes 688136 | tf_op jit(solution)/shard_map/ppermute | solution.py:115
  71.8 8.5 %collective-permute-start.21 = (bf16[32,7168]{1,0:T(8,128)(2,1)S(1)}, bf16[32,7168]{1,0:T(8,128)(2,1)S(1)}, u32[]{:S(2)}, u32[]{:S(2)}) collective-permute-start(bf16[32,7168]{1,0:T(8,128)(2,1)S(1)} %add_convert_fusion), channel_id=1, source_target_pairs={{0,16},{1,3},{2,18},{3,1},{4,20},{5,7},{6,22},{7,5},{8,24},{9,11},... | collective-permute-start | bytes 1376264 | tf_op jit(solution)/shard_map/ppermute | solution.py:115
  77.3 7.9 %collective-permute-start.27 = (bf16[16,7168]{1,0:T(8,128)(2,1)S(1)}, bf16[16,7168]{1,0:T(8,128)(2,1)S(1)}, u32[]{:S(2)}, u32[]{:S(2)}) collective-permute-start(bf16[16,7168]{1,0:T(8,128)(2,1)S(1)} %add_convert_fusion.7), channel_id=1, source_target_pairs={{0,4},{1,5},{2,6},{3,7},{4,8},{5,9},{6,10},{7,11},{8,12},{9,13},{1... | collective-permute-start | bytes 688136 | tf_op jit(solution)/shard_map/ppermute | solution.py:115
  80.4 7.5 %collective-permute-start.24 = (bf16[16,7168]{1,0:T(8,128)(2,1)S(1)}, bf16[16,7168]{1,0:T(8,128)(2,1)S(1)}, u32[]{:S(2)}, u32[]{:S(2)}) collective-permute-start(bf16[16,7168]{1,0:T(8,128)(2,1)S(1)} %add_convert_fusion.9), channel_id=1, source_target_pairs={{0,2},{1,17},{2,0},{3,19},{4,6},{5,21},{6,4},{7,23},{8,10},{9,25},... | collective-permute-start | bytes 688136 | tf_op jit(solution)/shard_map/ppermute | solution.py:115
  82.8 8.5 %collective-permute-start.22 = (bf16[32,7168]{1,0:T(8,128)(2,1)S(1)}, bf16[32,7168]{1,0:T(8,128)(2,1)S(1)}, u32[]{:S(2)}, u32[]{:S(2)}) collective-permute-start(bf16[32,7168]{1,0:T(8,128)(2,1)S(1)} %fusion.9), channel_id=1, source_target_pairs={{0,16},{1,3},{2,18},{3,1},{4,20},{5,7},{6,22},{7,5},{8,24},{9,11},... | collective-permute-start | bytes 1376264 | tf_op jit(solution)/shard_map/ppermute | solution.py:115
  88.0 7.9 %collective-permute-start.28 = (bf16[16,7168]{1,0:T(8,128)(2,1)S(1)}, bf16[16,7168]{1,0:T(8,128)(2,1)S(1)}, u32[]{:S(2)}, u32[]{:S(2)}) collective-permute-start(bf16[16,7168]{1,0:T(8,128)(2,1)S(1)} %add_convert_fusion.6), channel_id=1, source_target_pairs={{0,4},{1,5},{2,6},{3,7},{4,8},{5,9},{6,10},{7,11},{8,12},{9,13},{1... | collective-permute-start | bytes 688136 | tf_op jit(solution)/shard_map/ppermute | solution.py:115
  91.4 6.1 %collective-permute-start.23 = (bf16[16,7168]{1,0:T(8,128)(2,1)S(1)}, bf16[16,7168]{1,0:T(8,128)(2,1)S(1)}, u32[]{:S(2)}, u32[]{:S(2)}) collective-permute-start(bf16[16,7168]{1,0:T(8,128)(2,1)S(1)} %add_convert_fusion.10), channel_id=1, source_target_pairs={{0,2},{1,17},{2,0},{3,19},{4,6},{5,21},{6,4},{7,23},{8,10},{9,25},... | collective-permute-start | bytes 688136 | tf_op jit(solution)/shard_map/ppermute | solution.py:115
  92.6 11.5 %collective-permute-start.8 = (bf16[16,7168]{1,0:T(8,128)(2,1)S(1)}, bf16[16,7168]{1,0:T(8,128)(2,1)}, u32[]{:S(2)}, u32[]{:S(2)}) collective-permute-start(bf16[16,7168]{1,0:T(8,128)(2,1)S(1)} %add_convert_fusion.11), channel_id=1, source_target_pairs={{0,2},{1,17},{2,0},{3,19},{4,6},{5,21},{6,4},{7,23},{8,10},{9,25},... | collective-permute-start | bytes 688136 | tf_op jit(solution)/shard_map/ppermute | solution.py:115
  98.4 8.9 %collective-permute-start.29 = (bf16[16,7168]{1,0:T(8,128)(2,1)}, bf16[16,7168]{1,0:T(8,128)(2,1)}, u32[]{:S(2)}, u32[]{:S(2)}) collective-permute-start(bf16[16,7168]{1,0:T(8,128)(2,1)} %add_convert_fusion.5), channel_id=1, source_target_pairs={{0,4},{1,5},{2,6},{3,7},{4,8},{5,9},{6,10},{7,11},{8,12},{9,13},{1... | collective-permute-start | bytes 688136 | tf_op jit(solution)/shard_map/ppermute | solution.py:115
  (3 other events, 21.8 us)

commit v5 on v4

--- a/solution.py
+++ b/solution.py
@@ -126,7 +126,9 @@
         self.second = permutation(
             n_dev, lambda y, z, x, c: (y, z, 1 - x, c) if c else (1 - y, z, x, c)
         )
-        self.ring = permutation(n_dev, lambda y, z, x, c: (y, (z + 1) % line, x, c))
+        stops = list(range(0, line, 2)) + list(range(1, line, 2))[::-1]
+        following = {z: stops[(i + 1) % line] for i, z in enumerate(stops)}
+        self.ring = permutation(n_dev, lambda y, z, x, c: (y, following[z], x, c))
 
 
 def plus(*terms):
@@ -181,34 +183,40 @@
     )(expert_ids.T, gate_coef.T, hidden_in)
 
 
-def expert_kernel(sizes, sizes_out, n_experts, steps, me, gate, up, down, *refs):
+def hold_kernel(weight, *refs):
+    refs[-1][...] = jnp.zeros(refs[-1].shape, refs[-1].dtype)
+
+
+def hold(weight, *after):
+    return pl.pallas_call(
+        hold_kernel,
+        in_specs=[HELD] + [ANYWHERE] * len(after),
+        out_specs=HELD,
+        out_shape=jax.ShapeDtypeStruct((8, 128), jnp.float32),
+        compiler_params=pltpu.CompilerParams(vmem_limit_bytes=1 * 2**20),
+        cost_estimate=pl.CostEstimate(
+            flops=0, bytes_accessed=2 * math.prod(weight.shape), transcendentals=0
+        ),
+        name="hold",
+    )(weight, *after)
+
+
+def expert_kernel(sizes, sizes_out, n_experts, steps, me, w_gate, w_up, w_down, *refs):
     xs = refs[: len(sizes)]
-    outs = refs[-10 - len(sizes_out) : -10]
-    w_gate, w_up, w_down, acc_gate, acc_up, hidden, coef = refs[-10:-3]
-    gate_sem, up_sem, down_sem = refs[-3:]
-    width = w_gate.shape[0]
+    outs = refs[-4 - len(sizes_out) : -4]
+    acc_gate, acc_up, hidden, coef = refs[-4:]
+    width = w_gate.shape[1]
     chunk = width // steps
-    copy = pltpu.make_async_copy
     part = [pl.ds(k * chunk, chunk) for k in range(steps)]
-    gate_in = [copy(gate.at[0, p], w_gate.at[p], gate_sem.at[k]) for k, p in enumerate(part)]
-    up_in = [copy(up.at[0, p], w_up.at[p], up_sem.at[k]) for k, p in enumerate(part)]
-    down_in = [copy(down.at[0, :, p], w_down.at[:, p], down_sem.at[k]) for k, p in enumerate(part)]
-    for k in range(steps):
-        gate_in[k].start()
-        up_in[k].start()
-    for c in down_in:
-        c.start()
     tail = jnp.concatenate([x[:, width:] for x in xs], axis=0).astype(jnp.float32)
     lane = lax.broadcasted_iota(jnp.int32, tail.shape, 1)
     mine = (lane == me[0]) | (lane == me[0] + n_experts)
     picked = jnp.sum(jnp.where(mine, tail, 0.0), axis=1, keepdims=True)
     coef[...] = jnp.broadcast_to(picked, coef.shape)
     for k in range(steps):
-        gate_in[k].wait()
-        up_in[k].wait()
         xk = jnp.concatenate([x[:, part[k]] for x in xs], axis=0)
-        g = jnp.dot(xk, w_gate[part[k], :], preferred_element_type=jnp.float32)
-        u = jnp.dot(xk, w_up[part[k], :], preferred_element_type=jnp.float32)
+        g = jnp.dot(xk, w_gate[0, part[k], :], preferred_element_type=jnp.float32)
+        u = jnp.dot(xk, w_up[0, part[k], :], preferred_element_type=jnp.float32)
         if k == 0:
             acc_gate[...] = g
             acc_up[...] = u
@@ -218,8 +226,7 @@
     g = acc_gate[...]
     hidden[...] = (g / (1.0 + jnp.exp(-g)) * acc_up[...]).astype(jnp.bfloat16)
     for k in range(steps):
-        down_in[k].wait()
-        yk = jnp.dot(hidden[...], w_down[:, part[k]], preferred_element_type=jnp.float32)
+        yk = jnp.dot(hidden[...], w_down[0, :, part[k]], preferred_element_type=jnp.float32)
         yk = (yk * coef[:, :1]).astype(jnp.bfloat16)
         row = 0
         for out in outs:
@@ -238,22 +245,16 @@
     me = lax.axis_index("dev").astype(jnp.int32).reshape(1)
     return pl.pallas_call(
         functools.partial(expert_kernel, sizes, outs, n_experts, steps),
-        in_specs=[SCALARS] + [FAR] * 3 + [HELD] * len(xs) + [ANYWHERE] * len(after),
+        in_specs=[SCALARS] + [HELD] * 3 + [HELD] * len(xs) + [ANYWHERE] * len(after),
         out_specs=[HELD] * len(outs),
         scratch_shapes=[
-            pltpu.VMEM((width, hidden_width), jnp.bfloat16),
-            pltpu.VMEM((width, hidden_width), jnp.bfloat16),
-            pltpu.VMEM((hidden_width, width), jnp.bfloat16),
             pltpu.VMEM((m, hidden_width), jnp.float32),
             pltpu.VMEM((m, hidden_width), jnp.float32),
             pltpu.VMEM((m, hidden_width), jnp.bfloat16),
             pltpu.VMEM((m, 128), jnp.float32),
-            pltpu.SemaphoreType.DMA((steps,)),
-            pltpu.SemaphoreType.DMA((steps,)),
-            pltpu.SemaphoreType.DMA((steps,)),
         ],
         out_shape=[jax.ShapeDtypeStruct((r, width), jnp.bfloat16) for r in outs],
-        compiler_params=pltpu.CompilerParams(vmem_limit_bytes=33 * 2**20),
+        compiler_params=pltpu.CompilerParams(vmem_limit_bytes=8 * 2**20),
         cost_estimate=pl.CostEstimate(
             flops=6 * m * width * hidden_width,
             bytes_accessed=1,
@@ -277,7 +278,8 @@
     far = [mv.second(a) for a in near]
     pairs = [a for k in range(n) for a in (near[k], far[k])]
     own = cat(*pairs[: 2 * half])
-    early = expert_group([own, mv.core(own)], half, *weights, n_dev)
+    held = [hold(w, a) for w, a in zip(weights, (block[1], block[2], near[2]))]
+    early = expert_group([own, mv.core(own)], half, *weights, n_dev, *held)
     rows = block[0].shape[0]
     y_near, y_far = early[0 : 2 * half : 2], early[1 : 2 * half : 2]
     order = list(range(1, n)) + [0]

time: 110 us -> 100 us (0.909)
  waiting for transfers between devices: 37 us -> 25.8 us
  local copies, waits for them, and re-layouts: 4.22 us -> 12.7 us
  Pallas kernels: 20.1 us -> 13.8 us
    ppermute x30, waiting for transfers between devices: 37 us -> 25.8 us  [permutation(): return lambda a: lax.ppermute(a, AXES, pairs)]
    unnamed x18 -> x28, local copies, waits for them, and re-layouts: 3.06 us -> 11.5 us
    pallas_call x2, Pallas kernels: 18.2 us -> 11.9 us  [expert_group(): pl.pallas_call(functools.partial(expert_kernel, sizes, outs, n_experts, s...]
  transfers between devices with their start and end apart: 30 -> 30, of which waited for: 14 -> 15; matrix products, arithmetic and copies ran while one was open for 17% -> 17% of each run, Pallas kernels for 17% -> 12%
where the time goes in v5:
time: 100 us; the launch traced here: 99.6 us
  starting transfers between devices  29.9 us (30%)
  waiting for transfers between devices  25.8 us (26%)
  Pallas kernels  13.8 us (14%)
  local copies, waits for them, and re-layouts  12.7 us (13%)
  matrix products  7.91 us (8%)
  other arithmetic  7.26 us (7%)
  between operations  2.24 us (2%)
    ppermute x30, starting transfers between devices, permutation(): return lambda a: lax.ppermute(a, AXES, pairs)  29.9 us
    ppermute x30, waiting for transfers between devices, permutation(): return lambda a: lax.ppermute(a, AXES, pairs)  25.8 us
    pallas_call x2, Pallas kernels, expert_group(): pl.pallas_call(functools.partial(expert_kernel, sizes, outs, n_experts, s...  11.9 us
    unnamed x28, local copies, waits for them, and re-layouts  11.5 us
    dot_general x1, matrix products, attend(): jnp.einsum('rhl,rlc->rhc', weights, kv_cache[:, :, :LAT], preferred_eleme...  4.82 us
    convert_element_type x11, other arithmetic, plus(): return total.astype(jnp.bfloat16)  3.64 us
    dot_general x1, matrix products, attend(): jnp.einsum('rhk,rlk->rhl', query_lat, kv_cache, preferred_element_type=jn...  3.09 us
  transfers between devices with their start and end apart: 30, of which 15 were waited for; matrix products, arithmetic and copies ran while one was open for 17% of the time, Pallas kernels for 12%

profile of v5, /device:TPU:0, one launch (start us, length us, event | category | flops | bytes accessed | tf_op | source)
XLA Modules:
  0.0 99.6 jit_solution(8232913839748805614)
XLA Ops:
  0.6 1.9 %pack.1 = bf16[16,7296]{1,0:T(8,128)(2,1)} custom-call(s32[8,16]{1,0:T(8,128)} %bitcast.11, f32[8,16]{1,0:T(8,128)} %bitcast.12, bf16[16,7168]{1,0:T(8,128)(2,1)} %x.1), custom_call_target="tpu_custom_call" | custom-call | tf_op jit(solution)/shard_map/pack/pallas_call | solution.py:177
  2.5 2.9 %collective-permute-start = (bf16[16,7296]{1,0:T(8,128)(2,1)}, bf16[16,7296]{1,0:T(8,128)(2,1)}, u32[]{:S(2)}, u32[]{:S(2)}) collective-permute-start(bf16[16,7296]{1,0:T(8,128)(2,1)} %pack.1), channel_id=1, source_target_pairs={{0,2},{1,17},{2,0},{3,19},{4,6},{5,21},{6,4},{7,23},{8,10},{9,25},... | collective-permute-start | bytes 700424 | tf_op jit(solution)/shard_map/ppermute | solution.py:115
  5.5 2.6 %collective-permute-start.2 = (bf16[16,7296]{1,0:T(8,128)(2,1)}, bf16[16,7296]{1,0:T(8,128)(2,1)S(1)}, u32[]{:S(2)}, u32[]{:S(2)}) collective-permute-start(bf16[16,7296]{1,0:T(8,128)(2,1)} %pack.1), channel_id=1, source_target_pairs={{0,8},{1,9},{2,10},{3,11},{4,0},{5,1},{6,2},{7,3},{8,12},{9,13},{1... | collective-permute-start | bytes 700424 | tf_op jit(solution)/shard_map/ppermute | solution.py:115
  9.8 3.1 %fusion.8 = f32[16,64,128]{2,1,0:T(8,128)} fusion(bf16[16,64,576]{2,1,0:T(8,128)(2,1)S(1)} %copy-done, bf16[16,128,576]{1,2,0:T(8,128)(2,1)} %param.13, pred[16,128]{1,0:T(8,128)(4,1)S(1)} %iota_compare_fusion), kind=kOutput, calls=%fused_computation.7 | convolution fusion | flops 151257088 | bytes 4065280 | tf_op jit(solution)/shard_map/rhk,rlk->rhl/dot_general | solution.py:20
  12.9 1.6 %fusion.12 = f32[16,64]{1,0:T(8,128)S(1)} fusion(f32[16,64,128]{2,1,0:T(8,128)} %fusion.8), kind=kOutput, calls=%fused_computation.41 | output fusion | flops 262271 | bytes 528384 | tf_op jit(solution)/shard_map/sub | solution.py:27
  15.6 1.6 %collective-permute-start.1 = (bf16[32,7296]{1,0:T(8,128)(2,1)S(1)}, bf16[32,7296]{1,0:T(8,128)(2,1)S(1)}, u32[]{:S(2)}, u32[]{:S(2)}) collective-permute-start(bf16[32,7296]{1,0:T(8,128)(2,1)S(1)} %pad_maximum_fusion), channel_id=1, source_target_pairs={{0,16},{1,3},{2,18},{3,1},{4,20},{5,7},{6,22},{7,5},{8,24},{9,11},... | collective-permute-start | bytes 1400840 | tf_op jit(solution)/shard_map/ppermute | solution.py:115
  17.7 1.6 %collective-permute-start.6 = (bf16[16,7296]{1,0:T(8,128)(2,1)S(1)}, bf16[16,7296]{1,0:T(8,128)(2,1)S(1)}, u32[]{:S(2)}, u32[]{:S(2)}) collective-permute-start(bf16[16,7296]{1,0:T(8,128)(2,1)S(1)} %collective-permute-done.2.refs_0_), channel_id=1, source_target_pairs={{0,8},{1,9},{2,10},{3,11},{4,0},{5,1},{6,2},{7,3},{8,12},{9,13},{1... | collective-permute-start | bytes 700424 | tf_op jit(solution)/shard_map/ppermute | solution.py:115
  20.2 3.1 %copy-done.1 = bf16[1,7168,512]{2,1,0:T(8,128)(2,1)S(1)} copy-done((bf16[1,7168,512]{2,1,0:T(8,128)(2,1)S(1)}, bf16[1,7168,512]{2,1,0:T(8,128)(2,1)}, u32[]{:S(2)}) %copy-start.1) | copy-done | bytes 7340056
  23.3 1.7 %collective-permute-done.3 = bf16[16,7296]{1,0:T(8,128)(2,1)S(1)} collective-permute-done((bf16[16,7296]{1,0:T(8,128)(2,1)S(1)}, bf16[16,7296]{1,0:T(8,128)(2,1)S(1)}, u32[]{:S(2)}, u32[]{:S(2)}) %collective-permute-start.3) | collective-permute-done | bytes 233504 | tf_op jit(solution)/shard_map/ppermute | solution.py:115
  25.7 1.3 %collective-permute-start.7 = (bf16[16,7296]{1,0:T(8,128)(2,1)S(1)}, bf16[16,7296]{1,0:T(8,128)(2,1)S(1)}, u32[]{:S(2)}, u32[]{:S(2)}) collective-permute-start(bf16[16,7296]{1,0:T(8,128)(2,1)S(1)} %collective-permute-done.6.refs_0_), channel_id=1, source_target_pairs={{0,2},{1,17},{2,0},{3,19},{4,6},{5,21},{6,4},{7,23},{8,10},{9,25},... | collective-permute-start | bytes 700424 | tf_op jit(solution)/shard_map/ppermute | solution.py:115
  27.0 1.6 %collective-permute-start.12 = (bf16[16,7296]{1,0:T(8,128)(2,1)S(1)}, bf16[16,7296]{1,0:T(8,128)(2,1)S(1)}, u32[]{:S(2)}, u32[]{:S(2)}) collective-permute-start(bf16[16,7296]{1,0:T(8,128)(2,1)S(1)} %collective-permute-done.6.refs_0_), channel_id=1, source_target_pairs={{0,8},{1,9},{2,10},{3,11},{4,0},{5,1},{6,2},{7,3},{8,12},{9,13},{1... | collective-permute-start | bytes 700424 | tf_op jit(solution)/shard_map/ppermute | solution.py:115
  28.6 3.1 %copy-done.2 = bf16[1,7168,512]{2,1,0:T(8,128)(2,1)S(1)} copy-done((bf16[1,7168,512]{2,1,0:T(8,128)(2,1)S(1)}, bf16[1,7168,512]{2,1,0:T(8,128)(2,1)}, u32[]{:S(2)}) %copy-start.2) | copy-done | bytes 7340056
  31.7 2.6 %collective-permute-done.7 = bf16[16,7296]{1,0:T(8,128)(2,1)S(1)} collective-permute-done((bf16[16,7296]{1,0:T(8,128)(2,1)S(1)}, bf16[16,7296]{1,0:T(8,128)(2,1)S(1)}, u32[]{:S(2)}, u32[]{:S(2)}) %collective-permute-start.7) | collective-permute-done | bytes 233504 | tf_op jit(solution)/shard_map/ppermute | solution.py:115
  35.2 3.2 %copy-done.4 = bf16[1,512,7168]{2,1,0:T(8,128)(2,1)S(1)} copy-done((bf16[1,512,7168]{2,1,0:T(8,128)(2,1)S(1)}, bf16[1,512,7168]{2,1,0:T(8,128)(2,1)}, u32[]{:S(2)}) %copy-start.4) | copy-done | bytes 7340056
  38.5 2.7 %collective-permute-done.13 = bf16[16,7296]{1,0:T(8,128)(2,1)S(1)} collective-permute-done((bf16[16,7296]{1,0:T(8,128)(2,1)S(1)}, bf16[16,7296]{1,0:T(8,128)(2,1)S(1)}, u32[]{:S(2)}, u32[]{:S(2)}) %collective-permute-start.13) | collective-permute-done | bytes 233504 | tf_op jit(solution)/shard_map/ppermute | solution.py:115
  41.2 1.5 %collective-permute-start.14 = (bf16[32,7296]{1,0:T(8,128)(2,1)S(1)}, bf16[32,7296]{1,0:T(8,128)(2,1)S(1)}, u32[]{:S(2)}, u32[]{:S(2)}) collective-permute-start(bf16[32,7296]{1,0:T(8,128)(2,1)S(1)} %constant_dynamic-update-slice_fusion.11.refs_1_), channel_id=1, source_target_pairs={{0,16},{1,3},{2,18},{3,1},{4,20},{5,7},{6,22},{7,5},{8,24},{9,11},... | collective-permute-start | bytes 1400840 | tf_op jit(solution)/shard_map/ppermute | solution.py:115
  43.4 5.9 %experts.2 = (bf16[32,7168]{1,0:T(8,128)(2,1)S(1)}, bf16[32,7168]{1,0:T(8,128)(2,1)S(1)}, bf16[32,7168]{1,0:T(8,128)(2,1)S(1)}, bf16[32,7168]{1,0:T(8,128)(2,1)S...) custom-call(s32[1]{0:T(128)} %bitcast.me, bf16[1,7168,512]{2,1,0:T(8,128)(2,1)S(1)} %bitcast.10, ...), custom_call_target="tpu_custom_call" | custom-call | flops 5637144576 | bytes 1 | tf_op jit(solution)/shard_map/experts/pallas_call | solution.py:246
  52.6 1.4 %collective-permute-done.8 = bf16[64,7168]{1,0:T(8,128)(2,1)S(1)} collective-permute-done((bf16[64,7168]{1,0:T(8,128)(2,1)S(1)}, bf16[64,7168]{1,0:T(8,128)(2,1)S(1)}, u32[]{:S(2)}, u32[]{:S(2)}) %collective-permute-start.8) | collective-permute-done | bytes 917536 | tf_op jit(solution)/shard_map/ppermute | solution.py:115
  54.8 5.9 %experts.3 = (bf16[32,7168]{1,0:T(8,128)(2,1)S(1)}, bf16[32,7168]{1,0:T(8,128)(2,1)S(1)}, bf16[32,7168]{1,0:T(8,128)(2,1)S(1)}, bf16[32,7168]{1,0:T(8,128)(2,1)S...) custom-call(s32[1]{0:T(128)} %bitcast.me, bf16[1,7168,512]{2,1,0:T(8,128)(2,1)S(1)} %bitcast.10, ...), custom_call_target="tpu_custom_call" | custom-call | flops 5637144576 | bytes 1 | tf_op jit(solution)/shard_map/experts/pallas_call | solution.py:246
  61.4 1.4 %collective-permute-start.26 = (bf16[16,7168]{1,0:T(8,128)(2,1)S(1)}, bf16[16,7168]{1,0:T(8,128)(2,1)S(1)}, u32[]{:S(2)}, u32[]{:S(2)}) collective-permute-start(bf16[16,7168]{1,0:T(8,128)(2,1)S(1)} %add_convert_fusion.8), channel_id=1, source_target_pairs={{0,2},{1,17},{2,0},{3,19},{4,6},{5,21},{6,4},{7,23},{8,10},{9,25},... | collective-permute-start | bytes 688136 | tf_op jit(solution)/shard_map/ppermute | solution.py:115
  63.4 1.6 %collective-permute-start.21 = (bf16[32,7168]{1,0:T(8,128)(2,1)S(1)}, bf16[32,7168]{1,0:T(8,128)(2,1)S(1)}, u32[]{:S(2)}, u32[]{:S(2)}) collective-permute-start(bf16[32,7168]{1,0:T(8,128)(2,1)S(1)} %add_convert_fusion), channel_id=1, source_target_pairs={{0,16},{1,3},{2,18},{3,1},{4,20},{5,7},{6,22},{7,5},{8,24},{9,11},... | collective-permute-start | bytes 1376264 | tf_op jit(solution)/shard_map/ppermute | solution.py:115
  65.0 3.8 %collective-permute-done.26 = bf16[16,7168]{1,0:T(8,128)(2,1)S(1)} collective-permute-done((bf16[16,7168]{1,0:T(8,128)(2,1)S(1)}, bf16[16,7168]{1,0:T(8,128)(2,1)S(1)}, u32[]{:S(2)}, u32[]{:S(2)}) %collective-permute-start.26) | collective-permute-done | bytes 229408 | tf_op jit(solution)/shard_map/ppermute | solution.py:115
  68.9 1.6 %collective-permute-start.27 = (bf16[16,7168]{1,0:T(8,128)(2,1)S(1)}, bf16[16,7168]{1,0:T(8,128)(2,1)S(1)}, u32[]{:S(2)}, u32[]{:S(2)}) collective-permute-start(bf16[16,7168]{1,0:T(8,128)(2,1)S(1)} %add_convert_fusion.7), channel_id=1, source_target_pairs={{0,8},{1,9},{2,10},{3,11},{4,0},{5,1},{6,2},{7,3},{8,12},{9,13},{1... | collective-permute-start | bytes 688136 | tf_op jit(solution)/shard_map/ppermute | solution.py:115
  70.5 2.3 %collective-permute-done.21 = bf16[32,7168]{1,0:T(8,128)(2,1)S(1)} collective-permute-done((bf16[32,7168]{1,0:T(8,128)(2,1)S(1)}, bf16[32,7168]{1,0:T(8,128)(2,1)S(1)}, u32[]{:S(2)}, u32[]{:S(2)}) %collective-permute-start.21) | collective-permute-done | bytes 458784 | tf_op jit(solution)/shard_map/ppermute | solution.py:115
  74.8 1.5 %collective-permute-start.22 = (bf16[32,7168]{1,0:T(8,128)(2,1)S(1)}, bf16[32,7168]{1,0:T(8,128)(2,1)S(1)}, u32[]{:S(2)}, u32[]{:S(2)}) collective-permute-start(bf16[32,7168]{1,0:T(8,128)(2,1)S(1)} %fusion.9), channel_id=1, source_target_pairs={{0,16},{1,3},{2,18},{3,1},{4,20},{5,7},{6,22},{7,5},{8,24},{9,11},... | collective-permute-start | bytes 1376264 | tf_op jit(solution)/shard_map/ppermute | solution.py:115
  76.5 3.8 %collective-permute-done.24 = bf16[16,7168]{1,0:T(8,128)(2,1)S(1)} collective-permute-done((bf16[16,7168]{1,0:T(8,128)(2,1)S(1)}, bf16[16,7168]{1,0:T(8,128)(2,1)S(1)}, u32[]{:S(2)}, u32[]{:S(2)}) %collective-permute-start.24) | collective-permute-done | bytes 229408 | tf_op jit(solution)/shard_map/ppermute | solution.py:115
  80.5 1.6 %collective-permute-start.28 = (bf16[16,7168]{1,0:T(8,128)(2,1)S(1)}, bf16[16,7168]{1,0:T(8,128)(2,1)S(1)}, u32[]{:S(2)}, u32[]{:S(2)}) collective-permute-start(bf16[16,7168]{1,0:T(8,128)(2,1)S(1)} %add_convert_fusion.6), channel_id=1, source_target_pairs={{0,8},{1,9},{2,10},{3,11},{4,0},{5,1},{6,2},{7,3},{8,12},{9,13},{1... | collective-permute-start | bytes 688136 | tf_op jit(solution)/shard_map/ppermute | solution.py:115
  83.4 1.6 %collective-permute-start.23 = (bf16[16,7168]{1,0:T(8,128)(2,1)S(1)}, bf16[16,7168]{1,0:T(8,128)(2,1)S(1)}, u32[]{:S(2)}, u32[]{:S(2)}) collective-permute-start(bf16[16,7168]{1,0:T(8,128)(2,1)S(1)} %add_convert_fusion.10), channel_id=1, source_target_pairs={{0,2},{1,17},{2,0},{3,19},{4,6},{5,21},{6,4},{7,23},{8,10},{9,25},... | collective-permute-start | bytes 688136 | tf_op jit(solution)/shard_map/ppermute | solution.py:115
  86.6 2.9 %collective-permute-done.23 = bf16[16,7168]{1,0:T(8,128)(2,1)S(1)} collective-permute-done((bf16[16,7168]{1,0:T(8,128)(2,1)S(1)}, bf16[16,7168]{1,0:T(8,128)(2,1)S(1)}, u32[]{:S(2)}, u32[]{:S(2)}) %collective-permute-start.23) | collective-permute-done | bytes 229408 | tf_op jit(solution)/shard_map/ppermute | solution.py:115
  90.3 1.6 %collective-permute-start.29 = (bf16[16,7168]{1,0:T(8,128)(2,1)}, bf16[16,7168]{1,0:T(8,128)(2,1)}, u32[]{:S(2)}, u32[]{:S(2)}) collective-permute-start(bf16[16,7168]{1,0:T(8,128)(2,1)} %add_convert_fusion.5), channel_id=1, source_target_pairs={{0,8},{1,9},{2,10},{3,11},{4,0},{5,1},{6,2},{7,3},{8,12},{9,13},{1... | collective-permute-start | bytes 688136 | tf_op jit(solution)/shard_map/ppermute | solution.py:115
  91.9 4.8 %fusion.3 = bf16[16,64,512]{2,1,0:T(8,128)(2,1)} fusion(bf16[16,128,576]{1,2,0:T(8,128)(2,1)} %param.13, f32[16,64]{1,0:T(8,128)S(1)} %fusion.12, f32[16,64,128]{2,1,0:T(8,128)} %fusion.8), kind=kOutput, calls=%fused_computation.3 | convolution fusion | flops 135136384 | bytes 4198400 | tf_op jit(solution)/shard_map/rhl,rlc->rhc/dot_general | solution.py:30
  97.7 1.9 %add_convert_fusion.4 = bf16[16,7168]{1,0:T(8,128)(2,1)} fusion(bf16[16,7168]{1,0:T(8,128)(2,1)} %collective-permute-done.29, bf16[16,7168]{1,0:T(8,128)(2,1)} %collective-permute-done.10, bf16[32,7168]{1,0:T(8,128)(2,1)S(1)} %collective-permute-done.9, bf16[64,7168]{1,0:T(8,128)(2,1)S(1)} %collective-permute-done.8, bf16[32,7168]{1,0:T(8,128)(2,1)S(1)} %copy-done.7), kind=kLoop, calls=%fused_computation.16 | loop fusion | flops 1146880 | bytes 1376256 | tf_op jit(solution)/shard_map/convert_element_type | solution.py:138
  (87 shorter events, 17.5 us)
Async XLA Ops:
  2.5 11.9 %collective-permute-start = (bf16[16,7296]{1,0:T(8,128)(2,1)}, bf16[16,7296]{1,0:T(8,128)(2,1)}, u32[]{:S(2)}, u32[]{:S(2)}) collective-permute-start(bf16[16,7296]{1,0:T(8,128)(2,1)} %pack.1), channel_id=1, source_target_pairs={{0,2},{1,17},{2,0},{3,19},{4,6},{5,21},{6,4},{7,23},{8,10},{9,25},... | collective-permute-start | bytes 700424 | tf_op jit(solution)/shard_map/ppermute | solution.py:115
  5.5 11.7 %collective-permute-start.2 = (bf16[16,7296]{1,0:T(8,128)(2,1)}, bf16[16,7296]{1,0:T(8,128)(2,1)S(1)}, u32[]{:S(2)}, u32[]{:S(2)}) collective-permute-start(bf16[16,7296]{1,0:T(8,128)(2,1)} %pack.1), channel_id=1, source_target_pairs={{0,8},{1,9},{2,10},{3,11},{4,0},{5,1},{6,2},{7,3},{8,12},{9,13},{1... | collective-permute-start | bytes 700424 | tf_op jit(solution)/shard_map/ppermute | solution.py:115
  15.6 18.8 %collective-permute-start.1 = (bf16[32,7296]{1,0:T(8,128)(2,1)S(1)}, bf16[32,7296]{1,0:T(8,128)(2,1)S(1)}, u32[]{:S(2)}, u32[]{:S(2)}) collective-permute-start(bf16[32,7296]{1,0:T(8,128)(2,1)S(1)} %pad_maximum_fusion), channel_id=1, source_target_pairs={{0,16},{1,3},{2,18},{3,1},{4,20},{5,7},{6,22},{7,5},{8,24},{9,11},... | collective-permute-start | bytes 1400840 | tf_op jit(solution)/shard_map/ppermute | solution.py:115
  17.2 7.9 %collective-permute-start.3 = (bf16[16,7296]{1,0:T(8,128)(2,1)S(1)}, bf16[16,7296]{1,0:T(8,128)(2,1)S(1)}, u32[]{:S(2)}, u32[]{:S(2)}) collective-permute-start(bf16[16,7296]{1,0:T(8,128)(2,1)S(1)} %collective-permute-done.2.refs_0_), channel_id=1, source_target_pairs={{0,2},{1,17},{2,0},{3,19},{4,6},{5,21},{6,4},{7,23},{8,10},{9,25},... | collective-permute-start | bytes 700424 | tf_op jit(solution)/shard_map/ppermute | solution.py:115
  17.7 7.9 %collective-permute-start.6 = (bf16[16,7296]{1,0:T(8,128)(2,1)S(1)}, bf16[16,7296]{1,0:T(8,128)(2,1)S(1)}, u32[]{:S(2)}, u32[]{:S(2)}) collective-permute-start(bf16[16,7296]{1,0:T(8,128)(2,1)S(1)} %collective-permute-done.2.refs_0_), channel_id=1, source_target_pairs={{0,8},{1,9},{2,10},{3,11},{4,0},{5,1},{6,2},{7,3},{8,12},{9,13},{1... | collective-permute-start | bytes 700424 | tf_op jit(solution)/shard_map/ppermute | solution.py:115
  23.3 20.0 %copy-start.5 = (bf16[1,512,7168]{2,1,0:T(8,128)(2,1)S(1)}, bf16[1,512,7168]{2,1,0:T(8,128)(2,1)}, u32[]{:S(2)}) copy-start(bf16[1,512,7168]{2,1,0:T(8,128)(2,1)} %w_down.3) | copy-start | bytes 22020100
  25.1 10.0 %collective-permute-start.4 = (bf16[32,7296]{1,0:T(8,128)(2,1)S(1)}, bf16[32,7296]{1,0:T(8,128)(2,1)S(1)}, u32[]{:S(2)}, u32[]{:S(2)}) collective-permute-start(bf16[32,7296]{1,0:T(8,128)(2,1)S(1)} %pad_maximum_fusion.1), channel_id=1, source_target_pairs={{0,16},{1,3},{2,18},{3,1},{4,20},{5,7},{6,22},{7,5},{8,24},{9,11},... | collective-permute-start | bytes 1400840 | tf_op jit(solution)/shard_map/ppermute | solution.py:115
  25.7 8.6 %collective-permute-start.7 = (bf16[16,7296]{1,0:T(8,128)(2,1)S(1)}, bf16[16,7296]{1,0:T(8,128)(2,1)S(1)}, u32[]{:S(2)}, u32[]{:S(2)}) collective-permute-start(bf16[16,7296]{1,0:T(8,128)(2,1)S(1)} %collective-permute-done.6.refs_0_), channel_id=1, source_target_pairs={{0,2},{1,17},{2,0},{3,19},{4,6},{5,21},{6,4},{7,23},{8,10},{9,25},... | collective-permute-start | bytes 700424 | tf_op jit(solution)/shard_map/ppermute | solution.py:115
  27.0 7.5 %collective-permute-start.12 = (bf16[16,7296]{1,0:T(8,128)(2,1)S(1)}, bf16[16,7296]{1,0:T(8,128)(2,1)S(1)}, u32[]{:S(2)}, u32[]{:S(2)}) collective-permute-start(bf16[16,7296]{1,0:T(8,128)(2,1)S(1)} %collective-permute-done.6.refs_0_), channel_id=1, source_target_pairs={{0,8},{1,9},{2,10},{3,11},{4,0},{5,1},{6,2},{7,3},{8,12},{9,13},{1... | collective-permute-start | bytes 700424 | tf_op jit(solution)/shard_map/ppermute | solution.py:115
  34.3 8.6 %collective-permute-start.11 = (bf16[32,7296]{1,0:T(8,128)(2,1)S(1)}, bf16[32,7296]{1,0:T(8,128)(2,1)S(1)}, u32[]{:S(2)}, u32[]{:S(2)}) collective-permute-start(bf16[32,7296]{1,0:T(8,128)(2,1)S(1)} %get-tuple-element.27.refs_0_), channel_id=1, source_target_pairs={{0,16},{1,3},{2,18},{3,1},{4,20},{5,7},{6,22},{7,5},{8,24},{9,11},... | collective-permute-start | bytes 1400840 | tf_op jit(solution)/shard_map/ppermute | solution.py:115
  34.5 6.7 %collective-permute-start.13 = (bf16[16,7296]{1,0:T(8,128)(2,1)S(1)}, bf16[16,7296]{1,0:T(8,128)(2,1)S(1)}, u32[]{:S(2)}, u32[]{:S(2)}) collective-permute-start(bf16[16,7296]{1,0:T(8,128)(2,1)S(1)} %collective-permute-done.12), channel_id=1, source_target_pairs={{0,2},{1,17},{2,0},{3,19},{4,6},{5,21},{6,4},{7,23},{8,10},{9,25},... | collective-permute-start | bytes 700424 | tf_op jit(solution)/shard_map/ppermute | solution.py:115
  35.1 8.2 %collective-permute-start.5 = (bf16[128,7296]{1,0:T(8,128)(2,1)S(1)}, bf16[128,7296]{1,0:T(8,128)(2,1)S(1)}, u32[]{:S(2)}, u32[]{:S(2)}) collective-permute-start(bf16[128,7296]{1,0:T(8,128)(2,1)S(1)} %constant_dynamic-update-slice_fusion.refs_0_), channel_id=1, source_target_pairs={{0,1},{1,0},{2,3},{3,2},{4,5},{5,4},{6,7},{7,6},{8,9},{9,8},{10,11... | collective-permute-start | bytes 5603336 | tf_op jit(solution)/shard_map/ppermute | solution.py:115
  41.2 9.6 %collective-permute-start.14 = (bf16[32,7296]{1,0:T(8,128)(2,1)S(1)}, bf16[32,7296]{1,0:T(8,128)(2,1)S(1)}, u32[]{:S(2)}, u32[]{:S(2)}) collective-permute-start(bf16[32,7296]{1,0:T(8,128)(2,1)S(1)} %constant_dynamic-update-slice_fusion.11.refs_1_), channel_id=1, source_target_pairs={{0,16},{1,3},{2,18},{3,1},{4,20},{5,7},{6,22},{7,5},{8,24},{9,11},... | collective-permute-start | bytes 1400840 | tf_op jit(solution)/shard_map/ppermute | solution.py:115
  42.7 12.0 %collective-permute-start.16 = (bf16[32,7296]{1,0:T(8,128)(2,1)S(1)}, bf16[32,7296]{1,0:T(8,128)(2,1)S(1)}, u32[]{:S(2)}, u32[]{:S(2)}) collective-permute-start(bf16[32,7296]{1,0:T(8,128)(2,1)S(1)} %constant_dynamic-update-slice_fusion.11.refs_1_), channel_id=1, source_target_pairs={{0,1},{1,0},{2,3},{3,2},{4,5},{5,4},{6,7},{7,6},{8,9},{9,8},{10,11... | collective-permute-start | bytes 1400840 | tf_op jit(solution)/shard_map/ppermute | solution.py:115
  43.0 11.8 %collective-permute-start.15 = (bf16[64,7296]{1,0:T(8,128)(2,1)S(1)}, bf16[64,7296]{1,0:T(8,128)(2,1)S(1)}, u32[]{:S(2)}, u32[]{:S(2)}) collective-permute-start(bf16[64,7296]{1,0:T(8,128)(2,1)S(1)} %constant_dynamic-update-slice_fusion.8.refs_0_), channel_id=1, source_target_pairs={{0,1},{1,0},{2,3},{3,2},{4,5},{5,4},{6,7},{7,6},{8,9},{9,8},{10,11... | collective-permute-start | bytes 2801672 | tf_op jit(solution)/shard_map/ppermute | solution.py:115
  49.3 35.7 %copy-start.6 = (bf16[32,7168]{1,0:T(8,128)(2,1)}, bf16[32,7168]{1,0:T(8,128)(2,1)S(1)}, u32[]{:S(2)}) copy-start(bf16[32,7168]{1,0:T(8,128)(2,1)S(1)} %get-tuple-element.14) | copy-start | bytes 1376260
  49.3 2.5 %collective-permute-start.18 = (bf16[64,7168]{1,0:T(8,128)(2,1)S(1)}, bf16[64,7168]{1,0:T(8,128)(2,1)S(1)}, u32[]{:S(2)}, u32[]{:S(2)}) collective-permute-start(bf16[64,7168]{1,0:T(8,128)(2,1)S(1)} %get-tuple-element.17), channel_id=1, source_target_pairs={{0,1},{1,0},{2,3},{3,2},{4,5},{5,4},{6,7},{7,6},{8,9},{9,8},{10,11... | collective-permute-start | bytes 2752520 | tf_op jit(solution)/shard_map/ppermute | solution.py:115
  50.9 3.9 %collective-permute-start.17 = (bf16[32,7296]{1,0:T(8,128)(2,1)S(1)}, bf16[32,7296]{1,0:T(8,128)(2,1)S(1)}, u32[]{:S(2)}, u32[]{:S(2)}) collective-permute-start(bf16[32,7296]{1,0:T(8,128)(2,1)S(1)} %broadcast_add_fusion), channel_id=1, source_target_pairs={{0,1},{1,0},{2,3},{3,2},{4,5},{5,4},{6,7},{7,6},{8,9},{9,8},{10,11... | collective-permute-start | bytes 1400840 | tf_op jit(solution)/shard_map/ppermute | solution.py:115
  51.2 2.9 %collective-permute-start.8 = (bf16[64,7168]{1,0:T(8,128)(2,1)S(1)}, bf16[64,7168]{1,0:T(8,128)(2,1)S(1)}, u32[]{:S(2)}, u32[]{:S(2)}) collective-permute-start(bf16[64,7168]{1,0:T(8,128)(2,1)S(1)} %get-tuple-element.15), channel_id=1, source_target_pairs={{0,1},{1,0},{2,3},{3,2},{4,5},{5,4},{6,7},{7,6},{8,9},{9,8},{10,11... | collective-permute-start | bytes 2752520 | tf_op jit(solution)/shard_map/ppermute | solution.py:115
  52.0 9.3 %collective-permute-start.25 = (bf16[32,7168]{1,0:T(8,128)(2,1)S(1)}, bf16[32,7168]{1,0:T(8,128)(2,1)S(1)}, u32[]{:S(2)}, u32[]{:S(2)}) collective-permute-start(bf16[32,7168]{1,0:T(8,128)(2,1)S(1)} %add_convert_fusion.2.refs_6_), channel_id=1, source_target_pairs={{0,16},{1,3},{2,18},{3,1},{4,20},{5,7},{6,22},{7,5},{8,24},{9,11},... | collective-permute-start | bytes 1376264 | tf_op jit(solution)/shard_map/ppermute | solution.py:115
  54.2 30.8 %collective-permute-start.9 = (bf16[32,7168]{1,0:T(8,128)(2,1)S(1)}, bf16[32,7168]{1,0:T(8,128)(2,1)S(1)}, u32[]{:S(2)}, u32[]{:S(2)}) collective-permute-start(bf16[32,7168]{1,0:T(8,128)(2,1)S(1)} %add_convert_fusion.3.refs_7_), channel_id=1, source_target_pairs={{0,16},{1,3},{2,18},{3,1},{4,20},{5,7},{6,22},{7,5},{8,24},{9,11},... | collective-permute-start | bytes 1376264 | tf_op jit(solution)/shard_map/ppermute | solution.py:115
  60.7 2.5 %collective-permute-start.20 = (bf16[64,7168]{1,0:T(8,128)(2,1)S(1)}, bf16[64,7168]{1,0:T(8,128)(2,1)S(1)}, u32[]{:S(2)}, u32[]{:S(2)}) collective-permute-start(bf16[64,7168]{1,0:T(8,128)(2,1)S(1)} %get-tuple-element.23), channel_id=1, source_target_pairs={{0,1},{1,0},{2,3},{3,2},{4,5},{5,4},{6,7},{7,6},{8,9},{9,8},{10,11... | collective-permute-start | bytes 2752520 | tf_op jit(solution)/shard_map/ppermute | solution.py:115
  60.8 13.8 %collective-permute-start.19 = (bf16[64,7168]{1,0:T(8,128)(2,1)S(1)}, bf16[64,7168]{1,0:T(8,128)(2,1)S(1)}, u32[]{:S(2)}, u32[]{:S(2)}) collective-permute-start(bf16[64,7168]{1,0:T(8,128)(2,1)S(1)} %get-tuple-element.20), channel_id=1, source_target_pairs={{0,1},{1,0},{2,3},{3,2},{4,5},{5,4},{6,7},{7,6},{8,9},{9,8},{10,11... | collective-permute-start | bytes 2752520 | tf_op jit(solution)/shard_map/ppermute | solution.py:115
  61.4 7.4 %collective-permute-start.26 = (bf16[16,7168]{1,0:T(8,128)(2,1)S(1)}, bf16[16,7168]{1,0:T(8,128)(2,1)S(1)}, u32[]{:S(2)}, u32[]{:S(2)}) collective-permute-start(bf16[16,7168]{1,0:T(8,128)(2,1)S(1)} %add_convert_fusion.8), channel_id=1, source_target_pairs={{0,2},{1,17},{2,0},{3,19},{4,6},{5,21},{6,4},{7,23},{8,10},{9,25},... | collective-permute-start | bytes 688136 | tf_op jit(solution)/shard_map/ppermute | solution.py:115
  63.4 9.4 %collective-permute-start.21 = (bf16[32,7168]{1,0:T(8,128)(2,1)S(1)}, bf16[32,7168]{1,0:T(8,128)(2,1)S(1)}, u32[]{:S(2)}, u32[]{:S(2)}) collective-permute-start(bf16[32,7168]{1,0:T(8,128)(2,1)S(1)} %add_convert_fusion), channel_id=1, source_target_pairs={{0,16},{1,3},{2,18},{3,1},{4,20},{5,7},{6,22},{7,5},{8,24},{9,11},... | collective-permute-start | bytes 1376264 | tf_op jit(solution)/shard_map/ppermute | solution.py:115
  68.9 7.6 %collective-permute-start.27 = (bf16[16,7168]{1,0:T(8,128)(2,1)S(1)}, bf16[16,7168]{1,0:T(8,128)(2,1)S(1)}, u32[]{:S(2)}, u32[]{:S(2)}) collective-permute-start(bf16[16,7168]{1,0:T(8,128)(2,1)S(1)} %add_convert_fusion.7), channel_id=1, source_target_pairs={{0,8},{1,9},{2,10},{3,11},{4,0},{5,1},{6,2},{7,3},{8,12},{9,13},{1... | collective-permute-start | bytes 688136 | tf_op jit(solution)/shard_map/ppermute | solution.py:115
  72.9 7.5 %collective-permute-start.24 = (bf16[16,7168]{1,0:T(8,128)(2,1)S(1)}, bf16[16,7168]{1,0:T(8,128)(2,1)S(1)}, u32[]{:S(2)}, u32[]{:S(2)}) collective-permute-start(bf16[16,7168]{1,0:T(8,128)(2,1)S(1)} %add_convert_fusion.9), channel_id=1, source_target_pairs={{0,2},{1,17},{2,0},{3,19},{4,6},{5,21},{6,4},{7,23},{8,10},{9,25},... | collective-permute-start | bytes 688136 | tf_op jit(solution)/shard_map/ppermute | solution.py:115
  74.8 8.5 %collective-permute-start.22 = (bf16[32,7168]{1,0:T(8,128)(2,1)S(1)}, bf16[32,7168]{1,0:T(8,128)(2,1)S(1)}, u32[]{:S(2)}, u32[]{:S(2)}) collective-permute-start(bf16[32,7168]{1,0:T(8,128)(2,1)S(1)} %fusion.9), channel_id=1, source_target_pairs={{0,16},{1,3},{2,18},{3,1},{4,20},{5,7},{6,22},{7,5},{8,24},{9,11},... | collective-permute-start | bytes 1376264 | tf_op jit(solution)/shard_map/ppermute | solution.py:115
  80.5 6.1 %collective-permute-start.28 = (bf16[16,7168]{1,0:T(8,128)(2,1)S(1)}, bf16[16,7168]{1,0:T(8,128)(2,1)S(1)}, u32[]{:S(2)}, u32[]{:S(2)}) collective-permute-start(bf16[16,7168]{1,0:T(8,128)(2,1)S(1)} %add_convert_fusion.6), channel_id=1, source_target_pairs={{0,8},{1,9},{2,10},{3,11},{4,0},{5,1},{6,2},{7,3},{8,12},{9,13},{1... | collective-permute-start | bytes 688136 | tf_op jit(solution)/shard_map/ppermute | solution.py:115
  83.4 6.1 %collective-permute-start.23 = (bf16[16,7168]{1,0:T(8,128)(2,1)S(1)}, bf16[16,7168]{1,0:T(8,128)(2,1)S(1)}, u32[]{:S(2)}, u32[]{:S(2)}) collective-permute-start(bf16[16,7168]{1,0:T(8,128)(2,1)S(1)} %add_convert_fusion.10), channel_id=1, source_target_pairs={{0,2},{1,17},{2,0},{3,19},{4,6},{5,21},{6,4},{7,23},{8,10},{9,25},... | collective-permute-start | bytes 688136 | tf_op jit(solution)/shard_map/ppermute | solution.py:115
  85.1 11.6 %collective-permute-start.10 = (bf16[16,7168]{1,0:T(8,128)(2,1)S(1)}, bf16[16,7168]{1,0:T(8,128)(2,1)}, u32[]{:S(2)}, u32[]{:S(2)}) collective-permute-start(bf16[16,7168]{1,0:T(8,128)(2,1)S(1)} %add_convert_fusion.11), channel_id=1, source_target_pairs={{0,2},{1,17},{2,0},{3,19},{4,6},{5,21},{6,4},{7,23},{8,10},{9,25},... | collective-permute-start | bytes 688136 | tf_op jit(solution)/shard_map/ppermute | solution.py:115
  90.3 7.4 %collective-permute-start.29 = (bf16[16,7168]{1,0:T(8,128)(2,1)}, bf16[16,7168]{1,0:T(8,128)(2,1)}, u32[]{:S(2)}, u32[]{:S(2)}) collective-permute-start(bf16[16,7168]{1,0:T(8,128)(2,1)} %add_convert_fusion.5), channel_id=1, source_target_pairs={{0,8},{1,9},{2,10},{3,11},{4,0},{5,1},{6,2},{7,3},{8,12},{9,13},{1... | collective-permute-start | bytes 688136 | tf_op jit(solution)/shard_map/ppermute | solution.py:115
  (8 other events, 50.8 us)

commit v6 on v5

--- a/solution.py
+++ b/solution.py
@@ -181,6 +181,52 @@
         out_shape=jax.ShapeDtypeStruct((rows, width + tail), jnp.bfloat16),
         name="pack",
     )(expert_ids.T, gate_coef.T, hidden_in)
+
+
+def attend_kernel(lengths, q, kv, *refs):
+    out = refs[-1]
+    rows, heads, _ = q.shape
+    slots = kv.shape[2]
+    base = pl.program_id(0) * rows
+    position = lax.broadcasted_iota(jnp.int32, (heads, slots), 1)
+    scores = []
+    for r in range(rows):
+        s = jnp.dot(q[r], kv[r], preferred_element_type=jnp.float32) * score_scale
+        scores.append(jnp.where(position < lengths[base + r], s, -1e30))
+    scores = jnp.concatenate(scores, axis=0)
+    exponent = jnp.exp(scores - jnp.max(scores, axis=1, keepdims=True))
+    weights = exponent / jnp.sum(exponent, axis=1, keepdims=True)
+    weights = weights.astype(jnp.bfloat16)
+    for r in range(rows):
+        out[r] = lax.dot_general(
+            weights[r * heads : (r + 1) * heads],
+            kv[r, : out.shape[2]],
+            (((1,), (1,)), ((), ())),
+            preferred_element_type=jnp.float32,
+        ).astype(jnp.bfloat16)
+
+
+def attend_rows(query_lat, kv_cache, cache_len, *after):
+    rows, heads, width = query_lat.shape
+    slots = kv_cache.shape[1]
+    step = max(s for s in (8, 1) if rows % s == 0)
+    return pl.pallas_call(
+        attend_kernel,
+        grid=(rows // step,),
+        in_specs=[
+            SCALARS,
+            pl.BlockSpec((step, heads, width), lambda i: (i, 0, 0)),
+            pl.BlockSpec((step, width, slots), lambda i: (i, 0, 0)),
+        ]
+        + [ANYWHERE] * len(after),
+        out_specs=pl.BlockSpec((step, heads, LAT), lambda i: (i, 0, 0)),
+        out_shape=jax.ShapeDtypeStruct((rows, heads, LAT), jnp.bfloat16),
+        compiler_params=pltpu.CompilerParams(vmem_limit_bytes=40 * 2**20),
+        cost_estimate=pl.CostEstimate(
+            flops=20 * rows * heads * slots * (width + LAT), bytes_accessed=1, transcendentals=0
+        ),
+        name="attend",
+    )(cache_len, query_lat, jnp.swapaxes(kv_cache, 1, 2), *after)
 
 
 def hold_kernel(weight, *refs):
@@ -324,9 +370,10 @@
         routed_out = routed_sparse(
             hidden_in, expert_ids, gate_coef, *weights, half_rows, capacity
         )
+        attention = attend(query_lat, kv_cache, cache_len)
     else:
         routed_out = routed_dense(hidden_in, expert_ids, gate_coef, *weights)
-    attention = attend(query_lat, kv_cache, cache_len)
+        attention = attend_rows(query_lat, kv_cache, cache_len)
     return (attention, routed_out)
 
 

time: 100 us -> 96.5 us (0.965)
  starting transfers between devices: 29.9 us -> 41.9 us
  matrix products: 7.91 us -> 0 us
  local copies, waits for them, and re-layouts: 12.7 us -> 5.42 us
  other arithmetic: 7.26 us -> 3.14 us
  Pallas kernels: 13.8 us -> 16.8 us
    ppermute x30, starting transfers between devices: 29.9 us -> 41.9 us  [permutation(): return lambda a: lax.ppermute(a, AXES, pairs)]
    dot_general x2 -> x0, matrix products: 7.91 us -> none  [the longest x1 4.82 us: attend(): jnp.einsum('rhl,rlc->rhc', weights, kv_cache[:, :, :LAT], preferred_eleme...]
    unnamed x28 -> x26, local copies, waits for them, and re-layouts: 11.5 us -> 4.3 us
    pallas_call x0 -> x1, Pallas kernels: none -> 3.15 us  [attend_rows(): pl.pallas_call(attend_kernel, grid=(rows // step,), in_specs=[SCALARS, pl...]
    convert_element_type x11, other arithmetic: 3.64 us -> 1.94 us  [plus(): return total.astype(jnp.bfloat16)]
    sub x1 -> x0, other arithmetic: 1.58 us -> none  [attend(): exponent = jnp.exp(scores - top_score)]
  transfers between devices with their start and end apart: 30 -> 30, of which waited for: 15 -> 14; matrix products, arithmetic and copies ran while one was open for 17% -> 5% of each run, Pallas kernels for 12% -> 16%
where the time goes in v6:
time: 96.5 us; the launch traced here: 96.3 us
  starting transfers between devices  41.9 us (43%)
  waiting for transfers between devices  26.7 us (28%)
  Pallas kernels  16.8 us (17%)
  local copies, waits for them, and re-layouts  5.42 us (6%)
  other arithmetic  3.14 us (3%)
  between operations  2.21 us (2%)
    ppermute x30, starting transfers between devices, permutation(): return lambda a: lax.ppermute(a, AXES, pairs)  41.9 us
    ppermute x30, waiting for transfers between devices, permutation(): return lambda a: lax.ppermute(a, AXES, pairs)  26.7 us
    pallas_call x2, Pallas kernels, expert_group(): pl.pallas_call(functools.partial(expert_kernel, sizes, outs, n_experts, s...  11.9 us
    unnamed x26, local copies, waits for them, and re-layouts  4.3 us
    pallas_call x1, Pallas kernels, attend_rows(): pl.pallas_call(attend_kernel, grid=(rows // step,), in_specs=[SCALARS, pl...  3.15 us
    convert_element_type x11, other arithmetic, plus(): return total.astype(jnp.bfloat16)  1.94 us
  transfers between devices with their start and end apart: 30, of which 14 were waited for; matrix products, arithmetic and copies ran while one was open for 5% of the time, Pallas kernels for 16%

profile of v6, /device:TPU:0, one launch (start us, length us, event | category | flops | bytes accessed | tf_op | source)
XLA Modules:
  0.0 96.3 jit_solution(382684701856433175)
XLA Ops:
  0.6 1.8 %pack.1 = bf16[16,7296]{1,0:T(8,128)(2,1)} custom-call(s32[8,16]{1,0:T(8,128)} %bitcast.11, f32[8,16]{1,0:T(8,128)} %bitcast.12, bf16[16,7168]{1,0:T(8,128)(2,1)} %x.1), custom_call_target="tpu_custom_call" | custom-call | tf_op jit(solution)/shard_map/pack/pallas_call | solution.py:177
  2.4 2.9 %collective-permute-start = (bf16[16,7296]{1,0:T(8,128)(2,1)}, bf16[16,7296]{1,0:T(8,128)(2,1)S(1)}, u32[]{:S(2)}, u32[]{:S(2)}) collective-permute-start(bf16[16,7296]{1,0:T(8,128)(2,1)} %pack.1), channel_id=1, source_target_pairs={{0,2},{1,17},{2,0},{3,19},{4,6},{5,21},{6,4},{7,23},{8,10},{9,25},... | collective-permute-start | bytes 700424 | tf_op jit(solution)/shard_map/ppermute | solution.py:115
  5.4 2.6 %collective-permute-start.2 = (bf16[16,7296]{1,0:T(8,128)(2,1)}, bf16[16,7296]{1,0:T(8,128)(2,1)S(1)}, u32[]{:S(2)}, u32[]{:S(2)}) collective-permute-start(bf16[16,7296]{1,0:T(8,128)(2,1)} %pack.1), channel_id=1, source_target_pairs={{0,8},{1,9},{2,10},{3,11},{4,0},{5,1},{6,2},{7,3},{8,12},{9,13},{1... | collective-permute-start | bytes 700424 | tf_op jit(solution)/shard_map/ppermute | solution.py:115
  8.0 1.0 %constant_dynamic-update-slice_fusion.5 = bf16[128,7296]{1,0:T(8,128)(2,1)S(1)} fusion(bf16[16,7296]{1,0:T(8,128)(2,1)} %pack.1), kind=kLoop, calls=%fused_computation.21 | loop fusion | bytes 466944
  9.6 1.0 %pad_maximum_fusion = bf16[32,7296]{1,0:T(8,128)(2,1)S(1)} fusion(bf16[16,7296]{1,0:T(8,128)(2,1)S(1)} %collective-permute-done, bf16[16,7296]{1,0:T(8,128)(2,1)} %pack.1), kind=kLoop, calls=%fused_computation.4 | loop fusion | flops 933888 | bytes 933888 | tf_op jit(solution)/shard_map/concatenate | solution.py:319
  10.6 2.1 %collective-permute-start.1 = (bf16[32,7296]{1,0:T(8,128)(2,1)S(1)}, bf16[32,7296]{1,0:T(8,128)(2,1)S(1)}, u32[]{:S(2)}, u32[]{:S(2)}) collective-permute-start(bf16[32,7296]{1,0:T(8,128)(2,1)S(1)} %pad_maximum_fusion), channel_id=1, source_target_pairs={{0,16},{1,3},{2,18},{3,1},{4,20},{5,7},{6,22},{7,5},{8,24},{9,11},... | collective-permute-start | bytes 1400840 | tf_op jit(solution)/shard_map/ppermute | solution.py:115
  13.0 1.5 %collective-permute-start.3 = (bf16[16,7296]{1,0:T(8,128)(2,1)S(1)}, bf16[16,7296]{1,0:T(8,128)(2,1)S(1)}, u32[]{:S(2)}, u32[]{:S(2)}) collective-permute-start(bf16[16,7296]{1,0:T(8,128)(2,1)S(1)} %collective-permute-done.2.refs_0_), channel_id=1, source_target_pairs={{0,2},{1,17},{2,0},{3,19},{4,6},{5,21},{6,4},{7,23},{8,10},{9,25},... | collective-permute-start | bytes 700424 | tf_op jit(solution)/shard_map/ppermute | solution.py:115
  14.5 3.3 %collective-permute-start.6 = (bf16[16,7296]{1,0:T(8,128)(2,1)S(1)}, bf16[16,7296]{1,0:T(8,128)(2,1)S(1)}, u32[]{:S(2)}, u32[]{:S(2)}) collective-permute-start(bf16[16,7296]{1,0:T(8,128)(2,1)S(1)} %collective-permute-done.2.refs_0_), channel_id=1, source_target_pairs={{0,8},{1,9},{2,10},{3,11},{4,0},{5,1},{6,2},{7,3},{8,12},{9,13},{1... | collective-permute-start | bytes 700424 | tf_op jit(solution)/shard_map/ppermute | solution.py:115
  17.8 3.1 %copy-done = bf16[1,7168,512]{2,1,0:T(8,128)(2,1)S(1)} copy-done((bf16[1,7168,512]{2,1,0:T(8,128)(2,1)S(1)}, bf16[1,7168,512]{2,1,0:T(8,128)(2,1)}, u32[]{:S(2)}) %copy-start) | copy-done | bytes 7340056
  20.9 1.0 %collective-permute-start.4 = (bf16[32,7296]{1,0:T(8,128)(2,1)S(1)}, bf16[32,7296]{1,0:T(8,128)(2,1)S(1)}, u32[]{:S(2)}, u32[]{:S(2)}) collective-permute-start(bf16[32,7296]{1,0:T(8,128)(2,1)S(1)} %pad_maximum_fusion.1), channel_id=1, source_target_pairs={{0,16},{1,3},{2,18},{3,1},{4,20},{5,7},{6,22},{7,5},{8,24},{9,11},... | collective-permute-start | bytes 1400840 | tf_op jit(solution)/shard_map/ppermute | solution.py:115
  21.9 1.5 %collective-permute-start.7 = (bf16[16,7296]{1,0:T(8,128)(2,1)S(1)}, bf16[16,7296]{1,0:T(8,128)(2,1)S(1)}, u32[]{:S(2)}, u32[]{:S(2)}) collective-permute-start(bf16[16,7296]{1,0:T(8,128)(2,1)S(1)} %collective-permute-done.6.refs_0_), channel_id=1, source_target_pairs={{0,2},{1,17},{2,0},{3,19},{4,6},{5,21},{6,4},{7,23},{8,10},{9,25},... | collective-permute-start | bytes 700424 | tf_op jit(solution)/shard_map/ppermute | solution.py:115
  23.4 2.7 %collective-permute-start.12 = (bf16[16,7296]{1,0:T(8,128)(2,1)S(1)}, bf16[16,7296]{1,0:T(8,128)(2,1)S(1)}, u32[]{:S(2)}, u32[]{:S(2)}) collective-permute-start(bf16[16,7296]{1,0:T(8,128)(2,1)S(1)} %collective-permute-done.6.refs_0_), channel_id=1, source_target_pairs={{0,8},{1,9},{2,10},{3,11},{4,0},{5,1},{6,2},{7,3},{8,12},{9,13},{1... | collective-permute-start | bytes 700424 | tf_op jit(solution)/shard_map/ppermute | solution.py:115
  26.1 4.4 %collective-permute-done.7 = bf16[16,7296]{1,0:T(8,128)(2,1)S(1)} collective-permute-done((bf16[16,7296]{1,0:T(8,128)(2,1)S(1)}, bf16[16,7296]{1,0:T(8,128)(2,1)S(1)}, u32[]{:S(2)}, u32[]{:S(2)}) %collective-permute-start.7) | collective-permute-done | bytes 233504 | tf_op jit(solution)/shard_map/ppermute | solution.py:115
  30.7 1.8 %collective-permute-start.13 = (bf16[16,7296]{1,0:T(8,128)(2,1)S(1)}, bf16[16,7296]{1,0:T(8,128)(2,1)S(1)}, u32[]{:S(2)}, u32[]{:S(2)}) collective-permute-start(bf16[16,7296]{1,0:T(8,128)(2,1)S(1)} %collective-permute-done.12), channel_id=1, source_target_pairs={{0,2},{1,17},{2,0},{3,19},{4,6},{5,21},{6,4},{7,23},{8,10},{9,25},... | collective-permute-start | bytes 700424 | tf_op jit(solution)/shard_map/ppermute | solution.py:115
  32.8 6.7 %collective-permute-done.13 = bf16[16,7296]{1,0:T(8,128)(2,1)S(1)} collective-permute-done((bf16[16,7296]{1,0:T(8,128)(2,1)S(1)}, bf16[16,7296]{1,0:T(8,128)(2,1)S(1)}, u32[]{:S(2)}, u32[]{:S(2)}) %collective-permute-start.13) | collective-permute-done | bytes 233504 | tf_op jit(solution)/shard_map/ppermute | solution.py:115
  40.6 5.9 %experts.2 = (bf16[32,7168]{1,0:T(8,128)(2,1)S(1)}, bf16[32,7168]{1,0:T(8,128)(2,1)S(1)}, bf16[32,7168]{1,0:T(8,128)(2,1)S(1)}, bf16[32,7168]{1,0:T(8,128)(2,1)S...) custom-call(s32[1]{0:T(128)} %bitcast.1.me, bf16[1,7168,512]{2,1,0:T(8,128)(2,1)S(1)} %bitcast.7, ...), custom_call_target="tpu_custom_call" | custom-call | flops 5637144576 | bytes 1 | tf_op jit(solution)/shard_map/experts/pallas_call | solution.py:292
  49.2 1.6 %collective-permute-start.25 = (bf16[32,7168]{1,0:T(8,128)(2,1)S(1)}, bf16[32,7168]{1,0:T(8,128)(2,1)S(1)}, u32[]{:S(2)}, u32[]{:S(2)}) collective-permute-start(bf16[32,7168]{1,0:T(8,128)(2,1)S(1)} %add_convert_fusion.2.refs_6_), channel_id=1, source_target_pairs={{0,16},{1,3},{2,18},{3,1},{4,20},{5,7},{6,22},{7,5},{8,24},{9,11},... | collective-permute-start | bytes 1376264 | tf_op jit(solution)/shard_map/ppermute | solution.py:115
  51.5 1.5 %collective-permute-start.9 = (bf16[32,7168]{1,0:T(8,128)(2,1)S(1)}, bf16[32,7168]{1,0:T(8,128)(2,1)S(1)}, u32[]{:S(2)}, u32[]{:S(2)}) collective-permute-start(bf16[32,7168]{1,0:T(8,128)(2,1)S(1)} %add_convert_fusion.3.refs_7_), channel_id=1, source_target_pairs={{0,16},{1,3},{2,18},{3,1},{4,20},{5,7},{6,22},{7,5},{8,24},{9,11},... | collective-permute-start | bytes 1376264 | tf_op jit(solution)/shard_map/ppermute | solution.py:115
  53.0 5.9 %experts.3 = (bf16[32,7168]{1,0:T(8,128)(2,1)S(1)}, bf16[32,7168]{1,0:T(8,128)(2,1)S(1)}, bf16[32,7168]{1,0:T(8,128)(2,1)S(1)}, bf16[32,7168]{1,0:T(8,128)(2,1)S...) custom-call(s32[1]{0:T(128)} %bitcast.1.me, bf16[1,7168,512]{2,1,0:T(8,128)(2,1)S(1)} %bitcast.7, ...), custom_call_target="tpu_custom_call" | custom-call | flops 5637144576 | bytes 1 | tf_op jit(solution)/shard_map/experts/pallas_call | solution.py:292
  59.6 0.8 collective-permute-start.26
  60.4 1.0 %collective-permute-done.20 = bf16[64,7168]{1,0:T(8,128)(2,1)S(1)} collective-permute-done((bf16[64,7168]{1,0:T(8,128)(2,1)S(1)}, bf16[64,7168]{1,0:T(8,128)(2,1)S(1)}, u32[]{:S(2)}, u32[]{:S(2)}) %collective-permute-start.20) | collective-permute-done | bytes 917536 | tf_op jit(solution)/shard_map/ppermute | solution.py:115
  62.3 4.5 %collective-permute-done.26 = bf16[16,7168]{1,0:T(8,128)(2,1)S(1)} collective-permute-done((bf16[16,7168]{1,0:T(8,128)(2,1)S(1)}, bf16[16,7168]{1,0:T(8,128)(2,1)S(1)}, u32[]{:S(2)}, u32[]{:S(2)}) %collective-permute-start.26) | collective-permute-done | bytes 229408 | tf_op jit(solution)/shard_map/ppermute | solution.py:115
  66.9 3.3 %collective-permute-start.27 = (bf16[16,7168]{1,0:T(8,128)(2,1)S(1)}, bf16[16,7168]{1,0:T(8,128)(2,1)S(1)}, u32[]{:S(2)}, u32[]{:S(2)}) collective-permute-start(bf16[16,7168]{1,0:T(8,128)(2,1)S(1)} %add_convert_fusion.7), channel_id=1, source_target_pairs={{0,8},{1,9},{2,10},{3,11},{4,0},{5,1},{6,2},{7,3},{8,12},{9,13},{1... | collective-permute-start | bytes 688136 | tf_op jit(solution)/shard_map/ppermute | solution.py:115
  70.4 1.6 %collective-permute-start.24 = (bf16[16,7168]{1,0:T(8,128)(2,1)S(1)}, bf16[16,7168]{1,0:T(8,128)(2,1)S(1)}, u32[]{:S(2)}, u32[]{:S(2)}) collective-permute-start(bf16[16,7168]{1,0:T(8,128)(2,1)S(1)} %add_convert_fusion.9), channel_id=1, source_target_pairs={{0,2},{1,17},{2,0},{3,19},{4,6},{5,21},{6,4},{7,23},{8,10},{9,25},... | collective-permute-start | bytes 688136 | tf_op jit(solution)/shard_map/ppermute | solution.py:115
  73.3 1.3 %collective-permute-start.22 = (bf16[32,7168]{1,0:T(8,128)(2,1)S(1)}, bf16[32,7168]{1,0:T(8,128)(2,1)S(1)}, u32[]{:S(2)}, u32[]{:S(2)}) collective-permute-start(bf16[32,7168]{1,0:T(8,128)(2,1)S(1)} %fusion), channel_id=1, source_target_pairs={{0,16},{1,3},{2,18},{3,1},{4,20},{5,7},{6,22},{7,5},{8,24},{9,11},... | collective-permute-start | bytes 1376264 | tf_op jit(solution)/shard_map/ppermute | solution.py:115
  74.6 3.2 %collective-permute-done.24 = bf16[16,7168]{1,0:T(8,128)(2,1)S(1)} collective-permute-done((bf16[16,7168]{1,0:T(8,128)(2,1)S(1)}, bf16[16,7168]{1,0:T(8,128)(2,1)S(1)}, u32[]{:S(2)}, u32[]{:S(2)}) %collective-permute-start.24) | collective-permute-done | bytes 229408 | tf_op jit(solution)/shard_map/ppermute | solution.py:115
  77.9 3.3 %collective-permute-start.28 = (bf16[16,7168]{1,0:T(8,128)(2,1)S(1)}, bf16[16,7168]{1,0:T(8,128)(2,1)S(1)}, u32[]{:S(2)}, u32[]{:S(2)}) collective-permute-start(bf16[16,7168]{1,0:T(8,128)(2,1)S(1)} %add_convert_fusion.6), channel_id=1, source_target_pairs={{0,8},{1,9},{2,10},{3,11},{4,0},{5,1},{6,2},{7,3},{8,12},{9,13},{1... | collective-permute-start | bytes 688136 | tf_op jit(solution)/shard_map/ppermute | solution.py:115
  81.9 1.5 %collective-permute-start.23 = (bf16[16,7168]{1,0:T(8,128)(2,1)S(1)}, bf16[16,7168]{1,0:T(8,128)(2,1)S(1)}, u32[]{:S(2)}, u32[]{:S(2)}) collective-permute-start(bf16[16,7168]{1,0:T(8,128)(2,1)S(1)} %add_convert_fusion.10), channel_id=1, source_target_pairs={{0,2},{1,17},{2,0},{3,19},{4,6},{5,21},{6,4},{7,23},{8,10},{9,25},... | collective-permute-start | bytes 688136 | tf_op jit(solution)/shard_map/ppermute | solution.py:115
  84.8 3.3 %collective-permute-done.23 = bf16[16,7168]{1,0:T(8,128)(2,1)S(1)} collective-permute-done((bf16[16,7168]{1,0:T(8,128)(2,1)S(1)}, bf16[16,7168]{1,0:T(8,128)(2,1)S(1)}, u32[]{:S(2)}, u32[]{:S(2)}) %collective-permute-start.23) | collective-permute-done | bytes 229408 | tf_op jit(solution)/shard_map/ppermute | solution.py:115
  88.2 3.7 %collective-permute-start.29 = (bf16[16,7168]{1,0:T(8,128)(2,1)S(1)}, bf16[16,7168]{1,0:T(8,128)(2,1)S(1)}, u32[]{:S(2)}, u32[]{:S(2)}) collective-permute-start(bf16[16,7168]{1,0:T(8,128)(2,1)S(1)} %add_convert_fusion.5), channel_id=1, source_target_pairs={{0,8},{1,9},{2,10},{3,11},{4,0},{5,1},{6,2},{7,3},{8,12},{9,13},{1... | collective-permute-start | bytes 688136 | tf_op jit(solution)/shard_map/ppermute | solution.py:115
  91.8 3.2 %attend.1 = bf16[16,64,512]{2,1,0:T(8,128)(2,1)} custom-call(s32[16]{0:T(128)S(1)} %copy-done.4, bf16[16,64,576]{2,1,0:T(8,128)(2,1)S(1)} %copy-done.3, bf16[16,576,128]{2,1,0:T(8,128)(2,1)S(1)} %bitcast.10), custom_call_target="tpu_custom_call" | custom-call | flops 2852126720 | bytes 1 | tf_op jit(solution)/shard_map/attend/pallas_call | solution.py:213
  95.4 0.8 add_convert_fusion.4
  (83 shorter events, 10.4 us)
Async XLA Ops:
  2.4 7.2 %collective-permute-start = (bf16[16,7296]{1,0:T(8,128)(2,1)}, bf16[16,7296]{1,0:T(8,128)(2,1)S(1)}, u32[]{:S(2)}, u32[]{:S(2)}) collective-permute-start(bf16[16,7296]{1,0:T(8,128)(2,1)} %pack.1), channel_id=1, source_target_pairs={{0,2},{1,17},{2,0},{3,19},{4,6},{5,21},{6,4},{7,23},{8,10},{9,25},... | collective-permute-start | bytes 700424 | tf_op jit(solution)/shard_map/ppermute | solution.py:115
  5.4 7.6 %collective-permute-start.2 = (bf16[16,7296]{1,0:T(8,128)(2,1)}, bf16[16,7296]{1,0:T(8,128)(2,1)S(1)}, u32[]{:S(2)}, u32[]{:S(2)}) collective-permute-start(bf16[16,7296]{1,0:T(8,128)(2,1)} %pack.1), channel_id=1, source_target_pairs={{0,8},{1,9},{2,10},{3,11},{4,0},{5,1},{6,2},{7,3},{8,12},{9,13},{1... | collective-permute-start | bytes 700424 | tf_op jit(solution)/shard_map/ppermute | solution.py:115
  10.6 20.1 %collective-permute-start.1 = (bf16[32,7296]{1,0:T(8,128)(2,1)S(1)}, bf16[32,7296]{1,0:T(8,128)(2,1)S(1)}, u32[]{:S(2)}, u32[]{:S(2)}) collective-permute-start(bf16[32,7296]{1,0:T(8,128)(2,1)S(1)} %pad_maximum_fusion), channel_id=1, source_target_pairs={{0,16},{1,3},{2,18},{3,1},{4,20},{5,7},{6,22},{7,5},{8,24},{9,11},... | collective-permute-start | bytes 1400840 | tf_op jit(solution)/shard_map/ppermute | solution.py:115
  13.0 7.9 %collective-permute-start.3 = (bf16[16,7296]{1,0:T(8,128)(2,1)S(1)}, bf16[16,7296]{1,0:T(8,128)(2,1)S(1)}, u32[]{:S(2)}, u32[]{:S(2)}) collective-permute-start(bf16[16,7296]{1,0:T(8,128)(2,1)S(1)} %collective-permute-done.2.refs_0_), channel_id=1, source_target_pairs={{0,2},{1,17},{2,0},{3,19},{4,6},{5,21},{6,4},{7,23},{8,10},{9,25},... | collective-permute-start | bytes 700424 | tf_op jit(solution)/shard_map/ppermute | solution.py:115
  14.5 7.4 %collective-permute-start.6 = (bf16[16,7296]{1,0:T(8,128)(2,1)S(1)}, bf16[16,7296]{1,0:T(8,128)(2,1)S(1)}, u32[]{:S(2)}, u32[]{:S(2)}) collective-permute-start(bf16[16,7296]{1,0:T(8,128)(2,1)S(1)} %collective-permute-done.2.refs_0_), channel_id=1, source_target_pairs={{0,8},{1,9},{2,10},{3,11},{4,0},{5,1},{6,2},{7,3},{8,12},{9,13},{1... | collective-permute-start | bytes 700424 | tf_op jit(solution)/shard_map/ppermute | solution.py:115
  20.9 11.7 %collective-permute-start.4 = (bf16[32,7296]{1,0:T(8,128)(2,1)S(1)}, bf16[32,7296]{1,0:T(8,128)(2,1)S(1)}, u32[]{:S(2)}, u32[]{:S(2)}) collective-permute-start(bf16[32,7296]{1,0:T(8,128)(2,1)S(1)} %pad_maximum_fusion.1), channel_id=1, source_target_pairs={{0,16},{1,3},{2,18},{3,1},{4,20},{5,7},{6,22},{7,5},{8,24},{9,11},... | collective-permute-start | bytes 1400840 | tf_op jit(solution)/shard_map/ppermute | solution.py:115
  21.9 8.6 %collective-permute-start.7 = (bf16[16,7296]{1,0:T(8,128)(2,1)S(1)}, bf16[16,7296]{1,0:T(8,128)(2,1)S(1)}, u32[]{:S(2)}, u32[]{:S(2)}) collective-permute-start(bf16[16,7296]{1,0:T(8,128)(2,1)S(1)} %collective-permute-done.6.refs_0_), channel_id=1, source_target_pairs={{0,2},{1,17},{2,0},{3,19},{4,6},{5,21},{6,4},{7,23},{8,10},{9,25},... | collective-permute-start | bytes 700424 | tf_op jit(solution)/shard_map/ppermute | solution.py:115
  23.4 7.3 %collective-permute-start.12 = (bf16[16,7296]{1,0:T(8,128)(2,1)S(1)}, bf16[16,7296]{1,0:T(8,128)(2,1)S(1)}, u32[]{:S(2)}, u32[]{:S(2)}) collective-permute-start(bf16[16,7296]{1,0:T(8,128)(2,1)S(1)} %collective-permute-done.6.refs_0_), channel_id=1, source_target_pairs={{0,8},{1,9},{2,10},{3,11},{4,0},{5,1},{6,2},{7,3},{8,12},{9,13},{1... | collective-permute-start | bytes 700424 | tf_op jit(solution)/shard_map/ppermute | solution.py:115
  26.1 14.5 %slice-start = ((s8[7340032]{0:T(1024)(128)(4,1)}), s8[4194304]{0:T(1024)(128)(4,1)S(1)}, s32[]{:S(2)}) async-start(s8[7340032]{0:T(1024)(128)(4,1)} %bitcast.6), calls=%async_computation | async-start | bytes 8388608
  30.5 9.5 %collective-permute-start.11 = (bf16[32,7296]{1,0:T(8,128)(2,1)S(1)}, bf16[32,7296]{1,0:T(8,128)(2,1)S(1)}, u32[]{:S(2)}, u32[]{:S(2)}) collective-permute-start(bf16[32,7296]{1,0:T(8,128)(2,1)S(1)} %get-tuple-element.27.refs_0_), channel_id=1, source_target_pairs={{0,16},{1,3},{2,18},{3,1},{4,20},{5,7},{6,22},{7,5},{8,24},{9,11},... | collective-permute-start | bytes 1400840 | tf_op jit(solution)/shard_map/ppermute | solution.py:115
  30.7 8.7 %collective-permute-start.13 = (bf16[16,7296]{1,0:T(8,128)(2,1)S(1)}, bf16[16,7296]{1,0:T(8,128)(2,1)S(1)}, u32[]{:S(2)}, u32[]{:S(2)}) collective-permute-start(bf16[16,7296]{1,0:T(8,128)(2,1)S(1)} %collective-permute-done.12), channel_id=1, source_target_pairs={{0,2},{1,17},{2,0},{3,19},{4,6},{5,21},{6,4},{7,23},{8,10},{9,25},... | collective-permute-start | bytes 700424 | tf_op jit(solution)/shard_map/ppermute | solution.py:115
  32.6 8.0 %collective-permute-start.5 = (bf16[128,7296]{1,0:T(8,128)(2,1)S(1)}, bf16[128,7296]{1,0:T(8,128)(2,1)S(1)}, u32[]{:S(2)}, u32[]{:S(2)}) collective-permute-start(bf16[128,7296]{1,0:T(8,128)(2,1)S(1)} %constant_dynamic-update-slice_fusion.refs_0_), channel_id=1, source_target_pairs={{0,1},{1,0},{2,3},{3,2},{4,5},{5,4},{6,7},{7,6},{8,9},{9,8},{10,11... | collective-permute-start | bytes 5603336 | tf_op jit(solution)/shard_map/ppermute | solution.py:115
  39.5 8.6 %collective-permute-start.14 = (bf16[32,7296]{1,0:T(8,128)(2,1)S(1)}, bf16[32,7296]{1,0:T(8,128)(2,1)S(1)}, u32[]{:S(2)}, u32[]{:S(2)}) collective-permute-start(bf16[32,7296]{1,0:T(8,128)(2,1)S(1)} %constant_dynamic-update-slice_fusion.11.refs_1_), channel_id=1, source_target_pairs={{0,16},{1,3},{2,18},{3,1},{4,20},{5,7},{6,22},{7,5},{8,24},{9,11},... | collective-permute-start | bytes 1400840 | tf_op jit(solution)/shard_map/ppermute | solution.py:115
  40.0 13.0 %collective-permute-start.16 = (bf16[32,7296]{1,0:T(8,128)(2,1)S(1)}, bf16[32,7296]{1,0:T(8,128)(2,1)S(1)}, u32[]{:S(2)}, u32[]{:S(2)}) collective-permute-start(bf16[32,7296]{1,0:T(8,128)(2,1)S(1)} %constant_dynamic-update-slice_fusion.11.refs_1_), channel_id=1, source_target_pairs={{0,1},{1,0},{2,3},{3,2},{4,5},{5,4},{6,7},{7,6},{8,9},{9,8},{10,11... | collective-permute-start | bytes 1400840 | tf_op jit(solution)/shard_map/ppermute | solution.py:115
  40.0 12.9 %collective-permute-start.15 = (bf16[64,7296]{1,0:T(8,128)(2,1)S(1)}, bf16[64,7296]{1,0:T(8,128)(2,1)S(1)}, u32[]{:S(2)}, u32[]{:S(2)}) collective-permute-start(bf16[64,7296]{1,0:T(8,128)(2,1)S(1)} %constant_dynamic-update-slice_fusion.8.refs_0_), channel_id=1, source_target_pairs={{0,1},{1,0},{2,3},{3,2},{4,5},{5,4},{6,7},{7,6},{8,9},{9,8},{10,11... | collective-permute-start | bytes 2801672 | tf_op jit(solution)/shard_map/ppermute | solution.py:115
  46.6 2.5 %collective-permute-start.18 = (bf16[64,7168]{1,0:T(8,128)(2,1)S(1)}, bf16[64,7168]{1,0:T(8,128)(2,1)S(1)}, u32[]{:S(2)}, u32[]{:S(2)}) collective-permute-start(bf16[64,7168]{1,0:T(8,128)(2,1)S(1)} %get-tuple-element.17), channel_id=1, source_target_pairs={{0,1},{1,0},{2,3},{3,2},{4,5},{5,4},{6,7},{7,6},{8,9},{9,8},{10,11... | collective-permute-start | bytes 2752520 | tf_op jit(solution)/shard_map/ppermute | solution.py:115
  48.1 4.8 %collective-permute-start.17 = (bf16[32,7296]{1,0:T(8,128)(2,1)S(1)}, bf16[32,7296]{1,0:T(8,128)(2,1)S(1)}, u32[]{:S(2)}, u32[]{:S(2)}) collective-permute-start(bf16[32,7296]{1,0:T(8,128)(2,1)S(1)} %broadcast_add_fusion), channel_id=1, source_target_pairs={{0,1},{1,0},{2,3},{3,2},{4,5},{5,4},{6,7},{7,6},{8,9},{9,8},{10,11... | collective-permute-start | bytes 1400840 | tf_op jit(solution)/shard_map/ppermute | solution.py:115
  48.5 2.9 %collective-permute-start.8 = (bf16[64,7168]{1,0:T(8,128)(2,1)S(1)}, bf16[64,7168]{1,0:T(8,128)(2,1)S(1)}, u32[]{:S(2)}, u32[]{:S(2)}) collective-permute-start(bf16[64,7168]{1,0:T(8,128)(2,1)S(1)} %get-tuple-element.15), channel_id=1, source_target_pairs={{0,1},{1,0},{2,3},{3,2},{4,5},{5,4},{6,7},{7,6},{8,9},{9,8},{10,11... | collective-permute-start | bytes 2752520 | tf_op jit(solution)/shard_map/ppermute | solution.py:115
  49.2 10.3 %collective-permute-start.25 = (bf16[32,7168]{1,0:T(8,128)(2,1)S(1)}, bf16[32,7168]{1,0:T(8,128)(2,1)S(1)}, u32[]{:S(2)}, u32[]{:S(2)}) collective-permute-start(bf16[32,7168]{1,0:T(8,128)(2,1)S(1)} %add_convert_fusion.2.refs_6_), channel_id=1, source_target_pairs={{0,16},{1,3},{2,18},{3,1},{4,20},{5,7},{6,22},{7,5},{8,24},{9,11},... | collective-permute-start | bytes 1376264 | tf_op jit(solution)/shard_map/ppermute | solution.py:115
  51.5 32.0 %collective-permute-start.9 = (bf16[32,7168]{1,0:T(8,128)(2,1)S(1)}, bf16[32,7168]{1,0:T(8,128)(2,1)S(1)}, u32[]{:S(2)}, u32[]{:S(2)}) collective-permute-start(bf16[32,7168]{1,0:T(8,128)(2,1)S(1)} %add_convert_fusion.3.refs_7_), channel_id=1, source_target_pairs={{0,16},{1,3},{2,18},{3,1},{4,20},{5,7},{6,22},{7,5},{8,24},{9,11},... | collective-permute-start | bytes 1376264 | tf_op jit(solution)/shard_map/ppermute | solution.py:115
  58.9 2.5 %collective-permute-start.20 = (bf16[64,7168]{1,0:T(8,128)(2,1)S(1)}, bf16[64,7168]{1,0:T(8,128)(2,1)S(1)}, u32[]{:S(2)}, u32[]{:S(2)}) collective-permute-start(bf16[64,7168]{1,0:T(8,128)(2,1)S(1)} %get-tuple-element.23), channel_id=1, source_target_pairs={{0,1},{1,0},{2,3},{3,2},{4,5},{5,4},{6,7},{7,6},{8,9},{9,8},{10,11... | collective-permute-start | bytes 2752520 | tf_op jit(solution)/shard_map/ppermute | solution.py:115
  59.3 13.9 %collective-permute-start.19 = (bf16[64,7168]{1,0:T(8,128)(2,1)S(1)}, bf16[64,7168]{1,0:T(8,128)(2,1)S(1)}, u32[]{:S(2)}, u32[]{:S(2)}) collective-permute-start(bf16[64,7168]{1,0:T(8,128)(2,1)S(1)} %get-tuple-element.20), channel_id=1, source_target_pairs={{0,1},{1,0},{2,3},{3,2},{4,5},{5,4},{6,7},{7,6},{8,9},{9,8},{10,11... | collective-permute-start | bytes 2752520 | tf_op jit(solution)/shard_map/ppermute | solution.py:115
  59.6 7.2 %collective-permute-start.26 = (bf16[16,7168]{1,0:T(8,128)(2,1)S(1)}, bf16[16,7168]{1,0:T(8,128)(2,1)S(1)}, u32[]{:S(2)}, u32[]{:S(2)}) collective-permute-start(bf16[16,7168]{1,0:T(8,128)(2,1)S(1)} %add_convert_fusion.8), channel_id=1, source_target_pairs={{0,2},{1,17},{2,0},{3,19},{4,6},{5,21},{6,4},{7,23},{8,10},{9,25},... | collective-permute-start | bytes 688136 | tf_op jit(solution)/shard_map/ppermute | solution.py:115
  61.6 8.7 %collective-permute-start.21 = (bf16[32,7168]{1,0:T(8,128)(2,1)S(1)}, bf16[32,7168]{1,0:T(8,128)(2,1)S(1)}, u32[]{:S(2)}, u32[]{:S(2)}) collective-permute-start(bf16[32,7168]{1,0:T(8,128)(2,1)S(1)} %add_convert_fusion), channel_id=1, source_target_pairs={{0,16},{1,3},{2,18},{3,1},{4,20},{5,7},{6,22},{7,5},{8,24},{9,11},... | collective-permute-start | bytes 1376264 | tf_op jit(solution)/shard_map/ppermute | solution.py:115
  66.9 7.6 %collective-permute-start.27 = (bf16[16,7168]{1,0:T(8,128)(2,1)S(1)}, bf16[16,7168]{1,0:T(8,128)(2,1)S(1)}, u32[]{:S(2)}, u32[]{:S(2)}) collective-permute-start(bf16[16,7168]{1,0:T(8,128)(2,1)S(1)} %add_convert_fusion.7), channel_id=1, source_target_pairs={{0,8},{1,9},{2,10},{3,11},{4,0},{5,1},{6,2},{7,3},{8,12},{9,13},{1... | collective-permute-start | bytes 688136 | tf_op jit(solution)/shard_map/ppermute | solution.py:115
  70.4 7.3 %collective-permute-start.24 = (bf16[16,7168]{1,0:T(8,128)(2,1)S(1)}, bf16[16,7168]{1,0:T(8,128)(2,1)S(1)}, u32[]{:S(2)}, u32[]{:S(2)}) collective-permute-start(bf16[16,7168]{1,0:T(8,128)(2,1)S(1)} %add_convert_fusion.9), channel_id=1, source_target_pairs={{0,2},{1,17},{2,0},{3,19},{4,6},{5,21},{6,4},{7,23},{8,10},{9,25},... | collective-permute-start | bytes 688136 | tf_op jit(solution)/shard_map/ppermute | solution.py:115
  73.3 8.5 %collective-permute-start.22 = (bf16[32,7168]{1,0:T(8,128)(2,1)S(1)}, bf16[32,7168]{1,0:T(8,128)(2,1)S(1)}, u32[]{:S(2)}, u32[]{:S(2)}) collective-permute-start(bf16[32,7168]{1,0:T(8,128)(2,1)S(1)} %fusion), channel_id=1, source_target_pairs={{0,16},{1,3},{2,18},{3,1},{4,20},{5,7},{6,22},{7,5},{8,24},{9,11},... | collective-permute-start | bytes 1376264 | tf_op jit(solution)/shard_map/ppermute | solution.py:115
  77.7 14.1 %copy-start.3 = (bf16[16,64,576]{2,1,0:T(8,128)(2,1)S(1)}, bf16[16,64,576]{2,1,0:T(8,128)(2,1)}, u32[]{:S(2)}) copy-start(bf16[16,64,576]{2,1,0:T(8,128)(2,1)} %q.1) | copy-start | bytes 3538948
  77.9 6.9 %collective-permute-start.28 = (bf16[16,7168]{1,0:T(8,128)(2,1)S(1)}, bf16[16,7168]{1,0:T(8,128)(2,1)S(1)}, u32[]{:S(2)}, u32[]{:S(2)}) collective-permute-start(bf16[16,7168]{1,0:T(8,128)(2,1)S(1)} %add_convert_fusion.6), channel_id=1, source_target_pairs={{0,8},{1,9},{2,10},{3,11},{4,0},{5,1},{6,2},{7,3},{8,12},{9,13},{1... | collective-permute-start | bytes 688136 | tf_op jit(solution)/shard_map/ppermute | solution.py:115
  81.9 6.1 %collective-permute-start.23 = (bf16[16,7168]{1,0:T(8,128)(2,1)S(1)}, bf16[16,7168]{1,0:T(8,128)(2,1)S(1)}, u32[]{:S(2)}, u32[]{:S(2)}) collective-permute-start(bf16[16,7168]{1,0:T(8,128)(2,1)S(1)} %add_convert_fusion.10), channel_id=1, source_target_pairs={{0,2},{1,17},{2,0},{3,19},{4,6},{5,21},{6,4},{7,23},{8,10},{9,25},... | collective-permute-start | bytes 688136 | tf_op jit(solution)/shard_map/ppermute | solution.py:115
  83.5 11.4 %collective-permute-start.10 = (bf16[16,7168]{1,0:T(8,128)(2,1)S(1)}, bf16[16,7168]{1,0:T(8,128)(2,1)S(1)}, u32[]{:S(2)}, u32[]{:S(2)}) collective-permute-start(bf16[16,7168]{1,0:T(8,128)(2,1)S(1)} %add_convert_fusion.11), channel_id=1, source_target_pairs={{0,2},{1,17},{2,0},{3,19},{4,6},{5,21},{6,4},{7,23},{8,10},{9,25},... | collective-permute-start | bytes 688136 | tf_op jit(solution)/shard_map/ppermute | solution.py:115
  88.2 7.3 %collective-permute-start.29 = (bf16[16,7168]{1,0:T(8,128)(2,1)S(1)}, bf16[16,7168]{1,0:T(8,128)(2,1)S(1)}, u32[]{:S(2)}, u32[]{:S(2)}) collective-permute-start(bf16[16,7168]{1,0:T(8,128)(2,1)S(1)} %add_convert_fusion.5), channel_id=1, source_target_pairs={{0,8},{1,9},{2,10},{3,11},{4,0},{5,1},{6,2},{7,3},{8,12},{9,13},{1... | collective-permute-start | bytes 688136 | tf_op jit(solution)/shard_map/ppermute | solution.py:115
  (7 other events, 65.5 us)

commit v7 on v6

--- a/solution.py
+++ b/solution.py
@@ -128,7 +128,9 @@
         )
         stops = list(range(0, line, 2)) + list(range(1, line, 2))[::-1]
         following = {z: stops[(i + 1) % line] for i, z in enumerate(stops)}
+        before = {t: z for z, t in following.items()}
         self.ring = permutation(n_dev, lambda y, z, x, c: (y, following[z], x, c))
+        self.ring_back = permutation(n_dev, lambda y, z, x, c: (y, before[z], x, c))
 
 
 def plus(*terms):
@@ -317,35 +319,37 @@
     n = mv.line
     half = n // 2
     cat = lambda *a: jnp.concatenate(a, axis=0)
-    block = [pack_rows(hidden_in, expert_ids, gate_coef, n_dev)]
-    for _ in range(n - 1):
-        block.append(mv.ring(block[-1]))
-    near = [cat(b, mv.first(b)) for b in block]
-    far = [mv.second(a) for a in near]
-    pairs = [a for k in range(n) for a in (near[k], far[k])]
-    own = cat(*pairs[: 2 * half])
-    held = [hold(w, a) for w, a in zip(weights, (block[1], block[2], near[2]))]
+    block = {0: pack_rows(hidden_in, expert_ids, gate_coef, n_dev)}
+    arrival = sorted(range(n), key=lambda k: (min(k, n - k), k))
+    for k in arrival[1:]:
+        block[k] = mv.ring(block[k - 1]) if 2 * k <= n else mv.ring_back(block[(k + 1) % n])
+    near = {k: cat(block[k], mv.first(block[k])) for k in arrival}
+    far = {k: mv.second(near[k]) for k in arrival}
+    own = cat(*[a for k in range(half) for a in (near[k], far[k])])
+    held = [hold(w, a) for w, a in zip(weights, (near[0], block[2], near[arrival[2]]))]
     early = expert_group([own, mv.core(own)], half, *weights, n_dev, *held)
     rows = block[0].shape[0]
-    y_near, y_far = early[0 : 2 * half : 2], early[1 : 2 * half : 2]
     order = list(range(1, n)) + [0]
     mine, crossed, back = {}, {}, []
     for k in [k for k in order if k < half]:
         mine[k] = mv.core(early[2 * half + k])
-        back.append(plus(y_far[k], mine[k][2 * rows :]))
+        back.append(plus(early[2 * k + 1], mine[k][2 * rows :]))
         crossed[k] = mv.second(back[-1])
-    late = [cat(near[k], far[k]) for k in range(half, n - 1)] + pairs[2 * n - 2 :]
+    last = arrival[-1]
+    late = [cat(near[k], far[k]) for k in arrival[half:-1]] + [near[last], far[last]]
     theirs = [mv.core(a) for a in late[:-1]] + [mv.core(after(late[-1], early[-1]))]
     late = expert_group(late + theirs, n - half, *weights, n_dev, *back)
-    y_near, y_far = y_near + late[0 : 2 * (n - half) : 2], y_far + late[1 : 2 * (n - half) : 2]
+    spot = {k: i for i, k in enumerate(arrival[half:])}
     acc = ()
     for k in order:
         if k >= half:
-            mine[k] = mv.core(late[2 * (n - half) + k - half])
-            back = plus(y_far[k], mine[k][2 * rows :])
+            i = spot[k]
+            mine[k] = mv.core(late[2 * (n - half) + i])
+            back = plus(late[2 * i + 1], mine[k][2 * rows :])
             crossed[k] = mv.second(after(back, crossed[k - 1]) if k > half else back)
-        side = mv.first(plus(y_near[k][rows:], mine[k][rows : 2 * rows], crossed[k][rows:]))
-        total = plus(y_near[k][:rows], mine[k][:rows], crossed[k][:rows], side, *acc)
+        close = late[2 * spot[k]] if k >= half else early[2 * k]
+        side = mv.first(plus(close[rows:], mine[k][rows : 2 * rows], crossed[k][rows:]))
+        total = plus(close[:rows], mine[k][:rows], crossed[k][:rows], side, *acc)
         if k:
             acc = (mv.ring(total),)
     return total

time: 96.5 us -> 94.6 us (0.980)
  starting transfers between devices: 41.9 us -> 31.1 us
  waiting for transfers between devices: 26.7 us -> 35.6 us
    ppermute x30, starting transfers between devices: 41.9 us -> 31.1 us  [permutation(): return lambda a: lax.ppermute(a, AXES, pairs)]
    ppermute x30, waiting for transfers between devices: 26.7 us -> 35.6 us  [permutation(): return lambda a: lax.ppermute(a, AXES, pairs)]
where the time goes in v7:
time: 94.6 us; the launch traced here: 94.4 us
  waiting for transfers between devices  35.6 us (38%)
  starting transfers between devices  31.1 us (33%)
  Pallas kernels  16.8 us (18%)
  local copies, waits for them, and re-layouts  5.46 us (6%)
  other arithmetic  3.15 us (3%)
  between operations  2.23 us (2%)
    ppermute x30, waiting for transfers between devices, permutation(): return lambda a: lax.ppermute(a, AXES, pairs)  35.6 us
    ppermute x30, starting transfers between devices, permutation(): return lambda a: lax.ppermute(a, AXES, pairs)  31.1 us
    pallas_call x2, Pallas kernels, expert_group(): pl.pallas_call(functools.partial(expert_kernel, sizes, outs, n_experts, s...  11.9 us
    unnamed x26, local copies, waits for them, and re-layouts  4.34 us
    pallas_call x1, Pallas kernels, attend_rows(): pl.pallas_call(attend_kernel, grid=(rows // step,), in_specs=[SCALARS, pl...  3.15 us
    convert_element_type x11, other arithmetic, plus(): return total.astype(jnp.bfloat16)  1.95 us
  transfers between devices with their start and end apart: 30, of which 14 were waited for; matrix products, arithmetic and copies ran while one was open for 5% of the time, Pallas kernels for 16%

profile of v7, /device:TPU:0, one launch (start us, length us, event | category | flops | bytes accessed | tf_op | source)
XLA Modules:
  0.0 94.4 jit_solution(8900640259217826092)
XLA Ops:
  0.6 1.8 %pack.1 = bf16[16,7296]{1,0:T(8,128)(2,1)} custom-call(s32[8,16]{1,0:T(8,128)} %bitcast.11, f32[8,16]{1,0:T(8,128)} %bitcast.12, bf16[16,7168]{1,0:T(8,128)(2,1)} %x.1), custom_call_target="tpu_custom_call" | custom-call | tf_op jit(solution)/shard_map/pack/pallas_call | solution.py:179
  2.4 2.9 %collective-permute-start = (bf16[16,7296]{1,0:T(8,128)(2,1)}, bf16[16,7296]{1,0:T(8,128)(2,1)S(1)}, u32[]{:S(2)}, u32[]{:S(2)}) collective-permute-start(bf16[16,7296]{1,0:T(8,128)(2,1)} %pack.1), channel_id=1, source_target_pairs={{0,2},{1,17},{2,0},{3,19},{4,6},{5,21},{6,4},{7,23},{8,10},{9,25},... | collective-permute-start | bytes 700424 | tf_op jit(solution)/shard_map/ppermute | solution.py:115
  5.4 2.6 %collective-permute-start.2 = (bf16[16,7296]{1,0:T(8,128)(2,1)}, bf16[16,7296]{1,0:T(8,128)(2,1)S(1)}, u32[]{:S(2)}, u32[]{:S(2)}) collective-permute-start(bf16[16,7296]{1,0:T(8,128)(2,1)} %pack.1), channel_id=1, source_target_pairs={{0,8},{1,9},{2,10},{3,11},{4,0},{5,1},{6,2},{7,3},{8,12},{9,13},{1... | collective-permute-start | bytes 700424 | tf_op jit(solution)/shard_map/ppermute | solution.py:115
  8.0 1.0 %constant_dynamic-update-slice_fusion.5 = bf16[128,7296]{1,0:T(8,128)(2,1)S(1)} fusion(bf16[16,7296]{1,0:T(8,128)(2,1)} %pack.1), kind=kLoop, calls=%fused_computation.21 | loop fusion | bytes 466944
  9.6 1.0 %pad_maximum_fusion.refs_0_ = bf16[32,7296]{1,0:T(8,128)(2,1)S(1)} fusion(bf16[16,7296]{1,0:T(8,128)(2,1)S(1)} %collective-permute-done, bf16[16,7296]{1,0:T(8,128)(2,1)} %pack.1), kind=kLoop, calls=%fused_computation.4 | loop fusion | flops 933888 | bytes 933888 | tf_op jit(solution)/shard_map/concatenate | solution.py:321
  10.6 2.1 %collective-permute-start.1 = (bf16[32,7296]{1,0:T(8,128)(2,1)S(1)}, bf16[32,7296]{1,0:T(8,128)(2,1)S(1)}, u32[]{:S(2)}, u32[]{:S(2)}) collective-permute-start(bf16[32,7296]{1,0:T(8,128)(2,1)S(1)} %pad_maximum_fusion.refs_0_), channel_id=1, source_target_pairs={{0,16},{1,3},{2,18},{3,1},{4,20},{5,7},{6,22},{7,5},{8,24},{9,11},... | collective-permute-start | bytes 1400840 | tf_op jit(solution)/shard_map/ppermute | solution.py:115
  12.7 3.1 %copy-done = bf16[1,7168,512]{2,1,0:T(8,128)(2,1)S(1)} copy-done((bf16[1,7168,512]{2,1,0:T(8,128)(2,1)S(1)}, bf16[1,7168,512]{2,1,0:T(8,128)(2,1)}, u32[]{:S(2)}) %copy-start) | copy-done | bytes 7340056
  15.8 1.6 %collective-permute-start.3 = (bf16[16,7296]{1,0:T(8,128)(2,1)S(1)}, bf16[16,7296]{1,0:T(8,128)(2,1)S(1)}, u32[]{:S(2)}, u32[]{:S(2)}) collective-permute-start(bf16[16,7296]{1,0:T(8,128)(2,1)S(1)} %collective-permute-done.2), channel_id=1, source_target_pairs={{0,2},{1,17},{2,0},{3,19},{4,6},{5,21},{6,4},{7,23},{8,10},{9,25},... | collective-permute-start | bytes 700424 | tf_op jit(solution)/shard_map/ppermute | solution.py:115
  17.4 2.6 %collective-permute-start.6 = (bf16[16,7296]{1,0:T(8,128)(2,1)S(1)}, bf16[16,7296]{1,0:T(8,128)(2,1)S(1)}, u32[]{:S(2)}, u32[]{:S(2)}) collective-permute-start(bf16[16,7296]{1,0:T(8,128)(2,1)S(1)} %collective-permute-done.2), channel_id=1, source_target_pairs={{0,8},{1,9},{2,10},{3,11},{4,0},{5,1},{6,2},{7,3},{8,12},{9,13},{1... | collective-permute-start | bytes 700424 | tf_op jit(solution)/shard_map/ppermute | solution.py:115
  20.0 1.7 %collective-permute-start.8 = (bf16[16,7296]{1,0:T(8,128)(2,1)S(1)}, bf16[16,7296]{1,0:T(8,128)(2,1)S(1)}, u32[]{:S(2)}, u32[]{:S(2)}) collective-permute-start(bf16[16,7296]{1,0:T(8,128)(2,1)S(1)} %collective-permute-done.7), channel_id=1, source_target_pairs={{0,2},{1,17},{2,0},{3,19},{4,6},{5,21},{6,4},{7,23},{8,10},{9,25},... | collective-permute-start | bytes 700424 | tf_op jit(solution)/shard_map/ppermute | solution.py:115
  22.3 5.4 %collective-permute-done.8 = bf16[16,7296]{1,0:T(8,128)(2,1)S(1)} collective-permute-done((bf16[16,7296]{1,0:T(8,128)(2,1)S(1)}, bf16[16,7296]{1,0:T(8,128)(2,1)S(1)}, u32[]{:S(2)}, u32[]{:S(2)}) %collective-permute-start.8) | collective-permute-done | bytes 233504 | tf_op jit(solution)/shard_map/ppermute | solution.py:115
  27.8 2.5 %collective-permute-start.13 = (bf16[16,7296]{1,0:T(8,128)(2,1)S(1)}, bf16[16,7296]{1,0:T(8,128)(2,1)S(1)}, u32[]{:S(2)}, u32[]{:S(2)}) collective-permute-start(bf16[16,7296]{1,0:T(8,128)(2,1)S(1)} %collective-permute-done.6.refs_0_), channel_id=1, source_target_pairs={{0,2},{1,17},{2,0},{3,19},{4,6},{5,21},{6,4},{7,23},{8,10},{9,25},... | collective-permute-start | bytes 700424 | tf_op jit(solution)/shard_map/ppermute | solution.py:115
  30.4 1.4 %collective-permute-done.4 = bf16[32,7296]{1,0:T(8,128)(2,1)S(1)} collective-permute-done((bf16[32,7296]{1,0:T(8,128)(2,1)S(1)}, bf16[32,7296]{1,0:T(8,128)(2,1)S(1)}, u32[]{:S(2)}, u32[]{:S(2)}) %collective-permute-start.4) | collective-permute-done | bytes 466976 | tf_op jit(solution)/shard_map/ppermute | solution.py:115
  32.1 4.8 %collective-permute-done.13 = bf16[16,7296]{1,0:T(8,128)(2,1)S(1)} collective-permute-done((bf16[16,7296]{1,0:T(8,128)(2,1)S(1)}, bf16[16,7296]{1,0:T(8,128)(2,1)S(1)}, u32[]{:S(2)}, u32[]{:S(2)}) %collective-permute-start.13) | collective-permute-done | bytes 233504 | tf_op jit(solution)/shard_map/ppermute | solution.py:115
  37.0 2.0 %collective-permute-start.14 = (bf16[32,7296]{1,0:T(8,128)(2,1)S(1)}, bf16[32,7296]{1,0:T(8,128)(2,1)S(1)}, u32[]{:S(2)}, u32[]{:S(2)}) collective-permute-start(bf16[32,7296]{1,0:T(8,128)(2,1)S(1)} %constant_dynamic-update-slice_fusion.11.refs_1_), channel_id=1, source_target_pairs={{0,16},{1,3},{2,18},{3,1},{4,20},{5,7},{6,22},{7,5},{8,24},{9,11},... | collective-permute-start | bytes 1400840 | tf_op jit(solution)/shard_map/ppermute | solution.py:115
  39.6 5.9 %experts.2 = (bf16[32,7168]{1,0:T(8,128)(2,1)S(1)}, bf16[32,7168]{1,0:T(8,128)(2,1)S(1)}, bf16[32,7168]{1,0:T(8,128)(2,1)S(1)}, bf16[32,7168]{1,0:T(8,128)(2,1)S...) custom-call(s32[1]{0:T(128)} %bitcast.1.me, bf16[1,7168,512]{2,1,0:T(8,128)(2,1)S(1)} %bitcast.7, ...), custom_call_target="tpu_custom_call" | custom-call | flops 5637144576 | bytes 1 | tf_op jit(solution)/shard_map/experts/pallas_call | solution.py:294
  48.4 1.8 %collective-permute-done.9 = bf16[64,7168]{1,0:T(8,128)(2,1)S(1)} collective-permute-done((bf16[64,7168]{1,0:T(8,128)(2,1)S(1)}, bf16[64,7168]{1,0:T(8,128)(2,1)S(1)}, u32[]{:S(2)}, u32[]{:S(2)}) %collective-permute-start.9) | collective-permute-done | bytes 917536 | tf_op jit(solution)/shard_map/ppermute | solution.py:115
  51.0 5.9 %experts.3 = (bf16[32,7168]{1,0:T(8,128)(2,1)S(1)}, bf16[32,7168]{1,0:T(8,128)(2,1)S(1)}, bf16[32,7168]{1,0:T(8,128)(2,1)S(1)}, bf16[32,7168]{1,0:T(8,128)(2,1)S...) custom-call(s32[1]{0:T(128)} %bitcast.1.me, bf16[1,7168,512]{2,1,0:T(8,128)(2,1)S(1)} %bitcast.7, ...), custom_call_target="tpu_custom_call" | custom-call | flops 5637144576 | bytes 1 | tf_op jit(solution)/shard_map/experts/pallas_call | solution.py:294
  57.0 1.6 %collective-permute-start.20 = (bf16[64,7168]{1,0:T(8,128)(2,1)S(1)}, bf16[64,7168]{1,0:T(8,128)(2,1)S(1)}, u32[]{:S(2)}, u32[]{:S(2)}) collective-permute-start(bf16[64,7168]{1,0:T(8,128)(2,1)S(1)} %get-tuple-element.23), channel_id=1, source_target_pairs={{0,1},{1,0},{2,3},{3,2},{4,5},{5,4},{6,7},{7,6},{8,9},{9,8},{10,11... | collective-permute-start | bytes 2752520 | tf_op jit(solution)/shard_map/ppermute | solution.py:115
  58.7 1.0 %collective-permute-start.26 = (bf16[16,7168]{1,0:T(8,128)(2,1)S(1)}, bf16[16,7168]{1,0:T(8,128)(2,1)S(1)}, u32[]{:S(2)}, u32[]{:S(2)}) collective-permute-start(bf16[16,7168]{1,0:T(8,128)(2,1)S(1)} %add_convert_fusion.8), channel_id=1, source_target_pairs={{0,2},{1,17},{2,0},{3,19},{4,6},{5,21},{6,4},{7,23},{8,10},{9,25},... | collective-permute-start | bytes 688136 | tf_op jit(solution)/shard_map/ppermute | solution.py:115
  59.7 0.9 collective-permute-done.20
  61.3 4.4 %collective-permute-done.26 = bf16[16,7168]{1,0:T(8,128)(2,1)S(1)} collective-permute-done((bf16[16,7168]{1,0:T(8,128)(2,1)S(1)}, bf16[16,7168]{1,0:T(8,128)(2,1)S(1)}, u32[]{:S(2)}, u32[]{:S(2)}) %collective-permute-start.26) | collective-permute-done | bytes 229408 | tf_op jit(solution)/shard_map/ppermute | solution.py:115
  65.9 0.9 collective-permute-start.27
  66.8 2.5 %collective-permute-done.21 = bf16[32,7168]{1,0:T(8,128)(2,1)S(1)} collective-permute-done((bf16[32,7168]{1,0:T(8,128)(2,1)S(1)}, bf16[32,7168]{1,0:T(8,128)(2,1)S(1)}, u32[]{:S(2)}, u32[]{:S(2)}) %collective-permute-start.21) | collective-permute-done | bytes 458784 | tf_op jit(solution)/shard_map/ppermute | solution.py:115
  69.4 1.9 %collective-permute-start.24 = (bf16[16,7168]{1,0:T(8,128)(2,1)S(1)}, bf16[16,7168]{1,0:T(8,128)(2,1)S(1)}, u32[]{:S(2)}, u32[]{:S(2)}) collective-permute-start(bf16[16,7168]{1,0:T(8,128)(2,1)S(1)} %add_convert_fusion.9), channel_id=1, source_target_pairs={{0,2},{1,17},{2,0},{3,19},{4,6},{5,21},{6,4},{7,23},{8,10},{9,25},... | collective-permute-start | bytes 688136 | tf_op jit(solution)/shard_map/ppermute | solution.py:115
  73.2 3.7 %collective-permute-done.24 = bf16[16,7168]{1,0:T(8,128)(2,1)S(1)} collective-permute-done((bf16[16,7168]{1,0:T(8,128)(2,1)S(1)}, bf16[16,7168]{1,0:T(8,128)(2,1)S(1)}, u32[]{:S(2)}, u32[]{:S(2)}) %collective-permute-start.24) | collective-permute-done | bytes 229408 | tf_op jit(solution)/shard_map/ppermute | solution.py:115
  77.1 1.0 %collective-permute-start.28 = (bf16[16,7168]{1,0:T(8,128)(2,1)S(1)}, bf16[16,7168]{1,0:T(8,128)(2,1)S(1)}, u32[]{:S(2)}, u32[]{:S(2)}) collective-permute-start(bf16[16,7168]{1,0:T(8,128)(2,1)S(1)} %add_convert_fusion.6), channel_id=1, source_target_pairs={{0,8},{1,9},{2,10},{3,11},{4,0},{5,1},{6,2},{7,3},{8,12},{9,13},{1... | collective-permute-start | bytes 688136 | tf_op jit(solution)/shard_map/ppermute | solution.py:115
  78.0 3.1 %collective-permute-done.22 = bf16[32,7168]{1,0:T(8,128)(2,1)S(1)} collective-permute-done((bf16[32,7168]{1,0:T(8,128)(2,1)S(1)}, bf16[32,7168]{1,0:T(8,128)(2,1)S(1)}, u32[]{:S(2)}, u32[]{:S(2)}) %collective-permute-start.22) | collective-permute-done | bytes 458784 | tf_op jit(solution)/shard_map/ppermute | solution.py:115
  81.6 1.9 %collective-permute-start.11 = (bf16[16,7168]{1,0:T(8,128)(2,1)S(1)}, bf16[16,7168]{1,0:T(8,128)(2,1)S(1)}, u32[]{:S(2)}, u32[]{:S(2)}) collective-permute-start(bf16[16,7168]{1,0:T(8,128)(2,1)S(1)} %add_convert_fusion.11), channel_id=1, source_target_pairs={{0,2},{1,17},{2,0},{3,19},{4,6},{5,21},{6,4},{7,23},{8,10},{9,25},... | collective-permute-start | bytes 688136 | tf_op jit(solution)/shard_map/ppermute | solution.py:115
  83.5 3.8 %collective-permute-done.23 = bf16[16,7168]{1,0:T(8,128)(2,1)S(1)} collective-permute-done((bf16[16,7168]{1,0:T(8,128)(2,1)S(1)}, bf16[16,7168]{1,0:T(8,128)(2,1)S(1)}, u32[]{:S(2)}, u32[]{:S(2)}) %collective-permute-start.23) | collective-permute-done | bytes 229408 | tf_op jit(solution)/shard_map/ppermute | solution.py:115
  88.3 3.2 %attend.1 = bf16[16,64,512]{2,1,0:T(8,128)(2,1)} custom-call(s32[16]{0:T(128)S(1)} %copy-done.4, bf16[16,64,576]{2,1,0:T(8,128)(2,1)S(1)} %copy-done.3, bf16[16,576,128]{2,1,0:T(8,128)(2,1)S(1)} %bitcast.10), custom_call_target="tpu_custom_call" | custom-call | flops 2852126720 | bytes 1 | tf_op jit(solution)/shard_map/attend/pallas_call | solution.py:215
  91.5 2.1 %collective-permute-done.29 = bf16[16,7168]{1,0:T(8,128)(2,1)S(1)} collective-permute-done((bf16[16,7168]{1,0:T(8,128)(2,1)S(1)}, bf16[16,7168]{1,0:T(8,128)(2,1)S(1)}, u32[]{:S(2)}, u32[]{:S(2)}) %collective-permute-start.29) | collective-permute-done | bytes 229408 | tf_op jit(solution)/shard_map/ppermute | solution.py:115
  (83 shorter events, 10.0 us)
Async XLA Ops:
  2.4 7.2 %collective-permute-start = (bf16[16,7296]{1,0:T(8,128)(2,1)}, bf16[16,7296]{1,0:T(8,128)(2,1)S(1)}, u32[]{:S(2)}, u32[]{:S(2)}) collective-permute-start(bf16[16,7296]{1,0:T(8,128)(2,1)} %pack.1), channel_id=1, source_target_pairs={{0,2},{1,17},{2,0},{3,19},{4,6},{5,21},{6,4},{7,23},{8,10},{9,25},... | collective-permute-start | bytes 700424 | tf_op jit(solution)/shard_map/ppermute | solution.py:115
  5.4 10.4 %collective-permute-start.2 = (bf16[16,7296]{1,0:T(8,128)(2,1)}, bf16[16,7296]{1,0:T(8,128)(2,1)S(1)}, u32[]{:S(2)}, u32[]{:S(2)}) collective-permute-start(bf16[16,7296]{1,0:T(8,128)(2,1)} %pack.1), channel_id=1, source_target_pairs={{0,8},{1,9},{2,10},{3,11},{4,0},{5,1},{6,2},{7,3},{8,12},{9,13},{1... | collective-permute-start | bytes 700424 | tf_op jit(solution)/shard_map/ppermute | solution.py:115
  8.0 12.0 %collective-permute-start.7 = (bf16[16,7296]{1,0:T(8,128)(2,1)}, bf16[16,7296]{1,0:T(8,128)(2,1)S(1)}, u32[]{:S(2)}, u32[]{:S(2)}) collective-permute-start(bf16[16,7296]{1,0:T(8,128)(2,1)} %pack.1), channel_id=1, source_target_pairs={{0,4},{1,5},{2,6},{3,7},{4,12},{5,13},{6,14},{7,15},{8,0},{9,1},{1... | collective-permute-start | bytes 700424 | tf_op jit(solution)/shard_map/ppermute | solution.py:115
  10.6 19.8 %collective-permute-start.1 = (bf16[32,7296]{1,0:T(8,128)(2,1)S(1)}, bf16[32,7296]{1,0:T(8,128)(2,1)S(1)}, u32[]{:S(2)}, u32[]{:S(2)}) collective-permute-start(bf16[32,7296]{1,0:T(8,128)(2,1)S(1)} %pad_maximum_fusion.refs_0_), channel_id=1, source_target_pairs={{0,16},{1,3},{2,18},{3,1},{4,20},{5,7},{6,22},{7,5},{8,24},{9,11},... | collective-permute-start | bytes 1400840 | tf_op jit(solution)/shard_map/ppermute | solution.py:115
  15.8 16.2 %copy-start.1 = (bf16[1,512,7168]{2,1,0:T(8,128)(2,1)S(1)}, bf16[1,512,7168]{2,1,0:T(8,128)(2,1)}, u32[]{:S(2)}) copy-start(bf16[1,512,7168]{2,1,0:T(8,128)(2,1)} %w_down.3) | copy-start | bytes 22020100
  15.8 16.3 %slice-start.2 = ((s8[7340032]{0:T(1024)(128)(4,1)}), s8[4194304]{0:T(1024)(128)(4,1)S(1)}, s32[]{:S(2)}) async-start(s8[7340032]{0:T(1024)(128)(4,1)} %bitcast.8), calls=%async_computation.2 | async-start | bytes 8388608
  15.8 6.1 %collective-permute-start.3 = (bf16[16,7296]{1,0:T(8,128)(2,1)S(1)}, bf16[16,7296]{1,0:T(8,128)(2,1)S(1)}, u32[]{:S(2)}, u32[]{:S(2)}) collective-permute-start(bf16[16,7296]{1,0:T(8,128)(2,1)S(1)} %collective-permute-done.2), channel_id=1, source_target_pairs={{0,2},{1,17},{2,0},{3,19},{4,6},{5,21},{6,4},{7,23},{8,10},{9,25},... | collective-permute-start | bytes 700424 | tf_op jit(solution)/shard_map/ppermute | solution.py:115
  17.4 10.4 %collective-permute-start.6 = (bf16[16,7296]{1,0:T(8,128)(2,1)S(1)}, bf16[16,7296]{1,0:T(8,128)(2,1)S(1)}, u32[]{:S(2)}, u32[]{:S(2)}) collective-permute-start(bf16[16,7296]{1,0:T(8,128)(2,1)S(1)} %collective-permute-done.2), channel_id=1, source_target_pairs={{0,8},{1,9},{2,10},{3,11},{4,0},{5,1},{6,2},{7,3},{8,12},{9,13},{1... | collective-permute-start | bytes 700424 | tf_op jit(solution)/shard_map/ppermute | solution.py:115
  20.0 7.7 %collective-permute-start.8 = (bf16[16,7296]{1,0:T(8,128)(2,1)S(1)}, bf16[16,7296]{1,0:T(8,128)(2,1)S(1)}, u32[]{:S(2)}, u32[]{:S(2)}) collective-permute-start(bf16[16,7296]{1,0:T(8,128)(2,1)S(1)} %collective-permute-done.7), channel_id=1, source_target_pairs={{0,2},{1,17},{2,0},{3,19},{4,6},{5,21},{6,4},{7,23},{8,10},{9,25},... | collective-permute-start | bytes 700424 | tf_op jit(solution)/shard_map/ppermute | solution.py:115
  22.0 9.9 %collective-permute-start.4 = (bf16[32,7296]{1,0:T(8,128)(2,1)S(1)}, bf16[32,7296]{1,0:T(8,128)(2,1)S(1)}, u32[]{:S(2)}, u32[]{:S(2)}) collective-permute-start(bf16[32,7296]{1,0:T(8,128)(2,1)S(1)} %pad_maximum_fusion.1), channel_id=1, source_target_pairs={{0,16},{1,3},{2,18},{3,1},{4,20},{5,7},{6,22},{7,5},{8,24},{9,11},... | collective-permute-start | bytes 1400840 | tf_op jit(solution)/shard_map/ppermute | solution.py:115
  27.7 11.3 %collective-permute-start.12 = (bf16[32,7296]{1,0:T(8,128)(2,1)S(1)}, bf16[32,7296]{1,0:T(8,128)(2,1)S(1)}, u32[]{:S(2)}, u32[]{:S(2)}) collective-permute-start(bf16[32,7296]{1,0:T(8,128)(2,1)S(1)} %get-tuple-element.27.refs_0_), channel_id=1, source_target_pairs={{0,16},{1,3},{2,18},{3,1},{4,20},{5,7},{6,22},{7,5},{8,24},{9,11},... | collective-permute-start | bytes 1400840 | tf_op jit(solution)/shard_map/ppermute | solution.py:115
  27.8 9.1 %collective-permute-start.13 = (bf16[16,7296]{1,0:T(8,128)(2,1)S(1)}, bf16[16,7296]{1,0:T(8,128)(2,1)S(1)}, u32[]{:S(2)}, u32[]{:S(2)}) collective-permute-start(bf16[16,7296]{1,0:T(8,128)(2,1)S(1)} %collective-permute-done.6.refs_0_), channel_id=1, source_target_pairs={{0,2},{1,17},{2,0},{3,19},{4,6},{5,21},{6,4},{7,23},{8,10},{9,25},... | collective-permute-start | bytes 700424 | tf_op jit(solution)/shard_map/ppermute | solution.py:115
  31.9 7.7 %collective-permute-start.5 = (bf16[128,7296]{1,0:T(8,128)(2,1)S(1)}, bf16[128,7296]{1,0:T(8,128)(2,1)S(1)}, u32[]{:S(2)}, u32[]{:S(2)}) collective-permute-start(bf16[128,7296]{1,0:T(8,128)(2,1)S(1)} %constant_dynamic-update-slice_fusion.refs_0_), channel_id=1, source_target_pairs={{0,1},{1,0},{2,3},{3,2},{4,5},{5,4},{6,7},{7,6},{8,9},{9,8},{10,11... | collective-permute-start | bytes 5603336 | tf_op jit(solution)/shard_map/ppermute | solution.py:115
  37.0 9.9 %collective-permute-start.14 = (bf16[32,7296]{1,0:T(8,128)(2,1)S(1)}, bf16[32,7296]{1,0:T(8,128)(2,1)S(1)}, u32[]{:S(2)}, u32[]{:S(2)}) collective-permute-start(bf16[32,7296]{1,0:T(8,128)(2,1)S(1)} %constant_dynamic-update-slice_fusion.11.refs_1_), channel_id=1, source_target_pairs={{0,16},{1,3},{2,18},{3,1},{4,20},{5,7},{6,22},{7,5},{8,24},{9,11},... | collective-permute-start | bytes 1400840 | tf_op jit(solution)/shard_map/ppermute | solution.py:115
  39.0 12.0 %collective-permute-start.16 = (bf16[32,7296]{1,0:T(8,128)(2,1)S(1)}, bf16[32,7296]{1,0:T(8,128)(2,1)S(1)}, u32[]{:S(2)}, u32[]{:S(2)}) collective-permute-start(bf16[32,7296]{1,0:T(8,128)(2,1)S(1)} %constant_dynamic-update-slice_fusion.11.refs_1_), channel_id=1, source_target_pairs={{0,1},{1,0},{2,3},{3,2},{4,5},{5,4},{6,7},{7,6},{8,9},{9,8},{10,11... | collective-permute-start | bytes 1400840 | tf_op jit(solution)/shard_map/ppermute | solution.py:115
  39.0 12.0 %collective-permute-start.15 = (bf16[64,7296]{1,0:T(8,128)(2,1)S(1)}, bf16[64,7296]{1,0:T(8,128)(2,1)S(1)}, u32[]{:S(2)}, u32[]{:S(2)}) collective-permute-start(bf16[64,7296]{1,0:T(8,128)(2,1)S(1)} %constant_dynamic-update-slice_fusion.8.refs_0_), channel_id=1, source_target_pairs={{0,1},{1,0},{2,3},{3,2},{4,5},{5,4},{6,7},{7,6},{8,9},{9,8},{10,11... | collective-permute-start | bytes 2801672 | tf_op jit(solution)/shard_map/ppermute | solution.py:115
  45.6 2.5 %collective-permute-start.18 = (bf16[64,7168]{1,0:T(8,128)(2,1)S(1)}, bf16[64,7168]{1,0:T(8,128)(2,1)S(1)}, u32[]{:S(2)}, u32[]{:S(2)}) collective-permute-start(bf16[64,7168]{1,0:T(8,128)(2,1)S(1)} %get-tuple-element.17), channel_id=1, source_target_pairs={{0,1},{1,0},{2,3},{3,2},{4,5},{5,4},{6,7},{7,6},{8,9},{9,8},{10,11... | collective-permute-start | bytes 2752520 | tf_op jit(solution)/shard_map/ppermute | solution.py:115
  46.9 4.1 %collective-permute-start.17 = (bf16[32,7296]{1,0:T(8,128)(2,1)S(1)}, bf16[32,7296]{1,0:T(8,128)(2,1)S(1)}, u32[]{:S(2)}, u32[]{:S(2)}) collective-permute-start(bf16[32,7296]{1,0:T(8,128)(2,1)S(1)} %broadcast_add_fusion), channel_id=1, source_target_pairs={{0,1},{1,0},{2,3},{3,2},{4,5},{5,4},{6,7},{7,6},{8,9},{9,8},{10,11... | collective-permute-start | bytes 1400840 | tf_op jit(solution)/shard_map/ppermute | solution.py:115
  47.4 2.8 %collective-permute-start.9 = (bf16[64,7168]{1,0:T(8,128)(2,1)S(1)}, bf16[64,7168]{1,0:T(8,128)(2,1)S(1)}, u32[]{:S(2)}, u32[]{:S(2)}) collective-permute-start(bf16[64,7168]{1,0:T(8,128)(2,1)S(1)} %get-tuple-element.15), channel_id=1, source_target_pairs={{0,1},{1,0},{2,3},{3,2},{4,5},{5,4},{6,7},{7,6},{8,9},{9,8},{10,11... | collective-permute-start | bytes 2752520 | tf_op jit(solution)/shard_map/ppermute | solution.py:115
  48.2 10.4 %collective-permute-start.25 = (bf16[32,7168]{1,0:T(8,128)(2,1)S(1)}, bf16[32,7168]{1,0:T(8,128)(2,1)S(1)}, u32[]{:S(2)}, u32[]{:S(2)}) collective-permute-start(bf16[32,7168]{1,0:T(8,128)(2,1)S(1)} %add_convert_fusion.2.refs_6_), channel_id=1, source_target_pairs={{0,16},{1,3},{2,18},{3,1},{4,20},{5,7},{6,22},{7,5},{8,24},{9,11},... | collective-permute-start | bytes 1376264 | tf_op jit(solution)/shard_map/ppermute | solution.py:115
  50.3 31.2 %collective-permute-start.10 = (bf16[32,7168]{1,0:T(8,128)(2,1)S(1)}, bf16[32,7168]{1,0:T(8,128)(2,1)S(1)}, u32[]{:S(2)}, u32[]{:S(2)}) collective-permute-start(bf16[32,7168]{1,0:T(8,128)(2,1)S(1)} %add_convert_fusion.3.refs_7_), channel_id=1, source_target_pairs={{0,16},{1,3},{2,18},{3,1},{4,20},{5,7},{6,22},{7,5},{8,24},{9,11},... | collective-permute-start | bytes 1376264 | tf_op jit(solution)/shard_map/ppermute | solution.py:115
  57.0 3.7 %collective-permute-start.20 = (bf16[64,7168]{1,0:T(8,128)(2,1)S(1)}, bf16[64,7168]{1,0:T(8,128)(2,1)S(1)}, u32[]{:S(2)}, u32[]{:S(2)}) collective-permute-start(bf16[64,7168]{1,0:T(8,128)(2,1)S(1)} %get-tuple-element.23), channel_id=1, source_target_pairs={{0,1},{1,0},{2,3},{3,2},{4,5},{5,4},{6,7},{7,6},{8,9},{9,8},{10,11... | collective-permute-start | bytes 2752520 | tf_op jit(solution)/shard_map/ppermute | solution.py:115
  58.5 13.9 %collective-permute-start.19 = (bf16[64,7168]{1,0:T(8,128)(2,1)S(1)}, bf16[64,7168]{1,0:T(8,128)(2,1)S(1)}, u32[]{:S(2)}, u32[]{:S(2)}) collective-permute-start(bf16[64,7168]{1,0:T(8,128)(2,1)S(1)} %get-tuple-element.20), channel_id=1, source_target_pairs={{0,1},{1,0},{2,3},{3,2},{4,5},{5,4},{6,7},{7,6},{8,9},{9,8},{10,11... | collective-permute-start | bytes 2752520 | tf_op jit(solution)/shard_map/ppermute | solution.py:115
  58.7 7.0 %collective-permute-start.26 = (bf16[16,7168]{1,0:T(8,128)(2,1)S(1)}, bf16[16,7168]{1,0:T(8,128)(2,1)S(1)}, u32[]{:S(2)}, u32[]{:S(2)}) collective-permute-start(bf16[16,7168]{1,0:T(8,128)(2,1)S(1)} %add_convert_fusion.8), channel_id=1, source_target_pairs={{0,2},{1,17},{2,0},{3,19},{4,6},{5,21},{6,4},{7,23},{8,10},{9,25},... | collective-permute-start | bytes 688136 | tf_op jit(solution)/shard_map/ppermute | solution.py:115
  60.8 8.5 %collective-permute-start.21 = (bf16[32,7168]{1,0:T(8,128)(2,1)S(1)}, bf16[32,7168]{1,0:T(8,128)(2,1)S(1)}, u32[]{:S(2)}, u32[]{:S(2)}) collective-permute-start(bf16[32,7168]{1,0:T(8,128)(2,1)S(1)} %add_convert_fusion), channel_id=1, source_target_pairs={{0,16},{1,3},{2,18},{3,1},{4,20},{5,7},{6,22},{7,5},{8,24},{9,11},... | collective-permute-start | bytes 1376264 | tf_op jit(solution)/shard_map/ppermute | solution.py:115
  65.9 7.3 %collective-permute-start.27 = (bf16[16,7168]{1,0:T(8,128)(2,1)S(1)}, bf16[16,7168]{1,0:T(8,128)(2,1)S(1)}, u32[]{:S(2)}, u32[]{:S(2)}) collective-permute-start(bf16[16,7168]{1,0:T(8,128)(2,1)S(1)} %add_convert_fusion.7), channel_id=1, source_target_pairs={{0,8},{1,9},{2,10},{3,11},{4,0},{5,1},{6,2},{7,3},{8,12},{9,13},{1... | collective-permute-start | bytes 688136 | tf_op jit(solution)/shard_map/ppermute | solution.py:115
  69.4 7.5 %collective-permute-start.24 = (bf16[16,7168]{1,0:T(8,128)(2,1)S(1)}, bf16[16,7168]{1,0:T(8,128)(2,1)S(1)}, u32[]{:S(2)}, u32[]{:S(2)}) collective-permute-start(bf16[16,7168]{1,0:T(8,128)(2,1)S(1)} %add_convert_fusion.9), channel_id=1, source_target_pairs={{0,2},{1,17},{2,0},{3,19},{4,6},{5,21},{6,4},{7,23},{8,10},{9,25},... | collective-permute-start | bytes 688136 | tf_op jit(solution)/shard_map/ppermute | solution.py:115
  72.6 8.5 %collective-permute-start.22 = (bf16[32,7168]{1,0:T(8,128)(2,1)S(1)}, bf16[32,7168]{1,0:T(8,128)(2,1)S(1)}, u32[]{:S(2)}, u32[]{:S(2)}) collective-permute-start(bf16[32,7168]{1,0:T(8,128)(2,1)S(1)} %fusion), channel_id=1, source_target_pairs={{0,16},{1,3},{2,18},{3,1},{4,20},{5,7},{6,22},{7,5},{8,24},{9,11},... | collective-permute-start | bytes 1376264 | tf_op jit(solution)/shard_map/ppermute | solution.py:115
  77.1 6.4 %collective-permute-start.28 = (bf16[16,7168]{1,0:T(8,128)(2,1)S(1)}, bf16[16,7168]{1,0:T(8,128)(2,1)S(1)}, u32[]{:S(2)}, u32[]{:S(2)}) collective-permute-start(bf16[16,7168]{1,0:T(8,128)(2,1)S(1)} %add_convert_fusion.6), channel_id=1, source_target_pairs={{0,8},{1,9},{2,10},{3,11},{4,0},{5,1},{6,2},{7,3},{8,12},{9,13},{1... | collective-permute-start | bytes 688136 | tf_op jit(solution)/shard_map/ppermute | solution.py:115
  81.2 6.1 %collective-permute-start.23 = (bf16[16,7168]{1,0:T(8,128)(2,1)S(1)}, bf16[16,7168]{1,0:T(8,128)(2,1)S(1)}, u32[]{:S(2)}, u32[]{:S(2)}) collective-permute-start(bf16[16,7168]{1,0:T(8,128)(2,1)S(1)} %add_convert_fusion.10), channel_id=1, source_target_pairs={{0,2},{1,17},{2,0},{3,19},{4,6},{5,21},{6,4},{7,23},{8,10},{9,25},... | collective-permute-start | bytes 688136 | tf_op jit(solution)/shard_map/ppermute | solution.py:115
  81.6 9.9 %collective-permute-start.11 = (bf16[16,7168]{1,0:T(8,128)(2,1)S(1)}, bf16[16,7168]{1,0:T(8,128)(2,1)S(1)}, u32[]{:S(2)}, u32[]{:S(2)}) collective-permute-start(bf16[16,7168]{1,0:T(8,128)(2,1)S(1)} %add_convert_fusion.11), channel_id=1, source_target_pairs={{0,2},{1,17},{2,0},{3,19},{4,6},{5,21},{6,4},{7,23},{8,10},{9,25},... | collective-permute-start | bytes 688136 | tf_op jit(solution)/shard_map/ppermute | solution.py:115
  87.4 6.1 %collective-permute-start.29 = (bf16[16,7168]{1,0:T(8,128)(2,1)S(1)}, bf16[16,7168]{1,0:T(8,128)(2,1)S(1)}, u32[]{:S(2)}, u32[]{:S(2)}) collective-permute-start(bf16[16,7168]{1,0:T(8,128)(2,1)S(1)} %add_convert_fusion.5), channel_id=1, source_target_pairs={{0,8},{1,9},{2,10},{3,11},{4,0},{5,1},{6,2},{7,3},{8,12},{9,13},{1... | collective-permute-start | bytes 688136 | tf_op jit(solution)/shard_map/ppermute | solution.py:115
  (7 other events, 56.5 us)

commit v8 on v7

--- a/solution.py
+++ b/solution.py
@@ -346,7 +346,7 @@
             i = spot[k]
             mine[k] = mv.core(late[2 * (n - half) + i])
             back = plus(late[2 * i + 1], mine[k][2 * rows :])
-            crossed[k] = mv.second(after(back, crossed[k - 1]) if k > half else back)
+            crossed[k] = mv.second(back + crossed[k - 1] * 0 if k > half else back)
         close = late[2 * spot[k]] if k >= half else early[2 * k]
         side = mv.first(plus(close[rows:], mine[k][rows : 2 * rows], crossed[k][rows:]))
         total = plus(close[:rows], mine[k][:rows], crossed[k][:rows], side, *acc)

time: 94.6 us -> 94.2 us (level)
  transfers between devices with their start and end apart: 30 -> 30, of which waited for: 14 -> 15; matrix products, arithmetic and copies ran while one was open for 5% -> 4% of each run, Pallas kernels for 16% -> 16%
where the time goes in v8:
time: 94.2 us; the launch traced here: 94 us
  waiting for transfers between devices  36.2 us (38%)
  starting transfers between devices  31.2 us (33%)
  Pallas kernels  16.8 us (18%)
  local copies, waits for them, and re-layouts  4.95 us (5%)
  other arithmetic  3.21 us (3%)
  between operations  1.56 us (2%)
    ppermute x30, waiting for transfers between devices, permutation(): return lambda a: lax.ppermute(a, AXES, pairs)  36.2 us
    ppermute x30, starting transfers between devices, permutation(): return lambda a: lax.ppermute(a, AXES, pairs)  31.2 us
    pallas_call x2, Pallas kernels, expert_group(): pl.pallas_call(functools.partial(expert_kernel, sizes, outs, n_experts, s...  11.9 us
    unnamed x26, local copies, waits for them, and re-layouts  4.34 us
    pallas_call x1, Pallas kernels, attend_rows(): pl.pallas_call(attend_kernel, grid=(rows // step,), in_specs=[SCALARS, pl...  3.15 us
    convert_element_type x11, other arithmetic, plus(): return total.astype(jnp.bfloat16)  1.95 us
  transfers between devices with their start and end apart: 30, of which 15 were waited for; matrix products, arithmetic and copies ran while one was open for 4% of the time, Pallas kernels for 16%

profile of v8, /device:TPU:0, one launch (start us, length us, event | category | flops | bytes accessed | tf_op | source)
XLA Modules:
  0.0 94.0 jit_solution(7361979837436056286)
XLA Ops:
  0.6 1.8 %pack.1 = bf16[16,7296]{1,0:T(8,128)(2,1)} custom-call(s32[8,16]{1,0:T(8,128)} %bitcast.10, f32[8,16]{1,0:T(8,128)} %bitcast.11, bf16[16,7168]{1,0:T(8,128)(2,1)} %x.1), custom_call_target="tpu_custom_call" | custom-call | tf_op jit(solution)/shard_map/pack/pallas_call | solution.py:179
  2.4 2.9 %collective-permute-start = (bf16[16,7296]{1,0:T(8,128)(2,1)}, bf16[16,7296]{1,0:T(8,128)(2,1)S(1)}, u32[]{:S(2)}, u32[]{:S(2)}) collective-permute-start(bf16[16,7296]{1,0:T(8,128)(2,1)} %pack.1), channel_id=1, source_target_pairs={{0,2},{1,17},{2,0},{3,19},{4,6},{5,21},{6,4},{7,23},{8,10},{9,25},... | collective-permute-start | bytes 700424 | tf_op jit(solution)/shard_map/ppermute | solution.py:115
  5.4 2.6 %collective-permute-start.2 = (bf16[16,7296]{1,0:T(8,128)(2,1)}, bf16[16,7296]{1,0:T(8,128)(2,1)S(1)}, u32[]{:S(2)}, u32[]{:S(2)}) collective-permute-start(bf16[16,7296]{1,0:T(8,128)(2,1)} %pack.1), channel_id=1, source_target_pairs={{0,8},{1,9},{2,10},{3,11},{4,0},{5,1},{6,2},{7,3},{8,12},{9,13},{1... | collective-permute-start | bytes 700424 | tf_op jit(solution)/shard_map/ppermute | solution.py:115
  8.0 1.0 %constant_dynamic-update-slice_fusion.5 = bf16[128,7296]{1,0:T(8,128)(2,1)S(1)} fusion(bf16[16,7296]{1,0:T(8,128)(2,1)} %pack.1), kind=kLoop, calls=%fused_computation.21 | loop fusion | bytes 466944
  9.6 1.0 %pad_maximum_fusion.refs_0_ = bf16[32,7296]{1,0:T(8,128)(2,1)S(1)} fusion(bf16[16,7296]{1,0:T(8,128)(2,1)S(1)} %collective-permute-done, bf16[16,7296]{1,0:T(8,128)(2,1)} %pack.1), kind=kLoop, calls=%fused_computation.4 | loop fusion | flops 933888 | bytes 933888 | tf_op jit(solution)/shard_map/concatenate | solution.py:321
  10.6 2.1 %collective-permute-start.1 = (bf16[32,7296]{1,0:T(8,128)(2,1)S(1)}, bf16[32,7296]{1,0:T(8,128)(2,1)S(1)}, u32[]{:S(2)}, u32[]{:S(2)}) collective-permute-start(bf16[32,7296]{1,0:T(8,128)(2,1)S(1)} %pad_maximum_fusion.refs_0_), channel_id=1, source_target_pairs={{0,16},{1,3},{2,18},{3,1},{4,20},{5,7},{6,22},{7,5},{8,24},{9,11},... | collective-permute-start | bytes 1400840 | tf_op jit(solution)/shard_map/ppermute | solution.py:115
  12.7 3.1 %copy-done = bf16[1,7168,512]{2,1,0:T(8,128)(2,1)S(1)} copy-done((bf16[1,7168,512]{2,1,0:T(8,128)(2,1)S(1)}, bf16[1,7168,512]{2,1,0:T(8,128)(2,1)}, u32[]{:S(2)}) %copy-start) | copy-done | bytes 7340056
  15.8 1.6 %collective-permute-start.3 = (bf16[16,7296]{1,0:T(8,128)(2,1)S(1)}, bf16[16,7296]{1,0:T(8,128)(2,1)S(1)}, u32[]{:S(2)}, u32[]{:S(2)}) collective-permute-start(bf16[16,7296]{1,0:T(8,128)(2,1)S(1)} %collective-permute-done.2), channel_id=1, source_target_pairs={{0,2},{1,17},{2,0},{3,19},{4,6},{5,21},{6,4},{7,23},{8,10},{9,25},... | collective-permute-start | bytes 700424 | tf_op jit(solution)/shard_map/ppermute | solution.py:115
  17.4 2.6 %collective-permute-start.6 = (bf16[16,7296]{1,0:T(8,128)(2,1)S(1)}, bf16[16,7296]{1,0:T(8,128)(2,1)S(1)}, u32[]{:S(2)}, u32[]{:S(2)}) collective-permute-start(bf16[16,7296]{1,0:T(8,128)(2,1)S(1)} %collective-permute-done.2), channel_id=1, source_target_pairs={{0,8},{1,9},{2,10},{3,11},{4,0},{5,1},{6,2},{7,3},{8,12},{9,13},{1... | collective-permute-start | bytes 700424 | tf_op jit(solution)/shard_map/ppermute | solution.py:115
  20.0 1.7 %collective-permute-start.8 = (bf16[16,7296]{1,0:T(8,128)(2,1)S(1)}, bf16[16,7296]{1,0:T(8,128)(2,1)S(1)}, u32[]{:S(2)}, u32[]{:S(2)}) collective-permute-start(bf16[16,7296]{1,0:T(8,128)(2,1)S(1)} %collective-permute-done.7), channel_id=1, source_target_pairs={{0,2},{1,17},{2,0},{3,19},{4,6},{5,21},{6,4},{7,23},{8,10},{9,25},... | collective-permute-start | bytes 700424 | tf_op jit(solution)/shard_map/ppermute | solution.py:115
  22.3 5.4 %collective-permute-done.8 = bf16[16,7296]{1,0:T(8,128)(2,1)S(1)} collective-permute-done((bf16[16,7296]{1,0:T(8,128)(2,1)S(1)}, bf16[16,7296]{1,0:T(8,128)(2,1)S(1)}, u32[]{:S(2)}, u32[]{:S(2)}) %collective-permute-start.8) | collective-permute-done | bytes 233504 | tf_op jit(solution)/shard_map/ppermute | solution.py:115
  27.8 2.5 %collective-permute-start.13 = (bf16[16,7296]{1,0:T(8,128)(2,1)S(1)}, bf16[16,7296]{1,0:T(8,128)(2,1)S(1)}, u32[]{:S(2)}, u32[]{:S(2)}) collective-permute-start(bf16[16,7296]{1,0:T(8,128)(2,1)S(1)} %collective-permute-done.6.refs_0_), channel_id=1, source_target_pairs={{0,2},{1,17},{2,0},{3,19},{4,6},{5,21},{6,4},{7,23},{8,10},{9,25},... | collective-permute-start | bytes 700424 | tf_op jit(solution)/shard_map/ppermute | solution.py:115
  30.4 1.4 %collective-permute-done.4 = bf16[32,7296]{1,0:T(8,128)(2,1)S(1)} collective-permute-done((bf16[32,7296]{1,0:T(8,128)(2,1)S(1)}, bf16[32,7296]{1,0:T(8,128)(2,1)S(1)}, u32[]{:S(2)}, u32[]{:S(2)}) %collective-permute-start.4) | collective-permute-done | bytes 466976 | tf_op jit(solution)/shard_map/ppermute | solution.py:115
  32.1 4.8 %collective-permute-done.13 = bf16[16,7296]{1,0:T(8,128)(2,1)S(1)} collective-permute-done((bf16[16,7296]{1,0:T(8,128)(2,1)S(1)}, bf16[16,7296]{1,0:T(8,128)(2,1)S(1)}, u32[]{:S(2)}, u32[]{:S(2)}) %collective-permute-start.13) | collective-permute-done | bytes 233504 | tf_op jit(solution)/shard_map/ppermute | solution.py:115
  37.0 2.0 %collective-permute-start.14 = (bf16[32,7296]{1,0:T(8,128)(2,1)S(1)}, bf16[32,7296]{1,0:T(8,128)(2,1)S(1)}, u32[]{:S(2)}, u32[]{:S(2)}) collective-permute-start(bf16[32,7296]{1,0:T(8,128)(2,1)S(1)} %constant_dynamic-update-slice_fusion.11.refs_1_), channel_id=1, source_target_pairs={{0,16},{1,3},{2,18},{3,1},{4,20},{5,7},{6,22},{7,5},{8,24},{9,11},... | collective-permute-start | bytes 1400840 | tf_op jit(solution)/shard_map/ppermute | solution.py:115
  39.6 5.9 %experts.2 = (bf16[32,7168]{1,0:T(8,128)(2,1)S(1)}, bf16[32,7168]{1,0:T(8,128)(2,1)S(1)}, bf16[32,7168]{1,0:T(8,128)(2,1)S(1)}, bf16[32,7168]{1,0:T(8,128)(2,1)S...) custom-call(s32[1]{0:T(128)} %bitcast.1.me, bf16[1,7168,512]{2,1,0:T(8,128)(2,1)S(1)} %bitcast.6, ...), custom_call_target="tpu_custom_call" | custom-call | flops 5637144576 | bytes 1 | tf_op jit(solution)/shard_map/experts/pallas_call | solution.py:294
  48.4 1.8 %collective-permute-done.9 = bf16[64,7168]{1,0:T(8,128)(2,1)S(1)} collective-permute-done((bf16[64,7168]{1,0:T(8,128)(2,1)S(1)}, bf16[64,7168]{1,0:T(8,128)(2,1)S(1)}, u32[]{:S(2)}, u32[]{:S(2)}) %collective-permute-start.9) | collective-permute-done | bytes 917536 | tf_op jit(solution)/shard_map/ppermute | solution.py:115
  51.0 5.9 %experts.3 = (bf16[32,7168]{1,0:T(8,128)(2,1)S(1)}, bf16[32,7168]{1,0:T(8,128)(2,1)S(1)}, bf16[32,7168]{1,0:T(8,128)(2,1)S(1)}, bf16[32,7168]{1,0:T(8,128)(2,1)S...) custom-call(s32[1]{0:T(128)} %bitcast.1.me, bf16[1,7168,512]{2,1,0:T(8,128)(2,1)S(1)} %bitcast.6, ...), custom_call_target="tpu_custom_call" | custom-call | flops 5637144576 | bytes 1 | tf_op jit(solution)/shard_map/experts/pallas_call | solution.py:294
  57.0 1.6 %collective-permute-start.20 = (bf16[64,7168]{1,0:T(8,128)(2,1)S(1)}, bf16[64,7168]{1,0:T(8,128)(2,1)S(1)}, u32[]{:S(2)}, u32[]{:S(2)}) collective-permute-start(bf16[64,7168]{1,0:T(8,128)(2,1)S(1)} %get-tuple-element.23), channel_id=1, source_target_pairs={{0,1},{1,0},{2,3},{3,2},{4,5},{5,4},{6,7},{7,6},{8,9},{9,8},{10,11... | collective-permute-start | bytes 2752520 | tf_op jit(solution)/shard_map/ppermute | solution.py:115
  58.7 1.0 %collective-permute-start.26 = (bf16[16,7168]{1,0:T(8,128)(2,1)S(1)}, bf16[16,7168]{1,0:T(8,128)(2,1)S(1)}, u32[]{:S(2)}, u32[]{:S(2)}) collective-permute-start(bf16[16,7168]{1,0:T(8,128)(2,1)S(1)} %add_convert_fusion.8), channel_id=1, source_target_pairs={{0,2},{1,17},{2,0},{3,19},{4,6},{5,21},{6,4},{7,23},{8,10},{9,25},... | collective-permute-start | bytes 688136 | tf_op jit(solution)/shard_map/ppermute | solution.py:115
  59.7 0.9 collective-permute-done.20
  61.3 4.4 %collective-permute-done.26 = bf16[16,7168]{1,0:T(8,128)(2,1)S(1)} collective-permute-done((bf16[16,7168]{1,0:T(8,128)(2,1)S(1)}, bf16[16,7168]{1,0:T(8,128)(2,1)S(1)}, u32[]{:S(2)}, u32[]{:S(2)}) %collective-permute-start.26) | collective-permute-done | bytes 229408 | tf_op jit(solution)/shard_map/ppermute | solution.py:115
  66.8 2.5 %collective-permute-done.21 = bf16[32,7168]{1,0:T(8,128)(2,1)S(1)} collective-permute-done((bf16[32,7168]{1,0:T(8,128)(2,1)S(1)}, bf16[32,7168]{1,0:T(8,128)(2,1)S(1)}, u32[]{:S(2)}, u32[]{:S(2)}) %collective-permute-start.21) | collective-permute-done | bytes 458784 | tf_op jit(solution)/shard_map/ppermute | solution.py:115
  69.4 1.9 %collective-permute-start.24 = (bf16[16,7168]{1,0:T(8,128)(2,1)S(1)}, bf16[16,7168]{1,0:T(8,128)(2,1)S(1)}, u32[]{:S(2)}, u32[]{:S(2)}) collective-permute-start(bf16[16,7168]{1,0:T(8,128)(2,1)S(1)} %add_convert_fusion.9), channel_id=1, source_target_pairs={{0,2},{1,17},{2,0},{3,19},{4,6},{5,21},{6,4},{7,23},{8,10},{9,25},... | collective-permute-start | bytes 688136 | tf_op jit(solution)/shard_map/ppermute | solution.py:115
  72.1 5.9 %collective-permute-done.24 = bf16[16,7168]{1,0:T(8,128)(2,1)S(1)} collective-permute-done((bf16[16,7168]{1,0:T(8,128)(2,1)S(1)}, bf16[16,7168]{1,0:T(8,128)(2,1)S(1)}, u32[]{:S(2)}, u32[]{:S(2)}) %collective-permute-start.24) | collective-permute-done | bytes 229408 | tf_op jit(solution)/shard_map/ppermute | solution.py:115
  78.1 1.1 %collective-permute-start.28 = (bf16[16,7168]{1,0:T(8,128)(2,1)S(1)}, bf16[16,7168]{1,0:T(8,128)(2,1)S(1)}, u32[]{:S(2)}, u32[]{:S(2)}) collective-permute-start(bf16[16,7168]{1,0:T(8,128)(2,1)S(1)} %add_convert_fusion.6), channel_id=1, source_target_pairs={{0,8},{1,9},{2,10},{3,11},{4,0},{5,1},{6,2},{7,3},{8,12},{9,13},{1... | collective-permute-start | bytes 688136 | tf_op jit(solution)/shard_map/ppermute | solution.py:115
  80.1 1.0 %collective-permute-start.23 = (bf16[16,7168]{1,0:T(8,128)(2,1)S(1)}, bf16[16,7168]{1,0:T(8,128)(2,1)S(1)}, u32[]{:S(2)}, u32[]{:S(2)}) collective-permute-start(bf16[16,7168]{1,0:T(8,128)(2,1)S(1)} %add_convert_fusion.10), channel_id=1, source_target_pairs={{0,2},{1,17},{2,0},{3,19},{4,6},{5,21},{6,4},{7,23},{8,10},{9,25},... | collective-permute-start | bytes 688136 | tf_op jit(solution)/shard_map/ppermute | solution.py:115
  81.1 1.2 %collective-permute-start.11 = (bf16[16,7168]{1,0:T(8,128)(2,1)S(1)}, bf16[16,7168]{1,0:T(8,128)(2,1)S(1)}, u32[]{:S(2)}, u32[]{:S(2)}) collective-permute-start(bf16[16,7168]{1,0:T(8,128)(2,1)S(1)} %add_convert_fusion.11), channel_id=1, source_target_pairs={{0,2},{1,17},{2,0},{3,19},{4,6},{5,21},{6,4},{7,23},{8,10},{9,25},... | collective-permute-start | bytes 688136 | tf_op jit(solution)/shard_map/ppermute | solution.py:115
  82.3 1.9 %collective-permute-done.28 = bf16[16,7168]{1,0:T(8,128)(2,1)S(1)} collective-permute-done((bf16[16,7168]{1,0:T(8,128)(2,1)S(1)}, bf16[16,7168]{1,0:T(8,128)(2,1)S(1)}, u32[]{:S(2)}, u32[]{:S(2)}) %collective-permute-start.28) | collective-permute-done | bytes 229408 | tf_op jit(solution)/shard_map/ppermute | solution.py:115
  84.2 2.0 %collective-permute-done.23 = bf16[16,7168]{1,0:T(8,128)(2,1)S(1)} collective-permute-done((bf16[16,7168]{1,0:T(8,128)(2,1)S(1)}, bf16[16,7168]{1,0:T(8,128)(2,1)S(1)}, u32[]{:S(2)}, u32[]{:S(2)}) %collective-permute-start.23) | collective-permute-done | bytes 229408 | tf_op jit(solution)/shard_map/ppermute | solution.py:115
  87.2 3.2 %attend.1 = bf16[16,64,512]{2,1,0:T(8,128)(2,1)} custom-call(s32[16]{0:T(128)S(1)} %copy-done.4, bf16[16,64,576]{2,1,0:T(8,128)(2,1)S(1)} %copy-done.3, bf16[16,576,128]{2,1,0:T(8,128)(2,1)S(1)} %bitcast.9), custom_call_target="tpu_custom_call" | custom-call | flops 2852126720 | bytes 1 | tf_op jit(solution)/shard_map/attend/pallas_call | solution.py:215
  90.4 2.8 %collective-permute-done.29 = bf16[16,7168]{1,0:T(8,128)(2,1)S(1)} collective-permute-done((bf16[16,7168]{1,0:T(8,128)(2,1)S(1)}, bf16[16,7168]{1,0:T(8,128)(2,1)S(1)}, u32[]{:S(2)}, u32[]{:S(2)}) %collective-permute-start.29) | collective-permute-done | bytes 229408 | tf_op jit(solution)/shard_map/ppermute | solution.py:115
  (82 shorter events, 11.0 us)
Async XLA Ops:
  2.4 7.2 %collective-permute-start = (bf16[16,7296]{1,0:T(8,128)(2,1)}, bf16[16,7296]{1,0:T(8,128)(2,1)S(1)}, u32[]{:S(2)}, u32[]{:S(2)}) collective-permute-start(bf16[16,7296]{1,0:T(8,128)(2,1)} %pack.1), channel_id=1, source_target_pairs={{0,2},{1,17},{2,0},{3,19},{4,6},{5,21},{6,4},{7,23},{8,10},{9,25},... | collective-permute-start | bytes 700424 | tf_op jit(solution)/shard_map/ppermute | solution.py:115
  5.4 10.4 %collective-permute-start.2 = (bf16[16,7296]{1,0:T(8,128)(2,1)}, bf16[16,7296]{1,0:T(8,128)(2,1)S(1)}, u32[]{:S(2)}, u32[]{:S(2)}) collective-permute-start(bf16[16,7296]{1,0:T(8,128)(2,1)} %pack.1), channel_id=1, source_target_pairs={{0,8},{1,9},{2,10},{3,11},{4,0},{5,1},{6,2},{7,3},{8,12},{9,13},{1... | collective-permute-start | bytes 700424 | tf_op jit(solution)/shard_map/ppermute | solution.py:115
  8.0 12.0 %collective-permute-start.7 = (bf16[16,7296]{1,0:T(8,128)(2,1)}, bf16[16,7296]{1,0:T(8,128)(2,1)S(1)}, u32[]{:S(2)}, u32[]{:S(2)}) collective-permute-start(bf16[16,7296]{1,0:T(8,128)(2,1)} %pack.1), channel_id=1, source_target_pairs={{0,4},{1,5},{2,6},{3,7},{4,12},{5,13},{6,14},{7,15},{8,0},{9,1},{1... | collective-permute-start | bytes 700424 | tf_op jit(solution)/shard_map/ppermute | solution.py:115
  10.6 19.8 %collective-permute-start.1 = (bf16[32,7296]{1,0:T(8,128)(2,1)S(1)}, bf16[32,7296]{1,0:T(8,128)(2,1)S(1)}, u32[]{:S(2)}, u32[]{:S(2)}) collective-permute-start(bf16[32,7296]{1,0:T(8,128)(2,1)S(1)} %pad_maximum_fusion.refs_0_), channel_id=1, source_target_pairs={{0,16},{1,3},{2,18},{3,1},{4,20},{5,7},{6,22},{7,5},{8,24},{9,11},... | collective-permute-start | bytes 1400840 | tf_op jit(solution)/shard_map/ppermute | solution.py:115
  15.8 16.2 %copy-start.1 = (bf16[1,512,7168]{2,1,0:T(8,128)(2,1)S(1)}, bf16[1,512,7168]{2,1,0:T(8,128)(2,1)}, u32[]{:S(2)}) copy-start(bf16[1,512,7168]{2,1,0:T(8,128)(2,1)} %w_down.3) | copy-start | bytes 22020100
  15.8 16.3 %slice-start.2 = ((s8[7340032]{0:T(1024)(128)(4,1)}), s8[4194304]{0:T(1024)(128)(4,1)S(1)}, s32[]{:S(2)}) async-start(s8[7340032]{0:T(1024)(128)(4,1)} %bitcast.7), calls=%async_computation.2 | async-start | bytes 8388608
  15.8 6.1 %collective-permute-start.3 = (bf16[16,7296]{1,0:T(8,128)(2,1)S(1)}, bf16[16,7296]{1,0:T(8,128)(2,1)S(1)}, u32[]{:S(2)}, u32[]{:S(2)}) collective-permute-start(bf16[16,7296]{1,0:T(8,128)(2,1)S(1)} %collective-permute-done.2), channel_id=1, source_target_pairs={{0,2},{1,17},{2,0},{3,19},{4,6},{5,21},{6,4},{7,23},{8,10},{9,25},... | collective-permute-start | bytes 700424 | tf_op jit(solution)/shard_map/ppermute | solution.py:115
  17.4 10.4 %collective-permute-start.6 = (bf16[16,7296]{1,0:T(8,128)(2,1)S(1)}, bf16[16,7296]{1,0:T(8,128)(2,1)S(1)}, u32[]{:S(2)}, u32[]{:S(2)}) collective-permute-start(bf16[16,7296]{1,0:T(8,128)(2,1)S(1)} %collective-permute-done.2), channel_id=1, source_target_pairs={{0,8},{1,9},{2,10},{3,11},{4,0},{5,1},{6,2},{7,3},{8,12},{9,13},{1... | collective-permute-start | bytes 700424 | tf_op jit(solution)/shard_map/ppermute | solution.py:115
  20.0 7.7 %collective-permute-start.8 = (bf16[16,7296]{1,0:T(8,128)(2,1)S(1)}, bf16[16,7296]{1,0:T(8,128)(2,1)S(1)}, u32[]{:S(2)}, u32[]{:S(2)}) collective-permute-start(bf16[16,7296]{1,0:T(8,128)(2,1)S(1)} %collective-permute-done.7), channel_id=1, source_target_pairs={{0,2},{1,17},{2,0},{3,19},{4,6},{5,21},{6,4},{7,23},{8,10},{9,25},... | collective-permute-start | bytes 700424 | tf_op jit(solution)/shard_map/ppermute | solution.py:115
  22.0 9.9 %collective-permute-start.4 = (bf16[32,7296]{1,0:T(8,128)(2,1)S(1)}, bf16[32,7296]{1,0:T(8,128)(2,1)S(1)}, u32[]{:S(2)}, u32[]{:S(2)}) collective-permute-start(bf16[32,7296]{1,0:T(8,128)(2,1)S(1)} %pad_maximum_fusion.1), channel_id=1, source_target_pairs={{0,16},{1,3},{2,18},{3,1},{4,20},{5,7},{6,22},{7,5},{8,24},{9,11},... | collective-permute-start | bytes 1400840 | tf_op jit(solution)/shard_map/ppermute | solution.py:115
  27.7 11.3 %collective-permute-start.12 = (bf16[32,7296]{1,0:T(8,128)(2,1)S(1)}, bf16[32,7296]{1,0:T(8,128)(2,1)S(1)}, u32[]{:S(2)}, u32[]{:S(2)}) collective-permute-start(bf16[32,7296]{1,0:T(8,128)(2,1)S(1)} %get-tuple-element.27.refs_0_), channel_id=1, source_target_pairs={{0,16},{1,3},{2,18},{3,1},{4,20},{5,7},{6,22},{7,5},{8,24},{9,11},... | collective-permute-start | bytes 1400840 | tf_op jit(solution)/shard_map/ppermute | solution.py:115
  27.8 9.1 %collective-permute-start.13 = (bf16[16,7296]{1,0:T(8,128)(2,1)S(1)}, bf16[16,7296]{1,0:T(8,128)(2,1)S(1)}, u32[]{:S(2)}, u32[]{:S(2)}) collective-permute-start(bf16[16,7296]{1,0:T(8,128)(2,1)S(1)} %collective-permute-done.6.refs_0_), channel_id=1, source_target_pairs={{0,2},{1,17},{2,0},{3,19},{4,6},{5,21},{6,4},{7,23},{8,10},{9,25},... | collective-permute-start | bytes 700424 | tf_op jit(solution)/shard_map/ppermute | solution.py:115
  31.9 7.7 %collective-permute-start.5 = (bf16[128,7296]{1,0:T(8,128)(2,1)S(1)}, bf16[128,7296]{1,0:T(8,128)(2,1)S(1)}, u32[]{:S(2)}, u32[]{:S(2)}) collective-permute-start(bf16[128,7296]{1,0:T(8,128)(2,1)S(1)} %constant_dynamic-update-slice_fusion.refs_0_), channel_id=1, source_target_pairs={{0,1},{1,0},{2,3},{3,2},{4,5},{5,4},{6,7},{7,6},{8,9},{9,8},{10,11... | collective-permute-start | bytes 5603336 | tf_op jit(solution)/shard_map/ppermute | solution.py:115
  37.0 9.9 %collective-permute-start.14 = (bf16[32,7296]{1,0:T(8,128)(2,1)S(1)}, bf16[32,7296]{1,0:T(8,128)(2,1)S(1)}, u32[]{:S(2)}, u32[]{:S(2)}) collective-permute-start(bf16[32,7296]{1,0:T(8,128)(2,1)S(1)} %constant_dynamic-update-slice_fusion.11.refs_1_), channel_id=1, source_target_pairs={{0,16},{1,3},{2,18},{3,1},{4,20},{5,7},{6,22},{7,5},{8,24},{9,11},... | collective-permute-start | bytes 1400840 | tf_op jit(solution)/shard_map/ppermute | solution.py:115
  39.0 12.0 %collective-permute-start.16 = (bf16[32,7296]{1,0:T(8,128)(2,1)S(1)}, bf16[32,7296]{1,0:T(8,128)(2,1)S(1)}, u32[]{:S(2)}, u32[]{:S(2)}) collective-permute-start(bf16[32,7296]{1,0:T(8,128)(2,1)S(1)} %constant_dynamic-update-slice_fusion.11.refs_1_), channel_id=1, source_target_pairs={{0,1},{1,0},{2,3},{3,2},{4,5},{5,4},{6,7},{7,6},{8,9},{9,8},{10,11... | collective-permute-start | bytes 1400840 | tf_op jit(solution)/shard_map/ppermute | solution.py:115
  39.0 12.0 %collective-permute-start.15 = (bf16[64,7296]{1,0:T(8,128)(2,1)S(1)}, bf16[64,7296]{1,0:T(8,128)(2,1)S(1)}, u32[]{:S(2)}, u32[]{:S(2)}) collective-permute-start(bf16[64,7296]{1,0:T(8,128)(2,1)S(1)} %constant_dynamic-update-slice_fusion.8.refs_0_), channel_id=1, source_target_pairs={{0,1},{1,0},{2,3},{3,2},{4,5},{5,4},{6,7},{7,6},{8,9},{9,8},{10,11... | collective-permute-start | bytes 2801672 | tf_op jit(solution)/shard_map/ppermute | solution.py:115
  45.6 2.5 %collective-permute-start.18 = (bf16[64,7168]{1,0:T(8,128)(2,1)S(1)}, bf16[64,7168]{1,0:T(8,128)(2,1)S(1)}, u32[]{:S(2)}, u32[]{:S(2)}) collective-permute-start(bf16[64,7168]{1,0:T(8,128)(2,1)S(1)} %get-tuple-element.17), channel_id=1, source_target_pairs={{0,1},{1,0},{2,3},{3,2},{4,5},{5,4},{6,7},{7,6},{8,9},{9,8},{10,11... | collective-permute-start | bytes 2752520 | tf_op jit(solution)/shard_map/ppermute | solution.py:115
  46.9 4.1 %collective-permute-start.17 = (bf16[32,7296]{1,0:T(8,128)(2,1)S(1)}, bf16[32,7296]{1,0:T(8,128)(2,1)S(1)}, u32[]{:S(2)}, u32[]{:S(2)}) collective-permute-start(bf16[32,7296]{1,0:T(8,128)(2,1)S(1)} %broadcast_add_fusion), channel_id=1, source_target_pairs={{0,1},{1,0},{2,3},{3,2},{4,5},{5,4},{6,7},{7,6},{8,9},{9,8},{10,11... | collective-permute-start | bytes 1400840 | tf_op jit(solution)/shard_map/ppermute | solution.py:115
  47.4 2.8 %collective-permute-start.9 = (bf16[64,7168]{1,0:T(8,128)(2,1)S(1)}, bf16[64,7168]{1,0:T(8,128)(2,1)S(1)}, u32[]{:S(2)}, u32[]{:S(2)}) collective-permute-start(bf16[64,7168]{1,0:T(8,128)(2,1)S(1)} %get-tuple-element.15), channel_id=1, source_target_pairs={{0,1},{1,0},{2,3},{3,2},{4,5},{5,4},{6,7},{7,6},{8,9},{9,8},{10,11... | collective-permute-start | bytes 2752520 | tf_op jit(solution)/shard_map/ppermute | solution.py:115
  48.2 10.4 %collective-permute-start.25 = (bf16[32,7168]{1,0:T(8,128)(2,1)S(1)}, bf16[32,7168]{1,0:T(8,128)(2,1)S(1)}, u32[]{:S(2)}, u32[]{:S(2)}) collective-permute-start(bf16[32,7168]{1,0:T(8,128)(2,1)S(1)} %add_convert_fusion.2.refs_6_), channel_id=1, source_target_pairs={{0,16},{1,3},{2,18},{3,1},{4,20},{5,7},{6,22},{7,5},{8,24},{9,11},... | collective-permute-start | bytes 1376264 | tf_op jit(solution)/shard_map/ppermute | solution.py:115
  50.3 30.7 %collective-permute-start.10 = (bf16[32,7168]{1,0:T(8,128)(2,1)S(1)}, bf16[32,7168]{1,0:T(8,128)(2,1)S(1)}, u32[]{:S(2)}, u32[]{:S(2)}) collective-permute-start(bf16[32,7168]{1,0:T(8,128)(2,1)S(1)} %add_convert_fusion.3.refs_7_), channel_id=1, source_target_pairs={{0,16},{1,3},{2,18},{3,1},{4,20},{5,7},{6,22},{7,5},{8,24},{9,11},... | collective-permute-start | bytes 1376264 | tf_op jit(solution)/shard_map/ppermute | solution.py:115
  57.0 3.7 %collective-permute-start.20 = (bf16[64,7168]{1,0:T(8,128)(2,1)S(1)}, bf16[64,7168]{1,0:T(8,128)(2,1)S(1)}, u32[]{:S(2)}, u32[]{:S(2)}) collective-permute-start(bf16[64,7168]{1,0:T(8,128)(2,1)S(1)} %get-tuple-element.23), channel_id=1, source_target_pairs={{0,1},{1,0},{2,3},{3,2},{4,5},{5,4},{6,7},{7,6},{8,9},{9,8},{10,11... | collective-permute-start | bytes 2752520 | tf_op jit(solution)/shard_map/ppermute | solution.py:115
  58.5 12.7 %collective-permute-start.19 = (bf16[64,7168]{1,0:T(8,128)(2,1)S(1)}, bf16[64,7168]{1,0:T(8,128)(2,1)S(1)}, u32[]{:S(2)}, u32[]{:S(2)}) collective-permute-start(bf16[64,7168]{1,0:T(8,128)(2,1)S(1)} %get-tuple-element.20), channel_id=1, source_target_pairs={{0,1},{1,0},{2,3},{3,2},{4,5},{5,4},{6,7},{7,6},{8,9},{9,8},{10,11... | collective-permute-start | bytes 2752520 | tf_op jit(solution)/shard_map/ppermute | solution.py:115
  58.7 7.0 %collective-permute-start.26 = (bf16[16,7168]{1,0:T(8,128)(2,1)S(1)}, bf16[16,7168]{1,0:T(8,128)(2,1)S(1)}, u32[]{:S(2)}, u32[]{:S(2)}) collective-permute-start(bf16[16,7168]{1,0:T(8,128)(2,1)S(1)} %add_convert_fusion.8), channel_id=1, source_target_pairs={{0,2},{1,17},{2,0},{3,19},{4,6},{5,21},{6,4},{7,23},{8,10},{9,25},... | collective-permute-start | bytes 688136 | tf_op jit(solution)/shard_map/ppermute | solution.py:115
  60.8 8.5 %collective-permute-start.21 = (bf16[32,7168]{1,0:T(8,128)(2,1)S(1)}, bf16[32,7168]{1,0:T(8,128)(2,1)S(1)}, u32[]{:S(2)}, u32[]{:S(2)}) collective-permute-start(bf16[32,7168]{1,0:T(8,128)(2,1)S(1)} %add_convert_fusion), channel_id=1, source_target_pairs={{0,16},{1,3},{2,18},{3,1},{4,20},{5,7},{6,22},{7,5},{8,24},{9,11},... | collective-permute-start | bytes 1376264 | tf_op jit(solution)/shard_map/ppermute | solution.py:115
  65.9 6.2 %collective-permute-start.27 = (bf16[16,7168]{1,0:T(8,128)(2,1)S(1)}, bf16[16,7168]{1,0:T(8,128)(2,1)S(1)}, u32[]{:S(2)}, u32[]{:S(2)}) collective-permute-start(bf16[16,7168]{1,0:T(8,128)(2,1)S(1)} %add_convert_fusion.7), channel_id=1, source_target_pairs={{0,8},{1,9},{2,10},{3,11},{4,0},{5,1},{6,2},{7,3},{8,12},{9,13},{1... | collective-permute-start | bytes 688136 | tf_op jit(solution)/shard_map/ppermute | solution.py:115
  69.4 8.5 %collective-permute-start.24 = (bf16[16,7168]{1,0:T(8,128)(2,1)S(1)}, bf16[16,7168]{1,0:T(8,128)(2,1)S(1)}, u32[]{:S(2)}, u32[]{:S(2)}) collective-permute-start(bf16[16,7168]{1,0:T(8,128)(2,1)S(1)} %add_convert_fusion.9), channel_id=1, source_target_pairs={{0,2},{1,17},{2,0},{3,19},{4,6},{5,21},{6,4},{7,23},{8,10},{9,25},... | collective-permute-start | bytes 688136 | tf_op jit(solution)/shard_map/ppermute | solution.py:115
  71.4 8.5 %collective-permute-start.22 = (bf16[32,7168]{1,0:T(8,128)(2,1)S(1)}, bf16[32,7168]{1,0:T(8,128)(2,1)S(1)}, u32[]{:S(2)}, u32[]{:S(2)}) collective-permute-start(bf16[32,7168]{1,0:T(8,128)(2,1)S(1)} %fusion), channel_id=1, source_target_pairs={{0,16},{1,3},{2,18},{3,1},{4,20},{5,7},{6,22},{7,5},{8,24},{9,11},... | collective-permute-start | bytes 1376264 | tf_op jit(solution)/shard_map/ppermute | solution.py:115
  78.1 6.1 %collective-permute-start.28 = (bf16[16,7168]{1,0:T(8,128)(2,1)S(1)}, bf16[16,7168]{1,0:T(8,128)(2,1)S(1)}, u32[]{:S(2)}, u32[]{:S(2)}) collective-permute-start(bf16[16,7168]{1,0:T(8,128)(2,1)S(1)} %add_convert_fusion.6), channel_id=1, source_target_pairs={{0,8},{1,9},{2,10},{3,11},{4,0},{5,1},{6,2},{7,3},{8,12},{9,13},{1... | collective-permute-start | bytes 688136 | tf_op jit(solution)/shard_map/ppermute | solution.py:115
  80.1 6.1 %collective-permute-start.23 = (bf16[16,7168]{1,0:T(8,128)(2,1)S(1)}, bf16[16,7168]{1,0:T(8,128)(2,1)S(1)}, u32[]{:S(2)}, u32[]{:S(2)}) collective-permute-start(bf16[16,7168]{1,0:T(8,128)(2,1)S(1)} %add_convert_fusion.10), channel_id=1, source_target_pairs={{0,2},{1,17},{2,0},{3,19},{4,6},{5,21},{6,4},{7,23},{8,10},{9,25},... | collective-permute-start | bytes 688136 | tf_op jit(solution)/shard_map/ppermute | solution.py:115
  81.1 9.2 %collective-permute-start.11 = (bf16[16,7168]{1,0:T(8,128)(2,1)S(1)}, bf16[16,7168]{1,0:T(8,128)(2,1)S(1)}, u32[]{:S(2)}, u32[]{:S(2)}) collective-permute-start(bf16[16,7168]{1,0:T(8,128)(2,1)S(1)} %add_convert_fusion.11), channel_id=1, source_target_pairs={{0,2},{1,17},{2,0},{3,19},{4,6},{5,21},{6,4},{7,23},{8,10},{9,25},... | collective-permute-start | bytes 688136 | tf_op jit(solution)/shard_map/ppermute | solution.py:115
  86.3 6.8 %collective-permute-start.29 = (bf16[16,7168]{1,0:T(8,128)(2,1)S(1)}, bf16[16,7168]{1,0:T(8,128)(2,1)S(1)}, u32[]{:S(2)}, u32[]{:S(2)}) collective-permute-start(bf16[16,7168]{1,0:T(8,128)(2,1)S(1)} %add_convert_fusion.5), channel_id=1, source_target_pairs={{0,8},{1,9},{2,10},{3,11},{4,0},{5,1},{6,2},{7,3},{8,12},{9,13},{1... | collective-permute-start | bytes 688136 | tf_op jit(solution)/shard_map/ppermute | solution.py:115
  (7 other events, 50.0 us)
